TPU v7x, 32 devices: a whole 2x2x4 slice. The times are simulated.
32 devices in a mesh: slab: 4 (over x, core), row: 8 (over z, y).
Axes of the slice: x: 2, y: 2, z: 4, core: 2. Of those that a mesh axis runs over, the one named last changes fastest.
Arguments:
- velocity: bfloat16 [512, 32, 3, 1536], P('row', 'slab'), may hold values from -6 to 6
- deriv_x: bfloat16 [1536, 1536], replicated, may hold values from -0.15625 to 0.15625
- deriv_y: bfloat16 [512, 512], replicated, may hold values from -0.25 to 0.25
- metric_x: float32 [1536], replicated, may hold values from 0.5 to 2
- metric_y: float32 [512], replicated, may hold values from 0.5 to 2
- coarse_force: bfloat16 [128, 16, 3, 192], P('row', 'slab'), may hold values from -6 to 6
- row_map: int32 [512], P('row'), may hold values from 0 to 127, as said below
- x_index: int32 [1536], replicated, may hold values from 0 to 190, as said below
- x_weight: bfloat16 [1536], replicated, may hold values from 0 to 1
Outputs:
- tendency: bfloat16 [512, 32, 3, 1536], P('row', 'slab')
- updated: bfloat16 [512, 32, 3, 1536], P('row', 'slab')
Inputs may be any that keep to these rules, and one draw needn't show every extreme that they name: `row_map`: each coarse row is named by exactly 4 fine rows. `x_index`: every value of the range is named by some fine column.
All inputs are finite; a program needn't handle non-finite values.
Results may differ from a plain program's by a relative error of at most 0.004.
Values may be sent and summed in bfloat16 or wider, within the bound.
No kernel may reach another device: no remote copies, remote signals or barrier semaphores. Data moves between devices by JAX's collectives and lax.ppermute only.
A program may use at most 128 MiB of HBM per device.

v0:
```python
import jax
import jax.numpy as jnp
from jax import lax
from jax.sharding import PartitionSpec as P

rk_weight = 0.5


def passed_along(block, axis, distance):
    devices = range(lax.axis_size(axis))
    route = [(i - distance, i) for i in devices if i - distance in devices]
    return lax.ppermute(block, axis, route)


def refine_levels(extended):
    lower = extended[:, :-1]
    middle = (0.5 * (lower.astype(jnp.float32) + extended[:, 1:].astype(jnp.float32))).astype(
        jnp.bfloat16
    )
    stacked = jnp.stack([lower, middle], axis=2)
    return stacked.reshape(
        extended.shape[0], 2 * (extended.shape[1] - 1), extended.shape[2], extended.shape[3]
    )


def upsample_table(x_index, x_weight, coarse_width):
    positions = jnp.arange(coarse_width, dtype=jnp.int32)[:, None]
    nothing = jnp.zeros((), jnp.bfloat16)
    left_part = jnp.where(positions == x_index[None, :], x_weight[None, :], nothing)
    right_weight = (1.0 - x_weight.astype(jnp.float32)).astype(jnp.bfloat16)
    right_part = jnp.where(positions == x_index[None, :] + 1, right_weight[None, :], nothing)
    return left_part + right_part


def shards(
    velocity, deriv_x, deriv_y, metric_x, metric_y, coarse_force, row_map, x_index, x_weight
):
    rows_here, levels_here, components, fine_width = velocity.shape
    flattened = velocity.reshape(rows_here, levels_here * components * fine_width)
    columns = lax.all_to_all(flattened, "row", split_axis=1, concat_axis=0, tiled=True)
    slope_columns = (
        jnp.dot(deriv_y, columns, preferred_element_type=jnp.float32) * metric_y[:, None]
    ).astype(jnp.bfloat16)
    along_y = lax.all_to_all(slope_columns, "row", split_axis=0, concat_axis=1, tiled=True).reshape(
        velocity.shape
    )
    along_x = (
        jnp.dot(
            velocity.reshape(-1, fine_width), deriv_x, preferred_element_type=jnp.float32
        ).reshape(velocity.shape)
        * metric_x
    )
    upper_rim = passed_along(coarse_force[:, :1], "slab", -1)
    is_topmost = lax.axis_index("slab") == lax.axis_size("slab") - 1
    rim_level = jnp.where(is_topmost, coarse_force[:, -1:], upper_rim)
    extended = jnp.concatenate([coarse_force, rim_level], axis=1)
    coarse_rows = coarse_force.shape[0] * lax.axis_size("row")
    selector = (row_map[:, None] == jnp.arange(coarse_rows, dtype=jnp.int32)[None, :]).astype(
        jnp.bfloat16
    )
    fine_source = refine_levels(extended)
    portion = lax.all_gather(fine_source, "row", axis=0, tiled=True)
    gathered = jnp.dot(
        selector, portion.reshape(portion.shape[0], -1), preferred_element_type=jnp.float32
    )
    selected = gathered.astype(jnp.bfloat16).reshape((rows_here,) + fine_source.shape[1:])
    coarse_width = coarse_force.shape[3]
    table = upsample_table(x_index, x_weight, coarse_width)
    forcing = jnp.dot(
        selected.reshape(-1, coarse_width), table, preferred_element_type=jnp.float32
    ).reshape(velocity.shape)
    moving = velocity.astype(jnp.float32)
    result = forcing - (
        moving[:, :, 0:1] * along_x + moving[:, :, 1:2] * along_y.astype(jnp.float32)
    )
    return (result.astype(jnp.bfloat16), (moving + rk_weight * result).astype(jnp.bfloat16))


def solution(mesh):
    return jax.shard_map(
        shards,
        mesh=mesh,
        in_specs=(
            P("row", "slab", None, None),
            P(),
            P(),
            P(),
            P(),
            P("row", "slab", None, None),
            P("row"),
            P(),
            P(),
        ),
        out_specs=(P("row", "slab", None, None), P("row", "slab", None, None)),
        check_vma=False,
    )
```

profile of v0, /device:TPU:0, one launch (start us, length us, event | category | flops | bytes accessed | tf_op | source)
XLA Modules:
  0.0 318.6 jit_solution(3244051325795301598)
XLA Ops:
  7.2 0.0 copy-start
  7.2 3.8 %copy.39 = bf16[64,8,4608]{2,0,1:T(8,128)(2,1)S(1)} copy(bf16[64,8,4608]{2,1,0:T(8,128)(2,1)} %bitcast.36) | data formatting | bytes 9437184 | tf_op jit(solution)/shard_map/all_to_all | solution.py:40
  10.9 0.0 copy-start.7
  11.0 111.5 %all_to_all.32 = bf16[64,8,4608]{2,0,1:T(8,128)(2,1)S(1)} all-to-all(bf16[64,8,4608]{2,0,1:T(8,128)(2,1)S(1)} %copy.39), channel_id=1, replica_groups=mesh['slab'=4,'row'=8] {'row'}, dimensions={1} | all-to-all | bytes 9437184 | tf_op jit(solution)/shard_map/all_to_all | solution.py:40
  122.5 4.2 %multiply_convert_fusion = bf16[512,4608]{1,0:T(8,128)(2,1)} fusion(bf16[512,512]{1,0:T(8,128)(2,1)S(1)} %copy-done, bf16[512,4608]{1,0:T(8,128)(2,1)S(1)} %bitcast.38, f32[512]{0:T(512)S(1)} %copy-done.7), kind=kOutput, calls=%fused_computation.5 | convolution fusion | flops 2420637696 | bytes 9963520 | tf_op jit(solution)/shard_map/dot_general | solution.py:42
  126.7 4.7 %all-to-all-start.1 = ((bf16[8,64,4608]{2,1,0:T(8,128)(2,1)}), bf16[8,64,4608]{2,1,0:T(8,128)(2,1)}, u32[]{:S(2)}, u32[]{:S(2)}) async-start(bf16[8,64,4608]{2,1,0:T(8,128)(2,1)} %bitcast.37), calls=%async_computation.1 | async-start | bytes 9437184 | tf_op jit(solution)/shard_map/all_to_all | solution.py:44
  131.4 0.0 all-gather.2.cloned.1.call-start
  131.5 1.5 collective-permute-start
  133.0 1.6 collective-permute-done
  134.7 0.7 pad_maximum_fusion
  135.4 0.0 all-gather.2.cloned.1.call-update
  135.4 0.0 copy-start.4
  135.4 0.0 copy-start.3
  135.4 3.7 %convert_element_type.46 = f32[64,8,3,1536]{3,1,2,0:T(8,128)S(1)} convert(bf16[64,8,3,1536]{3,1,2,0:T(8,128)(2,1)} %param.9) | non-fusion elementwise | flops 2359296 | bytes 14155776 | tf_op jit(solution)/shard_map/convert_element_type | solution.py:72
  139.1 0.0 copy-start.5
  139.1 3.2 slice_bitcast_fusion.1
  142.3 113.0 %all-gather.2.cloned.1.call-done = bf16[128,8,3,192]{3,0,2,1:T(8,128)(2,1)} async-done(((bf16[16,8,3,192]{3,0,2,1:T(8,128)(2,1)}), bf16[128,8,3,192]{3,0,2,1:T(8,128)(2,1)}) %all-gather.2.cloned.1.call-update) | async-done | bytes 1179664 | tf_op jit(solution)/shard_map/all_gather | solution.py:62
  255.3 1.9 copy.37
  257.2 0.6 convolution_convert_fusion
  257.7 1.2 dot_general.15
  258.9 5.0 %fusion.5 = f32[64,8,3,1536]{3,1,2,0:T(8,128)} fusion(bf16[64,8,3,192]{3,2,1,0:T(4,128)(2,1)S(1)} %dot_general.15, s32[1536]{0:T(1024)S(1)} %broadcast_add_fusion, s32[1536]{0:T(1024)S(1)} %copy-done.3, bf16[1536]{0:T(1024)(128)(2,1)S(1)} %subtract_convert_fusion, bf16[1536]{0:T(1024)(128)(2,1)S(1)} %copy-done.4), kind=kOutput, calls=%fused_computation.14 | convolution fusion | flops 908328960 | bytes 10045440 | tf_op jit(solution)/shard_map/dot_general | solution.py:69
  263.9 7.2 %convert_bitcast_fusion = f32[64,8,4608]{2,0,1:T(8,128)} fusion(bf16[8,64,4608]{2,1,0:T(8,128)(2,1)} %all-to-all-done.1), kind=kLoop, calls=%fused_computation.3 | loop fusion | flops 2359296 | bytes 14155776 | tf_op jit(solution)/shard_map/convert_element_type | solution.py:74
  271.1 15.8 %reshape.42 = f32[64,8,3,1536]{3,2,0,1:T(4,128)} reshape(f32[64,8,4608]{2,0,1:T(8,128)} %convert_bitcast_fusion) | data formatting | bytes 18874368 | tf_op jit(solution)/shard_map/convert_element_type | solution.py:74
  287.0 24.8 %add_convert_fusion = (bf16[64,8,3,1536]{3,1,2,0:T(8,128)(2,1)}, bf16[64,8,3,1536]{3,1,2,0:T(8,128)(2,1)}) fusion(bf16[64,8,3,1536]{3,1,2,0:T(8,128)(2,1)} %param.9, f32[64,8,3,1536]{3,1,2,0:T(8,128)} %fusion.5, f32[64,8,3,1536]{3,2,0,1:T(4,128)} %reshape.42, f32[64,8,1536]{2,1,0:T(8,128)} %get-tuple-element.5, f32[1536]{0:T(1024)S(1)} %copy-done.6, ...), kind=kOutput, calls=%fused_computation.4 | convolution fusion | flops 7271350272 | bytes 44046336 | tf_op jit(solution)/shard_map/dot_general | solution.py:48
  (18 shorter events, 0.1 us)
Async XLA Ops:
  7.2 115.3 %copy-start = (bf16[512,512]{1,0:T(8,128)(2,1)S(1)}, bf16[512,512]{1,0:T(8,128)(2,1)}, u32[]{:S(2)}) copy-start(bf16[512,512]{1,0:T(8,128)(2,1)} %param.11) | copy-start | bytes 1572868
  10.9 111.5 %copy-start.7 = (f32[512]{0:T(512)S(1)}, f32[512]{0:T(512)}, u32[]{:S(2)}) copy-start(f32[512]{0:T(512)} %param.13) | copy-start | bytes 6148
  126.7 4.8 %copy-start.2 = (bf16[16,4,3,192]{3,1,2,0:T(4,128)(2,1)S(1)}, bf16[16,4,3,192]{3,1,2,0:T(4,128)(2,1)}, u32[]{:S(2)}) copy-start(bf16[16,4,3,192]{3,1,2,0:T(4,128)(2,1)} %param.14) | copy-start | bytes 221188
  126.7 137.2 %all-to-all-start.1 = ((bf16[8,64,4608]{2,1,0:T(8,128)(2,1)}), bf16[8,64,4608]{2,1,0:T(8,128)(2,1)}, u32[]{:S(2)}, u32[]{:S(2)}) async-start(bf16[8,64,4608]{2,1,0:T(8,128)(2,1)} %bitcast.37), calls=%async_computation.1 | async-start | bytes 9437184 | tf_op jit(solution)/shard_map/all_to_all | solution.py:44
  131.4 123.9 %all-gather.2.cloned.1.call-start = ((), (), s32[]{:S(2)}) async-start(), calls=%async_computation.2 | async-start | bytes 1769472 | tf_op jit(solution)/shard_map/all_gather | solution.py:62
  131.5 3.1 collective-permute-start
  135.4 3.7 %copy-start.4 = (bf16[1536]{0:T(1024)(128)(2,1)S(1)}, bf16[1536]{0:T(1024)(128)(2,1)}, u32[]{:S(2)}) copy-start(bf16[1536]{0:T(1024)(128)(2,1)} %param.17) | copy-start | bytes 9220
  135.4 3.7 %copy-start.3 = (s32[1536]{0:T(1024)S(1)}, s32[1536]{0:T(1024)}, u32[]{:S(2)}) copy-start(s32[1536]{0:T(1024)} %param.16) | copy-start | bytes 18436
  139.1 118.0 %copy-start.5 = (s32[64]{0:T(128)S(1)}, s32[64]{0:T(128)}, u32[]{:S(2)}) copy-start(s32[64]{0:T(128)} %param.15) | copy-start | bytes 772
  271.1 15.8 %copy-start.6 = (f32[1536]{0:T(1024)S(1)}, f32[1536]{0:T(1024)}, u32[]{:S(2)}) copy-start(f32[1536]{0:T(1024)} %param.12) | copy-start | bytes 18436
  287.0 24.8 %copy-start.1 = (bf16[512,512]{1,0:T(8,128)(2,1)S(1)}, bf16[512,512]{1,0:T(8,128)(2,1)}, u32[]{:S(2)}) copy-start(bf16[512,512]{1,0:T(8,128)(2,1)} %param.11) | copy-start | bytes 1572868
Sparse Core Ops, SparseCore 0:
  135.5 119.7 all-gather.1
where the time goes:
time: 319 us
  waiting for transfers between devices  115 us (36%)
  blocking collectives  111 us (35%)
  matrix products  34.6 us (11%)
  local copies, waits for them, and re-layouts  25.8 us (8%)
  between operations  14.2 us (4%)
  other arithmetic  11.6 us (4%)
  starting transfers between devices  6.24 us (2%)
    all_gather x1, waiting for transfers between devices, shards(): portion = lax.all_gather(fine_source, 'row', axis=0, tiled=True)  113 us
    all_to_all x1, blocking collectives, shards(): lax.all_to_all(flattened, 'row', split_axis=1, concat_axis=0, tiled=True)  111 us
    dot_general x1, matrix products, shards(): jnp.dot(velocity.reshape(-1, fine_width), deriv_x, preferred_element_type...  24.8 us
    convert_element_type x1, local copies, waits for them, and re-layouts, shards(): along_y.astype(jnp.float32)  15.8 us
    convert_element_type x1, other arithmetic, shards(): along_y.astype(jnp.float32)  7.2 us
  transfers between devices with their start and end apart: 3, of which 2 were waited for; matrix products, arithmetic and copies ran while one was open for 5% of the time, Pallas kernels for 0%

commit v1 on v0

v1 whole, which is shorter than its diff:
```python
import functools

import jax
import jax.numpy as jnp
from jax import lax
from jax.experimental import pallas as pl
from jax.experimental.pallas import tpu as pltpu
from jax.sharding import PartitionSpec as P

rk_weight = 0.5
vmem_bytes = 40 * 1024 * 1024
lanes = 128


def refine_levels(extended):
    lower = extended[:, :-1]
    middle = (0.5 * (lower.astype(jnp.float32) + extended[:, 1:].astype(jnp.float32))).astype(
        jnp.bfloat16
    )
    stacked = jnp.stack([lower, middle], axis=2)
    return stacked.reshape(
        extended.shape[0], 2 * (extended.shape[1] - 1), extended.shape[2], extended.shape[3]
    )


def upsample_table(x_index, x_weight, coarse_width):
    positions = jnp.arange(coarse_width, dtype=jnp.int32)[:, None]
    nothing = jnp.zeros((), jnp.bfloat16)
    left_part = jnp.where(positions == x_index[None, :], x_weight[None, :], nothing)
    right_weight = (1.0 - x_weight.astype(jnp.float32)).astype(jnp.bfloat16)
    right_part = jnp.where(positions == x_index[None, :] + 1, right_weight[None, :], nothing)
    return left_part + right_part


def chosen_levels(coarse_force, row_map):
    portion = lax.all_gather(coarse_force, "row", axis=0, tiled=True)
    coarse_rows = portion.shape[0]
    selector = (row_map[:, None] == jnp.arange(coarse_rows, dtype=jnp.int32)[None, :]).astype(
        jnp.bfloat16
    )
    chosen = (
        jnp.dot(selector, portion.reshape(coarse_rows, -1), preferred_element_type=jnp.float32)
        .astype(jnp.bfloat16)
        .reshape((row_map.shape[0],) + coarse_force.shape[1:])
    )
    slabs = lax.axis_size("slab")
    route = [(i + 1, i) for i in range(slabs - 1)]
    upper_rim = lax.ppermute(chosen[:, :1], "slab", route)
    is_topmost = lax.axis_index("slab") == slabs - 1
    rim_level = jnp.where(is_topmost, chosen[:, -1:], upper_rim)
    return refine_levels(jnp.concatenate([chosen, rim_level], axis=1))


def pack_kernel(component, width, v_ref, *refs):
    blocks, sem = refs[:-1], refs[-1]
    z = lax.axis_index("row") // 2
    copies = []
    for s, block in enumerate(blocks, start=1):
        offset = pl.multiple_of((z ^ s) * width, lanes)
        copies.append(
            pltpu.make_async_copy(
                v_ref.at[:, component, :, pl.ds(offset, width)], block, sem.at[s - 1]
            )
        )
    for copy in copies:
        copy.start()
    for copy in copies:
        copy.wait()


def pack(v, component, zs):
    rows, _, levels, fine_width = v.shape
    width = fine_width // zs
    block = jax.ShapeDtypeStruct((rows, levels, width), v.dtype)
    return pl.pallas_call(
        functools.partial(pack_kernel, component, width),
        out_shape=[block] * (zs - 1),
        in_specs=[pl.BlockSpec(memory_space=pl.ANY)],
        out_specs=[pl.BlockSpec(memory_space=pl.ANY)] * (zs - 1),
        scratch_shapes=[pltpu.SemaphoreType.DMA((zs - 1,))],
        cost_estimate=pl.CostEstimate(
            flops=0, bytes_accessed=2 * (zs - 1) * rows * levels * width * 2, transcendentals=0
        ),
        name="pack",
    )(v)


def slope_kernel(xi_ref, d_ref, m_ref, *refs):
    blocks, (send_ref, own_ref, x_all, y_send) = refs[:-4], refs[-4:]
    rows, levels, width = blocks[0].shape
    each = rows * levels
    for s, block in enumerate(blocks):
        x_all[s * each : (s + 1) * each, :] = (
            block[...].astype(jnp.float32).reshape(each, width)
        )
    count = rows * len(blocks)
    columns = jnp.concatenate(
        [x_all[pl.ds(l, count, stride=levels), :] for l in range(levels)], axis=1
    ).astype(jnp.bfloat16)
    slope = jnp.dot(d_ref[...], columns, preferred_element_type=jnp.float32) * m_ref[...]
    for l in range(levels):
        here = slice(l * width, (l + 1) * width)
        y_send[pl.ds(l, count, stride=levels), :] = slope[:count, here]
        own_ref[pl.ds(l, count, stride=levels), :] = slope[count:, here]
    send_ref[...] = y_send[...].reshape(count, levels, width).astype(jnp.bfloat16)


def slopes(v, component, arrived, order, deriv, metric):
    rows, _, levels, fine_width = v.shape
    zs = len(arrived) + 1
    width = fine_width // zs
    count = rows * zs
    steps = width // lanes
    block = pl.BlockSpec((rows, levels, lanes), lambda g, xi: (0, 0, g))
    return pl.pallas_call(
        slope_kernel,
        grid_spec=pltpu.PrefetchScalarGridSpec(
            num_scalar_prefetch=1,
            grid=(steps,),
            in_specs=[
                pl.BlockSpec(deriv.shape, lambda g, xi: (0, 0)),
                pl.BlockSpec(metric.shape, lambda g, xi: (0, 0)),
                pl.BlockSpec(
                    (rows, None, levels, lanes),
                    lambda g, xi: (0, component, 0, xi[0] * steps + g),
                ),
            ]
            + [block] * (zs - 1),
            out_specs=[
                pl.BlockSpec((count, levels, lanes), lambda g, xi: (0, 0, g)),
                pl.BlockSpec((count * levels, lanes), lambda g, xi: (0, g)),
            ],
            scratch_shapes=[
                pltpu.VMEM((count * levels, lanes), jnp.float32),
                pltpu.VMEM((count * levels, lanes), jnp.float32),
            ],
        ),
        out_shape=[
            jax.ShapeDtypeStruct((count, levels, width), jnp.bfloat16),
            jax.ShapeDtypeStruct((count * levels, width), jnp.float32),
        ],
        compiler_params=pltpu.CompilerParams(vmem_limit_bytes=vmem_bytes),
        cost_estimate=pl.CostEstimate(
            flops=4 * count * count * levels * width,
            bytes_accessed=8 * count * levels * width,
            transcendentals=0,
        ),
        name="slopes",
    )(order, deriv, metric, v, *arrived)


def base_kernel(v_ref, v0_ref, d_ref, m_ref, f_ref, t_ref, base_ref):
    rows, levels, width = v_ref.shape
    flat = v_ref[...].astype(jnp.float32).reshape(rows * levels, width).astype(jnp.bfloat16)
    along = jnp.dot(flat, d_ref[...], preferred_element_type=jnp.float32) * m_ref[...]
    force = f_ref[...].astype(jnp.float32).reshape(rows * levels, -1).astype(jnp.bfloat16)
    forcing = jnp.dot(force, t_ref[...], preferred_element_type=jnp.float32)
    carry = v0_ref[...].astype(jnp.float32).reshape(rows * levels, width)
    base_ref[...] = (forcing - carry * along).reshape(rows, levels, width)


def bases(v, component, deriv_x, metric_x, force, table):
    rows, _, levels, width = v.shape
    part = 32
    coarse_width = table.shape[0]
    return pl.pallas_call(
        base_kernel,
        grid=(rows // part,),
        in_specs=[
            pl.BlockSpec((part, None, levels, width), lambda g: (g, component, 0, 0)),
            pl.BlockSpec((part, None, levels, width), lambda g: (g, 0, 0, 0)),
            pl.BlockSpec(deriv_x.shape, lambda g: (0, 0)),
            pl.BlockSpec(metric_x.shape, lambda g: (0, 0)),
            pl.BlockSpec((None, part, levels, coarse_width), lambda g: (component, g, 0, 0)),
            pl.BlockSpec(table.shape, lambda g: (0, 0)),
        ],
        out_specs=pl.BlockSpec((part, levels, width), lambda g: (g, 0, 0)),
        out_shape=jax.ShapeDtypeStruct((rows, levels, width), jnp.float32),
        compiler_params=pltpu.CompilerParams(vmem_limit_bytes=vmem_bytes),
        cost_estimate=pl.CostEstimate(
            flops=2 * rows * levels * width * (width + coarse_width),
            bytes_accessed=8 * rows * levels * width + 2 * width * width,
            transcendentals=0,
        ),
        name="bases",
    )(v, v, deriv_x, metric_x, force, table)


def combine_kernel(xi_ref, base_ref, v_ref, v1_ref, y_ref, *refs):
    t_ref, u_ref = refs[-2:]
    t = base_ref[...] - v1_ref[...].astype(jnp.float32) * y_ref[...].astype(jnp.float32)
    t_ref[...] = t.astype(jnp.bfloat16)
    u_ref[...] = (v_ref[...].astype(jnp.float32) + rk_weight * t).astype(jnp.bfloat16)


def combine(v, component, s, order, base, along_y, outs):
    rows, _, levels, fine_width = v.shape
    width = along_y.shape[2]
    part = 16
    column = lambda c: pl.BlockSpec(
        (part, None, levels, width), lambda g, xi: (g, c, 0, xi[s])
    )
    whole = pl.BlockSpec(memory_space=pl.ANY)
    return pl.pallas_call(
        combine_kernel,
        grid_spec=pltpu.PrefetchScalarGridSpec(
            num_scalar_prefetch=1,
            grid=(rows // part,),
            in_specs=[
                pl.BlockSpec((part, levels, width), lambda g, xi: (g, 0, xi[s])),
                column(component),
                column(1),
                pl.BlockSpec((part, levels, width), lambda g, xi: (g, 0, 0)),
            ]
            + [whole] * len(outs),
            out_specs=[column(component), column(component)],
        ),
        out_shape=[jax.ShapeDtypeStruct(v.shape, v.dtype)] * 2,
        input_output_aliases={5: 0, 6: 1} if outs else {},
        compiler_params=pltpu.CompilerParams(vmem_limit_bytes=vmem_bytes),
        cost_estimate=pl.CostEstimate(
            flops=4 * rows * levels * width,
            bytes_accessed=14 * rows * levels * width,
            transcendentals=0,
        ),
        name="combine",
    )(order, base, v, v, along_y, *outs)


def ring_shards(
    velocity, deriv_x, deriv_y, metric_x, metric_y, coarse_force, row_map, x_index, x_weight
):
    rows, levels, components, fine_width = velocity.shape
    devices = lax.axis_size("row")
    zs = devices // 2
    me = lax.axis_index("row")
    order = ((me // 2) ^ jnp.arange(zs, dtype=jnp.int32)).astype(jnp.int32)
    v = jnp.transpose(velocity, (0, 2, 1, 3))
    partner = lambda s: [(i, i ^ (2 * s)) for i in range(devices)]
    far_first = sorted(range(1, zs), key=lambda s: -s)

    def exchange(blocks):
        moved = {s: lax.ppermute(blocks[s - 1], "row", partner(s)) for s in far_first}
        return [moved[s] for s in range(1, zs)]

    arrived = [exchange(pack(v, c, zs)) for c in range(components)]

    row_order = [me ^ (2 * s + 1) for s in range(zs)] + [me ^ (2 * s) for s in range(zs)]
    piece = lambda a, at, axis: lax.dynamic_slice_in_dim(a, at * rows, rows, axis)
    by_column = jnp.concatenate([piece(deriv_y, me ^ (2 * s), 1) for s in range(zs)], axis=1)
    deriv = jnp.concatenate([piece(by_column, at, 0) for at in row_order], axis=0)
    metric = jnp.concatenate([piece(metric_y, at, 0) for at in row_order], axis=0)[:, None]

    force = jnp.transpose(chosen_levels(coarse_force, row_map), (2, 0, 1, 3))
    table = upsample_table(x_index, x_weight, coarse_force.shape[3])

    outs = ()
    for c in range(components):
        send, own = slopes(v, c, arrived[c], order, deriv, metric)
        got = lax.ppermute(send, "row", [(i, i ^ 1) for i in range(devices)])
        total = (own.reshape(got.shape) + got.astype(jnp.float32)).astype(jnp.bfloat16)
        pieces = [total[s * rows : (s + 1) * rows] for s in range(zs)]
        along_y = pieces[:1] + exchange(pieces[1:])
        base = bases(v, c, deriv_x, metric_x[None, :], force, table)
        for s in [0] + far_first[::-1]:
            outs = combine(v, c, s, order, base, along_y[s], outs)
    tendency, updated = (jnp.transpose(o, (0, 2, 1, 3)) for o in outs)
    return tendency, updated


def general_shards(
    velocity, deriv_x, deriv_y, metric_x, metric_y, coarse_force, row_map, x_index, x_weight
):
    rows, levels, components, fine_width = velocity.shape
    flattened = velocity.reshape(rows, levels * components * fine_width)
    columns = lax.all_to_all(flattened, "row", split_axis=1, concat_axis=0, tiled=True)
    slope_columns = (
        jnp.dot(deriv_y, columns, preferred_element_type=jnp.float32) * metric_y[:, None]
    ).astype(jnp.bfloat16)
    along_y = lax.all_to_all(slope_columns, "row", split_axis=0, concat_axis=1, tiled=True).reshape(
        velocity.shape
    )
    along_x = (
        jnp.dot(
            velocity.reshape(-1, fine_width), deriv_x, preferred_element_type=jnp.float32
        ).reshape(velocity.shape)
        * metric_x
    )
    coarse_width = coarse_force.shape[3]
    force = chosen_levels(coarse_force, row_map)
    table = upsample_table(x_index, x_weight, coarse_width)
    forcing = jnp.dot(
        force.reshape(-1, coarse_width), table, preferred_element_type=jnp.float32
    ).reshape(velocity.shape)
    moving = velocity.astype(jnp.float32)
    result = forcing - (
        moving[:, :, 0:1] * along_x + moving[:, :, 1:2] * along_y.astype(jnp.float32)
    )
    return (result.astype(jnp.bfloat16), (moving + rk_weight * result).astype(jnp.bfloat16))


def solution(mesh):
    shards = ring_shards if mesh.shape["row"] == 8 else general_shards
    return jax.shard_map(
        shards,
        mesh=mesh,
        in_specs=(
            P("row", "slab", None, None),
            P(),
            P(),
            P(),
            P(),
            P("row", "slab", None, None),
            P("row"),
            P(),
            P(),
        ),
        out_specs=(P("row", "slab", None, None), P("row", "slab", None, None)),
        check_vma=False,
    )
```

time: 319 us -> 357 us (1.12)
  Pallas kernels: 0 us -> 161 us
  waiting for transfers between devices: 115 us -> 41.8 us
  starting transfers between devices: 6.24 us -> 62 us
  blocking collectives: 111 us -> 57.8 us
  matrix products: 34.6 us -> 1.43 us
  between operations: 14.2 us -> 1.09 us
  other arithmetic: 11.6 us -> 6.7 us
    pallas_call x0 -> x21, Pallas kernels: none -> 161 us  [the longest x3 111 us: pack(): pl.pallas_call(functools.partial(pack_kernel, component, width), out_shap...]
    all_gather x1 -> x0, waiting for transfers between devices: 113 us -> none  [shards(): portion = lax.all_gather(fine_source, 'row', axis=0, tiled=True)]
    all_to_all x1 -> x0, blocking collectives: 111 us -> none  [shards(): lax.all_to_all(flattened, 'row', split_axis=1, concat_axis=0, tiled=True)]
    ppermute x1 -> x22, starting transfers between devices: 1.47 us -> 62 us  [the longest x18 57 us: exchange(): lax.ppermute(blocks[s - 1], 'row', partner(s))]
    all_gather x0 -> x1, blocking collectives: none -> 57.8 us  [chosen_levels(): portion = lax.all_gather(coarse_force, 'row', axis=0, tiled=True)]
    ppermute x1 -> x22, waiting for transfers between devices: 1.6 us -> 41.8 us  [the longest x18 24.5 us: exchange(): lax.ppermute(blocks[s - 1], 'row', partner(s))]
    dot_general x4 -> x1, matrix products: 34.6 us -> 1.43 us  [chosen_levels(): jnp.dot(selector, portion.reshape(coarse_rows, -1), preferred_element_typ...]
    convert_element_type x1 -> x0, local copies, waits for them, and re-layouts: 15.8 us -> none  [shards(): along_y.astype(jnp.float32)]
  transfers between devices with their start and end apart: 3 -> 22, of which waited for: 2 -> 6; matrix products, arithmetic and copies ran while one was open for 5% -> 5% of each run, Pallas kernels for 0% -> 34%
where the time goes in v1:
time: 357 us; the launch traced here: 355 us
  Pallas kernels  161 us (45%)
  starting transfers between devices  62 us (17%)
  blocking collectives  57.8 us (16%)
  waiting for transfers between devices  41.8 us (12%)
  local copies, waits for them, and re-layouts  22.8 us (6%)
  other arithmetic  6.7 us (2%)
    pallas_call x3, Pallas kernels, pack(): pl.pallas_call(functools.partial(pack_kernel, component, width), out_shap...  111 us
    all_gather x1, blocking collectives, chosen_levels(): portion = lax.all_gather(coarse_force, 'row', axis=0, tiled=True)  57.8 us
    ppermute x18, starting transfers between devices, exchange(): lax.ppermute(blocks[s - 1], 'row', partner(s))  57 us
    pallas_call x12, Pallas kernels, combine(): pl.pallas_call(combine_kernel, grid_spec=pltpu.PrefetchScalarGridSpec(num...  28.6 us
    ppermute x18, waiting for transfers between devices, exchange(): lax.ppermute(blocks[s - 1], 'row', partner(s))  24.5 us
    ppermute x3, waiting for transfers between devices, ring_shards(): got = lax.ppermute(send, 'row', [(i, i ^ 1) for i in range(devices)])  17.3 us
    unnamed x47, local copies, waits for them, and re-layouts  14.4 us
    pallas_call x3, Pallas kernels, slopes(): pl.pallas_call(slope_kernel, grid_spec=pltpu.PrefetchScalarGridSpec(num_s...  11.7 us
  transfers between devices with their start and end apart: 22, of which 6 were waited for; matrix products, arithmetic and copies ran while one was open for 5% of the time, Pallas kernels for 34%

profile of v1, /device:TPU:0, one launch (start us, length us, event | category | flops | bytes accessed | tf_op | source)
XLA Modules:
  0.0 355.2 jit_solution(599474550383802113)
XLA Ops:
  0.6 36.9 %pack.5 = (bf16[64,8,384]{2,1,0:T(8,128)(2,1)}, bf16[64,8,384]{2,1,0:T(8,128)(2,1)}, bf16[64,8,384]{2,1,0:T(8,128)(2,1)}) custom-call(bf16[64,3,8,1536]{3,2,1,0:T(8,128)(2,1)} %bitcast.23), custom_call_target="tpu_custom_call" | custom-call | bytes 2359296 | tf_op jit(solution)/shard_map/pack/pallas_call | solution.py:75
  37.5 3.1 collective-permute-start.15
  40.6 2.6 collective-permute-start.16
  43.2 57.8 %all_gather.3 = bf16[128,4,3,192]{3,1,2,0:T(4,128)(2,1)S(1)} all-gather(bf16[16,4,3,192]{3,1,2,0:T(4,128)(2,1)S(1)} %copy-done.14), channel_id=1, replica_groups=mesh['slab'=4,'row'=8] {'row'}, dimensions={0}, use_global_device_ids=true | all-gather | bytes 663552 | tf_op jit(solution)/shard_map/all_gather | solution.py:36
  106.1 36.9 %pack.4 = (bf16[64,8,384]{2,1,0:T(8,128)(2,1)}, bf16[64,8,384]{2,1,0:T(8,128)(2,1)}, bf16[64,8,384]{2,1,0:T(8,128)(2,1)}) custom-call(bf16[64,3,8,1536]{3,2,1,0:T(8,128)(2,1)} %bitcast.24), custom_call_target="tpu_custom_call" | custom-call | bytes 2359296 | tf_op jit(solution)/shard_map/pack/pallas_call | solution.py:75
  145.1 3.4 collective-permute-start.9
  148.5 2.3 copy-done
  150.8 4.0 %slopes.5 = (bf16[256,8,384]{2,1,0:T(8,128)(2,1)}, f32[2048,384]{1,0:T(8,128)S(1)}) custom-call(s32[4]{0:T(128)S(1)} %iota_xor_fusion.xi_ref, bf16[512,256]{1,0:T(8,128)(2,1)S(1)} %dynamic-slice_dynamic-update-slice_fusion.d_ref, f32[512,1]{1,0:T(8,128)S(1)} %copy.59.m_ref, bf16[64,3,8,1536]{3,2,1,0:T(8,128)(2,1)S(1)} %bitcast.26, ...), custom_call_target="tpu_custom_call" | custom-call | flops 805306368 | bytes 6291456 | tf_op jit(solution)/shard_map/slopes/pallas_call | solution.py:115
  157.8 36.9 %pack.3 = (bf16[64,8,384]{2,1,0:T(8,128)(2,1)}, bf16[64,8,384]{2,1,0:T(8,128)(2,1)}, bf16[64,8,384]{2,1,0:T(8,128)(2,1)}) custom-call(bf16[64,3,8,1536]{3,2,1,0:T(8,128)(2,1)} %bitcast.25), custom_call_target="tpu_custom_call" | custom-call | bytes 2359296 | tf_op jit(solution)/shard_map/pack/pallas_call | solution.py:75
  195.6 2.9 collective-permute-start.2
  201.7 3.9 %slopes.4 = (bf16[256,8,384]{2,1,0:T(8,128)(2,1)}, f32[2048,384]{1,0:T(8,128)S(1)}) custom-call(s32[4]{0:T(128)S(1)} %iota_xor_fusion.xi_ref, bf16[512,256]{1,0:T(8,128)(2,1)S(1)} %dynamic-slice_dynamic-update-slice_fusion.d_ref, f32[512,1]{1,0:T(8,128)S(1)} %copy.59.m_ref, bf16[64,3,8,1536]{3,2,1,0:T(8,128)(2,1)S(1)} %bitcast.27, ...), custom_call_target="tpu_custom_call" | custom-call | flops 805306368 | bytes 6291456 | tf_op jit(solution)/shard_map/slopes/pallas_call | solution.py:115
  209.8 4.6 %collective-permute-done.1.refs_1_ = bf16[64,8,384]{2,1,0:T(8,128)(2,1)S(1)} collective-permute-done((bf16[64,8,384]{2,1,0:T(8,128)(2,1)}, bf16[64,8,384]{2,1,0:T(8,128)(2,1)S(1)}, u32[]{:S(2)}, u32[]{:S(2)}) %collective-permute-start.1) | collective-permute-done | bytes 393248 | tf_op jit(solution)/shard_map/ppermute | solution.py:243
  214.4 11.1 %collective-permute-done.2.refs_2_ = bf16[64,8,384]{2,1,0:T(8,128)(2,1)S(1)} collective-permute-done((bf16[64,8,384]{2,1,0:T(8,128)(2,1)}, bf16[64,8,384]{2,1,0:T(8,128)(2,1)S(1)}, u32[]{:S(2)}, u32[]{:S(2)}) %collective-permute-start.2) | collective-permute-done | bytes 393248 | tf_op jit(solution)/shard_map/ppermute | solution.py:243
  225.6 3.8 %slopes.3 = (bf16[256,8,384]{2,1,0:T(8,128)(2,1)}, f32[2048,384]{1,0:T(8,128)S(1)}) custom-call(s32[4]{0:T(128)S(1)} %iota_xor_fusion.xi_ref, bf16[512,256]{1,0:T(8,128)(2,1)S(1)} %dynamic-slice_dynamic-update-slice_fusion.d_ref, f32[512,1]{1,0:T(8,128)S(1)} %copy.59.m_ref, bf16[64,3,8,1536]{3,2,1,0:T(8,128)(2,1)S(1)} %bitcast.28, ...), custom_call_target="tpu_custom_call" | custom-call | flops 805306368 | bytes 6291456 | tf_op jit(solution)/shard_map/slopes/pallas_call | solution.py:115
  239.8 3.4 bases.5.base_ref
  245.3 8.1 %collective-permute-start.21 = (bf16[64,8,384]{2,1,0:T(8,128)(2,1)S(1)}, bf16[64,8,384]{2,1,0:T(8,128)(2,1)S(1)}, u32[]{:S(2)}, u32[]{:S(2)}) collective-permute-start(bf16[64,8,384]{2,1,0:T(8,128)(2,1)S(1)} %get-tuple-element.81), channel_id=1, source_target_pairs={{0,2},{1,3},{2,0},{3,1},{4,6},{5,7},{6,4},{7,5},{8,10},{9,11},{10,... | collective-permute-start | bytes 1179656 | tf_op jit(solution)/shard_map/ppermute | solution.py:243
  253.4 2.4 collective-permute-start.19
  259.8 17.3 %collective-permute-done.4 = bf16[256,8,384]{2,1,0:T(8,128)(2,1)} collective-permute-done((bf16[256,8,384]{2,1,0:T(8,128)(2,1)}, bf16[256,8,384]{2,1,0:T(8,128)(2,1)}, u32[]{:S(2)}, u32[]{:S(2)}) %collective-permute-start.4) | collective-permute-done | bytes 1572896 | tf_op jit(solution)/shard_map/ppermute | solution.py:260
  283.4 25.7 %collective-permute-start.6 = (bf16[64,8,384]{2,1,0:T(8,128)(2,1)}, bf16[64,8,384]{2,1,0:T(8,128)(2,1)S(1)}, u32[]{:S(2)}, u32[]{:S(2)}) collective-permute-start(bf16[64,8,384]{2,1,0:T(8,128)(2,1)} %get-tuple-element.90), channel_id=1, source_target_pairs={{0,4},{1,5},{2,6},{3,7},{4,0},{5,1},{6,2},{7,3},{8,12},{9,13},{10,... | collective-permute-start | bytes 1179656 | tf_op jit(solution)/shard_map/ppermute | solution.py:243
  309.1 2.4 collective-permute-start.5
  311.5 3.4 bases.4.base_ref
  314.9 3.7 %bases.3.base_ref = f32[64,8,1536]{2,1,0:T(8,128)S(1)} custom-call(bf16[64,3,8,1536]{3,2,1,0:T(8,128)(2,1)S(1)} %bitcast.33, bf16[64,3,8,1536]{3,2,1,0:T(8,128)(2,1)S(1)} %bitcast.34, bf16[1536,1536]{1,0:T(8,128)(2,1)S(1)} %copy-done.3, f32[1,1536]{1,0:T(1,128)S(1)} %broadcast_in_dim.33.m_ref, bf16[3,64,8,192]{3,2,1,0:T(8,128)(2,1)S(1)} %bitcast.61, ...), custom_call_target="tpu_custom_call" | custom-call | flops 2717908992 | bytes 11010048 | tf_op jit(solution)/shard_map/bases/pallas_call | solution.py:166
  336.1 3.9 %combine.19 = (bf16[64,3,8,1536]{3,2,1,0:T(8,128)(2,1)}, bf16[64,3,8,1536]{3,2,1,0:T(8,128)(2,1)}) custom-call(s32[4]{0:T(128)S(1)} %iota_xor_fusion.xi_ref, f32[64,8,1536]{2,1,0:T(8,128)S(1)} %bases.4.base_ref, bf16[64,3,8,1536]{3,2,1,0:T(8,128)(2,1)S(1)} %bitcast.49, ...), custom_call_target="tpu_custom_call", output_to_operand_aliasing={{0}: (5, {}), {1}: (6, {})} | custom-call | flops 786432 | bytes 2752512 | tf_op jit(solution)/shard_map/combine/pallas_call | solution.py:204
  344.5 6.2 %collective-permute-done.6.y_ref = bf16[64,8,384]{2,1,0:T(8,128)(2,1)S(1)} collective-permute-done((bf16[64,8,384]{2,1,0:T(8,128)(2,1)}, bf16[64,8,384]{2,1,0:T(8,128)(2,1)S(1)}, u32[]{:S(2)}, u32[]{:S(2)}) %collective-permute-start.6) | collective-permute-done | bytes 393248 | tf_op jit(solution)/shard_map/ppermute | solution.py:243
  (118 shorter events, 67.3 us)
Async XLA Ops:
  0.6 42.6 %copy-start.14 = (bf16[16,4,3,192]{3,1,2,0:T(4,128)(2,1)S(1)}, bf16[16,4,3,192]{3,1,2,0:T(4,128)(2,1)}, u32[]{:S(2)}) copy-start(bf16[16,4,3,192]{3,1,2,0:T(4,128)(2,1)} %param.14) | copy-start | bytes 221188
  0.6 101.8 %copy-start.19 = (s32[64]{0:T(128)S(1)}, s32[64]{0:T(128)}, u32[]{:S(2)}) copy-start(s32[64]{0:T(128)} %param.15) | copy-start | bytes 772
  37.5 107.4 %collective-permute-start.15 = (bf16[64,8,384]{2,1,0:T(8,128)(2,1)}, bf16[64,8,384]{2,1,0:T(8,128)(2,1)S(1)}, u32[]{:S(2)}, u32[]{:S(2)}) collective-permute-start(bf16[64,8,384]{2,1,0:T(8,128)(2,1)} %get-tuple-element.51), channel_id=1, source_target_pairs={{0,2},{1,3},{2,0},{3,1},{4,6},{5,7},{6,4},{7,5},{8,10},{9,11},{10,... | collective-permute-start | bytes 1179656 | tf_op jit(solution)/shard_map/ppermute | solution.py:243
  40.6 104.4 %collective-permute-start.16 = (bf16[64,8,384]{2,1,0:T(8,128)(2,1)}, bf16[64,8,384]{2,1,0:T(8,128)(2,1)S(1)}, u32[]{:S(2)}, u32[]{:S(2)}) collective-permute-start(bf16[64,8,384]{2,1,0:T(8,128)(2,1)} %get-tuple-element.52), channel_id=1, source_target_pairs={{0,4},{1,5},{2,6},{3,7},{4,0},{5,1},{6,2},{7,3},{8,12},{9,13},{10,... | collective-permute-start | bytes 1179656 | tf_op jit(solution)/shard_map/ppermute | solution.py:243
  43.2 105.3 %collective-permute-start.17 = (bf16[64,8,384]{2,1,0:T(8,128)(2,1)}, bf16[64,8,384]{2,1,0:T(8,128)(2,1)S(1)}, u32[]{:S(2)}, u32[]{:S(2)}) collective-permute-start(bf16[64,8,384]{2,1,0:T(8,128)(2,1)} %get-tuple-element.53), channel_id=1, source_target_pairs={{0,6},{1,7},{2,4},{3,5},{4,2},{5,3},{6,0},{7,1},{8,14},{9,15},{10,... | collective-permute-start | bytes 1179656 | tf_op jit(solution)/shard_map/ppermute | solution.py:243
  104.7 102.6 %collective-permute-start = (bf16[64,1,3,192]{3,0,2,1:T(8,128)(2,1)S(1)}, bf16[64,1,3,192]{3,0,2,1:T(8,128)(2,1)S(1)}, u32[]{:S(2)}, u32[]{:S(2)}) collective-permute-start(bf16[64,1,3,192]{3,0,2,1:T(8,128)(2,1)S(1)} %slice.61), channel_id=1, source_target_pairs={{8,0},{16,8},{24,16},{9,1},{17,9},{25,17},{10,2},{18,10},{26,18},{... | collective-permute-start | bytes 221192 | tf_op jit(solution)/shard_map/ppermute | solution.py:48
  143.0 51.9 %collective-permute-start.10 = (bf16[64,8,384]{2,1,0:T(8,128)(2,1)}, bf16[64,8,384]{2,1,0:T(8,128)(2,1)S(1)}, u32[]{:S(2)}, u32[]{:S(2)}) collective-permute-start(bf16[64,8,384]{2,1,0:T(8,128)(2,1)} %get-tuple-element.48), channel_id=1, source_target_pairs={{0,6},{1,7},{2,4},{3,5},{4,2},{5,3},{6,0},{7,1},{8,14},{9,15},{10,... | collective-permute-start | bytes 1179656 | tf_op jit(solution)/shard_map/ppermute | solution.py:243
  145.0 50.6 %collective-permute-start.8 = (bf16[64,8,384]{2,1,0:T(8,128)(2,1)}, bf16[64,8,384]{2,1,0:T(8,128)(2,1)S(1)}, u32[]{:S(2)}, u32[]{:S(2)}) collective-permute-start(bf16[64,8,384]{2,1,0:T(8,128)(2,1)} %get-tuple-element.46), channel_id=1, source_target_pairs={{0,2},{1,3},{2,0},{3,1},{4,6},{5,7},{6,4},{7,5},{8,10},{9,11},{10,... | collective-permute-start | bytes 1179656 | tf_op jit(solution)/shard_map/ppermute | solution.py:243
  145.1 53.4 %collective-permute-start.9 = (bf16[64,8,384]{2,1,0:T(8,128)(2,1)}, bf16[64,8,384]{2,1,0:T(8,128)(2,1)S(1)}, u32[]{:S(2)}, u32[]{:S(2)}) collective-permute-start(bf16[64,8,384]{2,1,0:T(8,128)(2,1)} %get-tuple-element.47), channel_id=1, source_target_pairs={{0,4},{1,5},{2,6},{3,7},{4,0},{5,1},{6,2},{7,3},{8,12},{9,13},{10,... | collective-permute-start | bytes 1179656 | tf_op jit(solution)/shard_map/ppermute | solution.py:243
  156.4 86.8 %collective-permute-start.18 = (bf16[256,8,384]{2,1,0:T(8,128)(2,1)}, bf16[256,8,384]{2,1,0:T(8,128)(2,1)}, u32[]{:S(2)}, u32[]{:S(2)}) collective-permute-start(bf16[256,8,384]{2,1,0:T(8,128)(2,1)} %get-tuple-element.55), channel_id=1, source_target_pairs={{0,1},{1,0},{2,3},{3,2},{4,5},{5,4},{6,7},{7,6},{8,9},{9,8},{10,11... | collective-permute-start | bytes 4718600 | tf_op jit(solution)/shard_map/ppermute | solution.py:260
  194.9 19.5 %collective-permute-start.1 = (bf16[64,8,384]{2,1,0:T(8,128)(2,1)}, bf16[64,8,384]{2,1,0:T(8,128)(2,1)S(1)}, u32[]{:S(2)}, u32[]{:S(2)}) collective-permute-start(bf16[64,8,384]{2,1,0:T(8,128)(2,1)} %get-tuple-element.41), channel_id=1, source_target_pairs={{0,2},{1,3},{2,0},{3,1},{4,6},{5,7},{6,4},{7,5},{8,10},{9,11},{10,... | collective-permute-start | bytes 1179656 | tf_op jit(solution)/shard_map/ppermute | solution.py:243
  195.6 30.0 %collective-permute-start.2 = (bf16[64,8,384]{2,1,0:T(8,128)(2,1)}, bf16[64,8,384]{2,1,0:T(8,128)(2,1)S(1)}, u32[]{:S(2)}, u32[]{:S(2)}) collective-permute-start(bf16[64,8,384]{2,1,0:T(8,128)(2,1)} %get-tuple-element.42), channel_id=1, source_target_pairs={{0,4},{1,5},{2,6},{3,7},{4,0},{5,1},{6,2},{7,3},{8,12},{9,13},{10,... | collective-permute-start | bytes 1179656 | tf_op jit(solution)/shard_map/ppermute | solution.py:243
  198.5 27.1 %collective-permute-start.3 = (bf16[64,8,384]{2,1,0:T(8,128)(2,1)}, bf16[64,8,384]{2,1,0:T(8,128)(2,1)S(1)}, u32[]{:S(2)}, u32[]{:S(2)}) collective-permute-start(bf16[64,8,384]{2,1,0:T(8,128)(2,1)} %get-tuple-element.43), channel_id=1, source_target_pairs={{0,6},{1,7},{2,4},{3,5},{4,2},{5,3},{6,0},{7,1},{8,14},{9,15},{10,... | collective-permute-start | bytes 1179656 | tf_op jit(solution)/shard_map/ppermute | solution.py:243
  207.3 48.6 %collective-permute-start.11 = (bf16[256,8,384]{2,1,0:T(8,128)(2,1)}, bf16[256,8,384]{2,1,0:T(8,128)(2,1)}, u32[]{:S(2)}, u32[]{:S(2)}) collective-permute-start(bf16[256,8,384]{2,1,0:T(8,128)(2,1)} %get-tuple-element.50), channel_id=1, source_target_pairs={{0,1},{1,0},{2,3},{3,2},{4,5},{5,4},{6,7},{7,6},{8,9},{9,8},{10,11... | collective-permute-start | bytes 4718600 | tf_op jit(solution)/shard_map/ppermute | solution.py:260
  231.1 46.0 %collective-permute-start.4 = (bf16[256,8,384]{2,1,0:T(8,128)(2,1)}, bf16[256,8,384]{2,1,0:T(8,128)(2,1)}, u32[]{:S(2)}, u32[]{:S(2)}) collective-permute-start(bf16[256,8,384]{2,1,0:T(8,128)(2,1)} %get-tuple-element.45), channel_id=1, source_target_pairs={{0,1},{1,0},{2,3},{3,2},{4,5},{5,4},{6,7},{7,6},{8,9},{9,8},{10,11... | collective-permute-start | bytes 4718600 | tf_op jit(solution)/shard_map/ppermute | solution.py:260
  245.3 35.2 %collective-permute-start.21 = (bf16[64,8,384]{2,1,0:T(8,128)(2,1)S(1)}, bf16[64,8,384]{2,1,0:T(8,128)(2,1)S(1)}, u32[]{:S(2)}, u32[]{:S(2)}) collective-permute-start(bf16[64,8,384]{2,1,0:T(8,128)(2,1)S(1)} %get-tuple-element.81), channel_id=1, source_target_pairs={{0,2},{1,3},{2,0},{3,1},{4,6},{5,7},{6,4},{7,5},{8,10},{9,11},{10,... | collective-permute-start | bytes 1179656 | tf_op jit(solution)/shard_map/ppermute | solution.py:243
  253.4 29.8 %collective-permute-start.20 = (bf16[64,8,384]{2,1,0:T(8,128)(2,1)S(1)}, bf16[64,8,384]{2,1,0:T(8,128)(2,1)S(1)}, u32[]{:S(2)}, u32[]{:S(2)}) collective-permute-start(bf16[64,8,384]{2,1,0:T(8,128)(2,1)S(1)} %get-tuple-element.82), channel_id=1, source_target_pairs={{0,4},{1,5},{2,6},{3,7},{4,0},{5,1},{6,2},{7,3},{8,12},{9,13},{10,... | collective-permute-start | bytes 1179656 | tf_op jit(solution)/shard_map/ppermute | solution.py:243
  253.4 29.9 %collective-permute-start.19 = (bf16[64,8,384]{2,1,0:T(8,128)(2,1)S(1)}, bf16[64,8,384]{2,1,0:T(8,128)(2,1)S(1)}, u32[]{:S(2)}, u32[]{:S(2)}) collective-permute-start(bf16[64,8,384]{2,1,0:T(8,128)(2,1)S(1)} %get-tuple-element.83), channel_id=1, source_target_pairs={{0,6},{1,7},{2,4},{3,5},{4,2},{5,3},{6,0},{7,1},{8,14},{9,15},{10,... | collective-permute-start | bytes 1179656 | tf_op jit(solution)/shard_map/ppermute | solution.py:243
  258.7 50.3 %collective-permute-start.14 = (bf16[64,8,384]{2,1,0:T(8,128)(2,1)S(1)}, bf16[64,8,384]{2,1,0:T(8,128)(2,1)S(1)}, u32[]{:S(2)}, u32[]{:S(2)}) collective-permute-start(bf16[64,8,384]{2,1,0:T(8,128)(2,1)S(1)} %get-tuple-element.85), channel_id=1, source_target_pairs={{0,2},{1,3},{2,0},{3,1},{4,6},{5,7},{6,4},{7,5},{8,10},{9,11},{10,... | collective-permute-start | bytes 1179656 | tf_op jit(solution)/shard_map/ppermute | solution.py:243
  277.0 56.8 %collective-permute-start.13 = (bf16[64,8,384]{2,1,0:T(8,128)(2,1)}, bf16[64,8,384]{2,1,0:T(8,128)(2,1)S(1)}, u32[]{:S(2)}, u32[]{:S(2)}) collective-permute-start(bf16[64,8,384]{2,1,0:T(8,128)(2,1)} %get-tuple-element.86), channel_id=1, source_target_pairs={{0,4},{1,5},{2,6},{3,7},{4,0},{5,1},{6,2},{7,3},{8,12},{9,13},{10,... | collective-permute-start | bytes 1179656 | tf_op jit(solution)/shard_map/ppermute | solution.py:243
  280.5 55.6 %collective-permute-start.12 = (bf16[64,8,384]{2,1,0:T(8,128)(2,1)}, bf16[64,8,384]{2,1,0:T(8,128)(2,1)}, u32[]{:S(2)}, u32[]{:S(2)}) collective-permute-start(bf16[64,8,384]{2,1,0:T(8,128)(2,1)} %get-tuple-element.87), channel_id=1, source_target_pairs={{0,6},{1,7},{2,4},{3,5},{4,2},{5,3},{6,0},{7,1},{8,14},{9,15},{10,... | collective-permute-start | bytes 1179656 | tf_op jit(solution)/shard_map/ppermute | solution.py:243
  283.3 58.9 %collective-permute-start.7 = (bf16[64,8,384]{2,1,0:T(8,128)(2,1)}, bf16[64,8,384]{2,1,0:T(8,128)(2,1)S(1)}, u32[]{:S(2)}, u32[]{:S(2)}) collective-permute-start(bf16[64,8,384]{2,1,0:T(8,128)(2,1)} %get-tuple-element.89), channel_id=1, source_target_pairs={{0,2},{1,3},{2,0},{3,1},{4,6},{5,7},{6,4},{7,5},{8,10},{9,11},{10,... | collective-permute-start | bytes 1179656 | tf_op jit(solution)/shard_map/ppermute | solution.py:243
  283.4 67.3 %collective-permute-start.6 = (bf16[64,8,384]{2,1,0:T(8,128)(2,1)}, bf16[64,8,384]{2,1,0:T(8,128)(2,1)S(1)}, u32[]{:S(2)}, u32[]{:S(2)}) collective-permute-start(bf16[64,8,384]{2,1,0:T(8,128)(2,1)} %get-tuple-element.90), channel_id=1, source_target_pairs={{0,4},{1,5},{2,6},{3,7},{4,0},{5,1},{6,2},{7,3},{8,12},{9,13},{10,... | collective-permute-start | bytes 1179656 | tf_op jit(solution)/shard_map/ppermute | solution.py:243
  309.1 43.9 %collective-permute-start.5 = (bf16[64,8,384]{2,1,0:T(8,128)(2,1)}, bf16[64,8,384]{2,1,0:T(8,128)(2,1)S(1)}, u32[]{:S(2)}, u32[]{:S(2)}) collective-permute-start(bf16[64,8,384]{2,1,0:T(8,128)(2,1)} %get-tuple-element.91), channel_id=1, source_target_pairs={{0,6},{1,7},{2,4},{3,5},{4,2},{5,3},{6,0},{7,1},{8,14},{9,15},{10,... | collective-permute-start | bytes 1179656 | tf_op jit(solution)/shard_map/ppermute | solution.py:243
  (18 other events, 280.9 us)

commit v2 on v0

v2 whole, which is shorter than its diff:
```python
import functools

import jax
import jax.numpy as jnp
from jax import lax
from jax.experimental import pallas as pl
from jax.experimental.pallas import tpu as pltpu
from jax.sharding import PartitionSpec as P

rk_weight = 0.5
mib = 1024 * 1024
lanes = 128
in_flight = 5
light = pl.CostEstimate(flops=1, bytes_accessed=1, transcendentals=0)


def refine_levels(extended):
    lower = extended[:, :-1]
    middle = (0.5 * (lower.astype(jnp.float32) + extended[:, 1:].astype(jnp.float32))).astype(
        jnp.bfloat16
    )
    stacked = jnp.stack([lower, middle], axis=2)
    return stacked.reshape(
        extended.shape[0], 2 * (extended.shape[1] - 1), extended.shape[2], extended.shape[3]
    )


def upsample_table(x_index, x_weight, coarse_width):
    positions = jnp.arange(coarse_width, dtype=jnp.int32)[:, None]
    nothing = jnp.zeros((), jnp.bfloat16)
    left_part = jnp.where(positions == x_index[None, :], x_weight[None, :], nothing)
    right_weight = (1.0 - x_weight.astype(jnp.float32)).astype(jnp.bfloat16)
    right_part = jnp.where(positions == x_index[None, :] + 1, right_weight[None, :], nothing)
    return left_part + right_part


def chosen_levels(portion, coarse_rows, row_map):
    selector = (row_map[:, None] == coarse_rows[None, :]).astype(jnp.bfloat16)
    chosen = (
        jnp.dot(
            selector, portion.reshape(portion.shape[0], -1), preferred_element_type=jnp.float32
        )
        .astype(jnp.bfloat16)
        .reshape((row_map.shape[0],) + portion.shape[1:])
    )
    return extended_levels(chosen)


def extended_levels(chosen):
    slabs = lax.axis_size("slab")
    route = [(i + 1, i) for i in range(slabs - 1)]
    upper_rim = lax.ppermute(chosen[:, :1], "slab", route)
    is_topmost = lax.axis_index("slab") == slabs - 1
    rim_level = jnp.where(is_topmost, chosen[:, -1:], upper_rim)
    return refine_levels(jnp.concatenate([chosen, rim_level], axis=1))


def pack_kernel(xi_ref, v_ref, *refs):
    blocks, wide = refs[:-1], refs[-1]
    rows, comps, levels, width = v_ref.shape
    half = levels // 2
    for c in range(comps):
        for j in range(width // lanes):
            lane = slice(j * lanes, (j + 1) * lanes)
            wide[...] = v_ref[:, c, :, lane].astype(jnp.float32).reshape(rows * levels, lanes)
            for i, block in enumerate(blocks):
                start = (xi_ref[0] ^ i) * half
                for l in range(half):
                    level = wide[pl.ds(start + l, rows, stride=levels), :]
                    block[c * half + l, :, lane] = level.astype(block.dtype)


def pack(v, comps, s, prefetch):
    rows, _, levels, fine_width = v.shape
    zs = prefetch.shape[0] - 1
    width = fine_width // zs
    planes = len(comps) * levels // 2
    part = rows // 2
    block = jax.ShapeDtypeStruct((2 * planes, part, width), v.dtype)
    return pl.pallas_call(
        pack_kernel,
        grid_spec=pltpu.PrefetchScalarGridSpec(
            num_scalar_prefetch=1,
            grid=(2,),
            in_specs=[
                pl.BlockSpec(
                    (part, len(comps), levels, width),
                    lambda g, xi: (g, comps[0] // len(comps), 0, xi[1 + s]),
                )
            ],
            out_specs=[pl.BlockSpec((planes, part, width), lambda g, xi: (g, 0, 0))] * 2,
            scratch_shapes=[pltpu.VMEM((part * levels, lanes), jnp.float32)],
        ),
        out_shape=[block] * 2,
        compiler_params=pltpu.CompilerParams(vmem_limit_bytes=60 * mib),
        cost_estimate=light,
        name="pack",
    )(prefetch, v)


def slope_kernel(planes, d_ref, m_ref, *refs):
    count = len(refs) // 2
    sources, results = refs[:count], refs[count:]
    part, width = sources[0].shape[1:]
    for q in range(planes):
        columns = jnp.concatenate(
            [source[h * planes + q] for source in sources for h in range(2)], axis=0
        )
        slope = jnp.dot(d_ref[...], columns, preferred_element_type=jnp.float32) * m_ref[...]
        slope = slope.astype(jnp.bfloat16)
        for k, result in enumerate(results):
            for h in range(2):
                at = (2 * k + h) * part
                result[h * planes + q] = slope[at : at + part]


def slopes(blocks, planes, deriv, metric):
    part, width = blocks[0].shape[1:]
    count = len(blocks)
    result = jax.ShapeDtypeStruct((2 * planes, part, width), jnp.bfloat16)
    area = deriv.shape[0] * planes * width
    return pl.pallas_call(
        functools.partial(slope_kernel, planes),
        in_specs=[pl.BlockSpec(memory_space=pltpu.VMEM)] * (2 + count),
        out_specs=[pl.BlockSpec(memory_space=pltpu.VMEM)] * count,
        out_shape=[result] * count,
        compiler_params=pltpu.CompilerParams(vmem_limit_bytes=32 * mib),
        cost_estimate=light,
        name="slopes",
    )(deriv, metric, *blocks)


def hold_kernel(block_ref, *refs):
    refs[-1][...] = block_ref[...]


def hold(block, after):
    return pl.pallas_call(
        hold_kernel,
        in_specs=[pl.BlockSpec(memory_space=pltpu.VMEM)]
        + [pl.BlockSpec(memory_space=pl.ANY)] * len(after),
        out_specs=pl.BlockSpec(memory_space=pltpu.VMEM),
        out_shape=jax.ShapeDtypeStruct(block.shape, block.dtype),
        compiler_params=pltpu.CompilerParams(vmem_limit_bytes=8 * mib),
        cost_estimate=light,
        name="hold",
    )(block, *after)


def base_kernel(v_ref, v0_ref, d_ref, m_ref, f_ref, t_ref, base_ref):
    rows, levels, width = v_ref.shape
    flat = v_ref[...].astype(jnp.float32).reshape(rows * levels, width).astype(jnp.bfloat16)
    along = jnp.dot(flat, d_ref[...], preferred_element_type=jnp.float32) * m_ref[...]
    force = f_ref[...].astype(jnp.float32).reshape(rows * levels, -1).astype(jnp.bfloat16)
    forcing = jnp.dot(force, t_ref[...], preferred_element_type=jnp.float32)
    carry = v0_ref[...].astype(jnp.float32).reshape(rows * levels, width)
    base_ref[...] = (forcing - carry * along).reshape(rows, levels, width)


def bases(v, component, deriv_x, metric_x, force, table):
    rows, _, levels, width = v.shape
    part = 32
    coarse_width = table.shape[0]
    return pl.pallas_call(
        base_kernel,
        grid=(rows // part,),
        in_specs=[
            pl.BlockSpec((part, None, levels, width), lambda g: (g, component, 0, 0)),
            pl.BlockSpec((part, None, levels, width), lambda g: (g, 0, 0, 0)),
            pl.BlockSpec(deriv_x.shape, lambda g: (0, 0)),
            pl.BlockSpec(metric_x.shape, lambda g: (0, 0)),
            pl.BlockSpec((None, part, levels, coarse_width), lambda g: (component, g, 0, 0)),
            pl.BlockSpec(table.shape, lambda g: (0, 0)),
        ],
        out_specs=pl.BlockSpec((part, levels, width), lambda g: (g, 0, 0)),
        out_shape=jax.ShapeDtypeStruct((rows, levels, width), jnp.float32),
        compiler_params=pltpu.CompilerParams(vmem_limit_bytes=32 * mib),
        cost_estimate=light,
        name="bases",
    )(v, v, deriv_x, metric_x, force, table)


def combine_kernel(xi_ref, base_ref, v_ref, v1_ref, near_ref, far_ref, *refs):
    t_ref, u_ref, along = refs[-3:]
    rows, levels, width = base_ref.shape
    half = levels // 2
    for j in range(width // lanes):
        lane = slice(j * lanes, (j + 1) * lanes)
        for i, block in enumerate((near_ref, far_ref)):
            start = (xi_ref[0] ^ i) * half
            for l in range(half):
                plane = block[l, :, lane].astype(jnp.float32)
                along[pl.ds(start + l, rows, stride=levels), :] = plane
        along_y = along[...].reshape(rows, levels, lanes)
        t = base_ref[:, :, lane] - v1_ref[:, :, lane].astype(jnp.float32) * along_y
        t_ref[:, :, lane] = t.astype(jnp.bfloat16)
        moved = v_ref[:, :, lane].astype(jnp.float32) + rk_weight * t
        u_ref[:, :, lane] = moved.astype(jnp.bfloat16)


def combine(v, component, at, s, prefetch, base, near, far, outs):
    rows, _, levels, fine_width = v.shape
    part, width = near.shape[1:]
    half = levels // 2
    per_half = near.shape[0] // 2 // half
    column = lambda c: pl.BlockSpec(
        (part, None, levels, width), lambda g, xi: (g, c, 0, xi[1 + s])
    )
    planes = pl.BlockSpec((half, part, width), lambda g, xi: (g * per_half + at, 0, 0))
    return pl.pallas_call(
        combine_kernel,
        grid_spec=pltpu.PrefetchScalarGridSpec(
            num_scalar_prefetch=1,
            grid=(rows // part,),
            in_specs=[
                pl.BlockSpec((part, levels, width), lambda g, xi: (g, 0, xi[1 + s])),
                column(component),
                column(1),
                planes,
                planes,
            ]
            + [pl.BlockSpec(memory_space=pl.ANY)] * len(outs),
            out_specs=[column(component), column(component)],
            scratch_shapes=[pltpu.VMEM((part * levels, lanes), jnp.float32)],
        ),
        out_shape=[jax.ShapeDtypeStruct(v.shape, v.dtype)] * 2,
        input_output_aliases={6: 0, 7: 1} if outs else {},
        compiler_params=pltpu.CompilerParams(vmem_limit_bytes=16 * mib),
        cost_estimate=light,
        name="combine",
    )(prefetch, base, v, v, near, far, *outs)


def ring_shards(
    velocity, deriv_x, deriv_y, metric_x, metric_y, coarse_force, row_map, x_index, x_weight
):
    rows, levels, components, fine_width = velocity.shape
    devices = lax.axis_size("row")
    zs = devices // 2
    me = lax.axis_index("row").astype(jnp.int32)
    prefetch = jnp.concatenate([(me % 2)[None], (me // 2) ^ jnp.arange(zs, dtype=jnp.int32)])
    v = jnp.transpose(velocity, (0, 2, 1, 3))
    arrival = [0, 4, 2, 5, 6, 3, 7, 1]
    place = {k: at for at, k in enumerate(arrival)}
    moved = []

    def trade(block, k):
        if len(moved) >= in_flight:
            block, moved[-in_flight] = lax.optimization_barrier((block, moved[-in_flight]))
        moved.append(lax.ppermute(block, "row", [(i, i ^ k) for i in range(devices)]))
        return moved[-1]

    def exchange(blocks):
        here = [blocks[0]]
        for k, block in zip(arrival[1:], blocks[1:]):
            here.append(trade(block, k))
        return here

    coarse_here, coarse_levels, _, coarse_width = coarse_force.shape
    row_size = coarse_levels * components * coarse_width
    coarse = jnp.transpose(coarse_force, (0, 2, 1, 3))
    portion = jnp.concatenate([coarse, trade(coarse, 4)], axis=0)

    chunks = [(0, 1), (2,)]
    arrived = []
    for comps in chunks:
        blocks = {}
        for s in (2, 1, 3, 0):
            blocks[2 * s], blocks[2 * s + 1] = pack(v, comps, s, prefetch)
        arrived.append(exchange([blocks[k] for k in arrival]))
        k = 2 if len(arrived) == 1 else 1
        portion = jnp.concatenate([portion, trade(portion, k)], axis=0)

    partners = [me ^ k for k in arrival]
    piece = lambda a, at, axis: lax.dynamic_slice_in_dim(a, at * rows, rows, axis)
    by_column = jnp.concatenate([piece(deriv_y, at, 1) for at in partners], axis=1)
    deriv = jnp.concatenate([piece(by_column, at, 0) for at in partners], axis=0)
    metric = jnp.concatenate([piece(metric_y, at, 0) for at in partners], axis=0)[:, None]

    holders = jnp.stack([me ^ k for k in (0, 4, 2, 6, 1, 5, 3, 7)])
    coarse_rows = (
        holders[:, None] * coarse_here + jnp.arange(coarse_here, dtype=jnp.int32)
    ).reshape(-1)
    portion = portion.reshape(-1, row_size)
    selector = (row_map[:, None] == coarse_rows[None, :]).astype(jnp.bfloat16)
    chosen = jnp.dot(selector, portion, preferred_element_type=jnp.float32).astype(jnp.bfloat16)
    chosen = chosen.reshape(rows, components, coarse_levels, coarse_width)
    force = jnp.transpose(
        extended_levels(jnp.transpose(chosen, (0, 2, 1, 3))), (2, 0, 1, 3)
    )
    table = upsample_table(x_index, x_weight, coarse_width)

    base = [
        bases(v, c, deriv_x, metric_x[None, :], force, table) for c in range(components)
    ]
    outs = ()
    for comps, blocks in zip(chunks, arrived):
        sent = list(slopes(blocks, len(comps) * levels // 2, deriv, metric))
        if outs:
            sent[-1] = hold(sent[-1], (*outs, base[comps[0]]))
        along_y = exchange(sent)
        for at, c in enumerate(comps):
            for s in (2, 3, 1, 0):
                near, far = along_y[place[2 * s]], along_y[place[2 * s + 1]]
                outs = combine(v, c, at, s, prefetch, base[c], near, far, outs)
    tendency, updated = (jnp.transpose(o, (0, 2, 1, 3)) for o in outs)
    return tendency, updated


def general_shards(
    velocity, deriv_x, deriv_y, metric_x, metric_y, coarse_force, row_map, x_index, x_weight
):
    rows, levels, components, fine_width = velocity.shape
    flattened = velocity.reshape(rows, levels * components * fine_width)
    columns = lax.all_to_all(flattened, "row", split_axis=1, concat_axis=0, tiled=True)
    slope_columns = (
        jnp.dot(deriv_y, columns, preferred_element_type=jnp.float32) * metric_y[:, None]
    ).astype(jnp.bfloat16)
    along_y = lax.all_to_all(slope_columns, "row", split_axis=0, concat_axis=1, tiled=True).reshape(
        velocity.shape
    )
    along_x = (
        jnp.dot(
            velocity.reshape(-1, fine_width), deriv_x, preferred_element_type=jnp.float32
        ).reshape(velocity.shape)
        * metric_x
    )
    coarse_width = coarse_force.shape[3]
    portion = lax.all_gather(coarse_force, "row", axis=0, tiled=True)
    force = chosen_levels(portion, jnp.arange(portion.shape[0], dtype=jnp.int32), row_map)
    table = upsample_table(x_index, x_weight, coarse_width)
    forcing = jnp.dot(
        force.reshape(-1, coarse_width), table, preferred_element_type=jnp.float32
    ).reshape(velocity.shape)
    moving = velocity.astype(jnp.float32)
    result = forcing - (
        moving[:, :, 0:1] * along_x + moving[:, :, 1:2] * along_y.astype(jnp.float32)
    )
    return (result.astype(jnp.bfloat16), (moving + rk_weight * result).astype(jnp.bfloat16))


def solution(mesh):
    shards = ring_shards if mesh.shape["row"] == 8 else general_shards
    return jax.shard_map(
        shards,
        mesh=mesh,
        in_specs=(
            P("row", "slab", None, None),
            P(),
            P(),
            P(),
            P(),
            P("row", "slab", None, None),
            P("row"),
            P(),
            P(),
        ),
        out_specs=(P("row", "slab", None, None), P("row", "slab", None, None)),
        check_vma=False,
    )
```

time: 319 us -> 237 us (0.74)
  blocking collectives: 111 us -> 0 us
  Pallas kernels: 0 us -> 62.1 us
  starting transfers between devices: 6.24 us -> 63.6 us
  waiting for transfers between devices: 115 us -> 63.7 us
  matrix products: 34.6 us -> 1.74 us
  between operations: 14.2 us -> 0.99 us
  local copies, waits for them, and re-layouts: 25.8 us -> 32.5 us
    all_gather x1 -> x0, waiting for transfers between devices: 113 us -> none  [shards(): portion = lax.all_gather(fine_source, 'row', axis=0, tiled=True)]
    all_to_all x1 -> x0, blocking collectives: 111 us -> none  [shards(): lax.all_to_all(flattened, 'row', split_axis=1, concat_axis=0, tiled=True)]
    ppermute x1 -> x32, starting transfers between devices: 1.47 us -> 63.6 us  [the longest x31 62.2 us: trade(): lax.ppermute(block, 'row', [(i, i ^ k) for i in range(devices)])]
    ppermute x1 -> x32, waiting for transfers between devices: 1.6 us -> 63.7 us  [the longest x31 63.7 us: trade(): lax.ppermute(block, 'row', [(i, i ^ k) for i in range(devices)])]
    pallas_call x0 -> x26, Pallas kernels: none -> 62.1 us  [the longest x12 22.8 us: combine(): pl.pallas_call(combine_kernel, grid_spec=pltpu.PrefetchScalarGridSpec(num...]
    dot_general x4 -> x1, matrix products: 34.6 us -> 1.74 us  [ring_shards(): jnp.dot(selector, portion, preferred_element_type=jnp.float32)]
    unnamed x17 -> x56, local copies, waits for them, and re-layouts: 0.06 us -> 18.4 us
    convert_element_type x1 -> x0, local copies, waits for them, and re-layouts: 15.8 us -> none  [shards(): along_y.astype(jnp.float32)]
  transfers between devices with their start and end apart: 3 -> 32, of which waited for: 2 -> 6; matrix products, arithmetic and copies ran while one was open for 5% -> 12% of each run, Pallas kernels for 0% -> 24%
where the time goes in v2:
time: 237 us; the launch traced here: 236 us
  waiting for transfers between devices  63.7 us (27%)
  starting transfers between devices  63.6 us (27%)
  Pallas kernels  62.1 us (26%)
  local copies, waits for them, and re-layouts  32.5 us (14%)
  other arithmetic  11 us (5%)
    ppermute x31, waiting for transfers between devices, trade(): lax.ppermute(block, 'row', [(i, i ^ k) for i in range(devices)])  63.7 us
    ppermute x31, starting transfers between devices, trade(): lax.ppermute(block, 'row', [(i, i ^ k) for i in range(devices)])  62.2 us
    pallas_call x12, Pallas kernels, combine(): pl.pallas_call(combine_kernel, grid_spec=pltpu.PrefetchScalarGridSpec(num...  22.8 us
    pallas_call x8, Pallas kernels, pack(): pl.pallas_call(pack_kernel, grid_spec=pltpu.PrefetchScalarGridSpec(num_sc...  21.9 us
    unnamed x56, local copies, waits for them, and re-layouts  18.4 us
    pallas_call x3, Pallas kernels, bases(): pl.pallas_call(base_kernel, grid=(rows // part,), in_specs=[pl.BlockSpec(...  10.4 us
    pallas_call x2, Pallas kernels, slopes(): pl.pallas_call(functools.partial(slope_kernel, planes), in_specs=[pl.Bloc...  6.91 us
    ppermute x3, local copies, waits for them, and re-layouts, trade(): lax.ppermute(block, 'row', [(i, i ^ k) for i in range(devices)])  5.07 us
  transfers between devices with their start and end apart: 32, of which 6 were waited for; matrix products, arithmetic and copies ran while one was open for 12% of the time, Pallas kernels for 24%

profile of v2, /device:TPU:0, one launch (start us, length us, event | category | flops | bytes accessed | tf_op | source)
XLA Modules:
  0.0 235.7 jit_solution(6204783119942431978)
XLA Ops:
  1.3 3.0 %pack.13 = (bf16[16,32,384]{2,1,0:T(8,128)(2,1)}, bf16[16,32,384]{2,1,0:T(8,128)(2,1)}) custom-call(s32[5]{0:T(128)} %pad_add_fusion.xi_ref, bf16[64,3,8,1536]{3,2,1,0:T(8,128)(2,1)} %bitcast.33), custom_call_target="tpu_custom_call" | custom-call | flops 1 | bytes 1 | tf_op jit(solution)/shard_map/pack/pallas_call | solution.py:80
  4.3 3.0 %collective-permute-start.12 = (bf16[16,32,384]{2,1,0:T(8,128)(2,1)}, bf16[16,32,384]{2,1,0:T(8,128)(2,1)S(1)}, u32[]{:S(2)}, u32[]{:S(2)}) collective-permute-start(bf16[16,32,384]{2,1,0:T(8,128)(2,1)} %get-tuple-element.102), channel_id=1, source_target_pairs={{0,2},{1,3},{2,0},{3,1},{4,6},{5,7},{6,4},{7,5},{8,10},{9,11},{10,... | collective-permute-start | bytes 1179656 | tf_op jit(solution)/shard_map/ppermute | solution.py:250
  7.3 2.9 %pack.8 = (bf16[16,32,384]{2,1,0:T(8,128)(2,1)}, bf16[16,32,384]{2,1,0:T(8,128)(2,1)}) custom-call(s32[5]{0:T(128)} %pad_add_fusion.xi_ref, bf16[64,3,8,1536]{3,2,1,0:T(8,128)(2,1)} %bitcast.34), custom_call_target="tpu_custom_call" | custom-call | flops 1 | bytes 1 | tf_op jit(solution)/shard_map/pack/pallas_call | solution.py:80
  10.2 2.6 %collective-permute-start.3 = (bf16[16,32,384]{2,1,0:T(8,128)(2,1)}, bf16[16,32,384]{2,1,0:T(8,128)(2,1)S(1)}, u32[]{:S(2)}, u32[]{:S(2)}) collective-permute-start(bf16[16,32,384]{2,1,0:T(8,128)(2,1)} %get-tuple-element.88), channel_id=1, source_target_pairs={{0,4},{1,5},{2,6},{3,7},{4,0},{5,1},{6,2},{7,3},{8,12},{9,13},{10,... | collective-permute-start | bytes 1179656 | tf_op jit(solution)/shard_map/ppermute | solution.py:250
  13.2 3.5 %collective-permute-start.1 = (bf16[16,32,384]{2,1,0:T(8,128)(2,1)}, bf16[16,32,384]{2,1,0:T(8,128)(2,1)S(1)}, u32[]{:S(2)}, u32[]{:S(2)}) collective-permute-start(bf16[16,32,384]{2,1,0:T(8,128)(2,1)} %get-tuple-element.84), channel_id=1, source_target_pairs={{0,5},{1,4},{2,7},{3,6},{4,1},{5,0},{6,3},{7,2},{8,13},{9,12},{10,... | collective-permute-start | bytes 1179656 | tf_op jit(solution)/shard_map/ppermute | solution.py:250
  16.7 2.9 %pack.10 = (bf16[16,32,384]{2,1,0:T(8,128)(2,1)}, bf16[16,32,384]{2,1,0:T(8,128)(2,1)}) custom-call(s32[5]{0:T(128)} %pad_add_fusion.xi_ref, bf16[64,3,8,1536]{3,2,1,0:T(8,128)(2,1)} %bitcast.35), custom_call_target="tpu_custom_call" | custom-call | flops 1 | bytes 1 | tf_op jit(solution)/shard_map/pack/pallas_call | solution.py:80
  22.5 28.2 %collective-permute-done.3.refs_1_ = bf16[16,32,384]{2,1,0:T(8,128)(2,1)S(1)} collective-permute-done((bf16[16,32,384]{2,1,0:T(8,128)(2,1)}, bf16[16,32,384]{2,1,0:T(8,128)(2,1)S(1)}, u32[]{:S(2)}, u32[]{:S(2)}) %collective-permute-start.3) | collective-permute-done | bytes 393248 | tf_op jit(solution)/shard_map/ppermute | solution.py:250
  50.7 3.4 %collective-permute-start.4 = (bf16[16,32,384]{2,1,0:T(8,128)(2,1)}, bf16[16,32,384]{2,1,0:T(8,128)(2,1)S(1)}, u32[]{:S(2)}, u32[]{:S(2)}) collective-permute-start(bf16[16,32,384]{2,1,0:T(8,128)(2,1)} %get-tuple-element.89), channel_id=1, source_target_pairs={{0,7},{1,6},{2,5},{3,4},{4,3},{5,2},{6,1},{7,0},{8,15},{9,14},{10,... | collective-permute-start | bytes 1179656 | tf_op jit(solution)/shard_map/ppermute | solution.py:250
  55.1 2.9 %pack.15 = (bf16[16,32,384]{2,1,0:T(8,128)(2,1)}, bf16[16,32,384]{2,1,0:T(8,128)(2,1)}) custom-call(s32[5]{0:T(128)} %pad_add_fusion.xi_ref, bf16[64,3,8,1536]{3,2,1,0:T(8,128)(2,1)} %bitcast.36), custom_call_target="tpu_custom_call" | custom-call | flops 1 | bytes 1 | tf_op jit(solution)/shard_map/pack/pallas_call | solution.py:80
  58.7 5.1 %collective-permute-start.13 = (bf16[16,32,384]{2,1,0:T(8,128)(2,1)}, bf16[16,32,384]{2,1,0:T(8,128)(2,1)}, u32[]{:S(2)}, u32[]{:S(2)}) collective-permute-start(bf16[16,32,384]{2,1,0:T(8,128)(2,1)} %get-tuple-element.103), channel_id=1, source_target_pairs={{0,1},{1,0},{2,3},{3,2},{4,5},{5,4},{6,7},{7,6},{8,9},{9,8},{10,11... | collective-permute-start | bytes 1179656 | tf_op jit(solution)/shard_map/ppermute | solution.py:250
  63.8 6.9 %collective-permute-done.1.refs_3_ = bf16[16,32,384]{2,1,0:T(8,128)(2,1)S(1)} collective-permute-done((bf16[16,32,384]{2,1,0:T(8,128)(2,1)}, bf16[16,32,384]{2,1,0:T(8,128)(2,1)S(1)}, u32[]{:S(2)}, u32[]{:S(2)}) %collective-permute-start.1) | collective-permute-done | bytes 393248 | tf_op jit(solution)/shard_map/ppermute | solution.py:250
  75.9 2.7 %pack.12 = (bf16[8,32,384]{2,1,0:T(8,128)(2,1)}, bf16[8,32,384]{2,1,0:T(8,128)(2,1)}) custom-call(s32[5]{0:T(128)} %pad_add_fusion.xi_ref, bf16[64,3,8,1536]{3,2,1,0:T(8,128)(2,1)} %bitcast.39), custom_call_target="tpu_custom_call" | custom-call | flops 1 | bytes 1 | tf_op jit(solution)/shard_map/pack/pallas_call | solution.py:80
  83.0 4.7 %collective-permute-start.5 = (bf16[8,32,384]{2,1,0:T(8,128)(2,1)}, bf16[8,32,384]{2,1,0:T(8,128)(2,1)S(1)}, u32[]{:S(2)}, u32[]{:S(2)}) collective-permute-start(bf16[8,32,384]{2,1,0:T(8,128)(2,1)} %get-tuple-element.90), channel_id=1, source_target_pairs={{0,5},{1,4},{2,7},{3,6},{4,1},{5,0},{6,3},{7,2},{8,13},{9,12},{10,... | collective-permute-start | bytes 589832 | tf_op jit(solution)/shard_map/ppermute | solution.py:250
  92.2 9.9 %collective-permute-done.5.refs_3_ = bf16[8,32,384]{2,1,0:T(8,128)(2,1)S(1)} collective-permute-done((bf16[8,32,384]{2,1,0:T(8,128)(2,1)}, bf16[8,32,384]{2,1,0:T(8,128)(2,1)S(1)}, u32[]{:S(2)}, u32[]{:S(2)}) %collective-permute-start.5) | collective-permute-done | bytes 196640 | tf_op jit(solution)/shard_map/ppermute | solution.py:250
  117.4 4.4 %slopes.3 = (bf16[16,32,384]{2,1,0:T(8,128)(2,1)S(1)}, bf16[16,32,384]{2,1,0:T(8,128)(2,1)}, bf16[16,32,384]{2,1,0:T(8,128)(2,1)}, bf16[16,32,384]{2,1,0:T(8,128...) custom-call(bf16[512,512]{1,0:T(8,128)(2,1)S(1)} %dynamic-slice_dyna, ...), custom_call_target="tpu_custom_call" | custom-call | flops 1 | bytes 1 | tf_op jit(solution)/shard_map/slopes/pallas_call | solution.py:122
  126.3 3.0 %collective-permute-start.22 = (bf16[16,32,384]{2,1,0:T(8,128)(2,1)}, bf16[16,32,384]{2,1,0:T(8,128)(2,1)S(1)}, u32[]{:S(2)}, u32[]{:S(2)}) collective-permute-start(bf16[16,32,384]{2,1,0:T(8,128)(2,1)} %get-tuple-element.125), channel_id=1, source_target_pairs={{0,4},{1,5},{2,6},{3,7},{4,0},{5,1},{6,2},{7,3},{8,12},{9,13},{10,... | collective-permute-start | bytes 1179656 | tf_op jit(solution)/shard_map/ppermute | solution.py:250
  149.1 9.9 %collective-permute-done.24.far_ref = bf16[16,32,384]{2,1,0:T(8,128)(2,1)S(1)} collective-permute-done((bf16[16,32,384]{2,1,0:T(8,128)(2,1)}, bf16[16,32,384]{2,1,0:T(8,128)(2,1)S(1)}, u32[]{:S(2)}, u32[]{:S(2)}) %collective-permute-start.24) | collective-permute-done | bytes 393248 | tf_op jit(solution)/shard_map/ppermute | solution.py:250
  159.0 12.1 %collective-permute-start.25 = (bf16[8,32,384]{2,1,0:T(8,128)(2,1)S(1)}, bf16[8,32,384]{2,1,0:T(8,128)(2,1)S(1)}, u32[]{:S(2)}, u32[]{:S(2)}) collective-permute-start(bf16[8,32,384]{2,1,0:T(8,128)(2,1)S(1)} %get-tuple-element.146), channel_id=1, source_target_pairs={{0,2},{1,3},{2,0},{3,1},{4,6},{5,7},{6,4},{7,5},{8,10},{9,11},{10,... | collective-permute-start | bytes 589832 | tf_op jit(solution)/shard_map/ppermute | solution.py:250
  171.1 8.0 %collective-permute-done.22.near_ref = bf16[16,32,384]{2,1,0:T(8,128)(2,1)S(1)} collective-permute-done((bf16[16,32,384]{2,1,0:T(8,128)(2,1)}, bf16[16,32,384]{2,1,0:T(8,128)(2,1)S(1)}, u32[]{:S(2)}, u32[]{:S(2)}) %collective-permute-start.22) | collective-permute-done | bytes 393248 | tf_op jit(solution)/shard_map/ppermute | solution.py:250
  189.5 3.5 %bases.5.base_ref = f32[64,8,1536]{2,1,0:T(8,128)S(1)} custom-call(bf16[64,3,8,1536]{3,2,1,0:T(8,128)(2,1)S(1)} %bitcast.41, bf16[64,3,8,1536]{3,2,1,0:T(8,128)(2,1)S(1)} %bitcast.42, bf16[1536,1536]{1,0:T(8,128)(2,1)S(1)} %copy-done.3, f32[1,1536]{1,0:T(1,128)S(1)} %broadcast_in_dim.38.m_ref, bf16[3,64,8,192]{3,2,1,0:T(8,128)(2,1)S(1)} %bitcast.73, ...), custom_call_target="tpu_custom_call" | custom-call | flops 1 | bytes 1 | tf_op jit(solution)/shard_map/bases/pallas_call | solution.py:164
  192.9 3.5 %bases.4.base_ref = f32[64,8,1536]{2,1,0:T(8,128)S(1)} custom-call(bf16[64,3,8,1536]{3,2,1,0:T(8,128)(2,1)S(1)} %bitcast.43, bf16[64,3,8,1536]{3,2,1,0:T(8,128)(2,1)S(1)} %bitcast.44, bf16[1536,1536]{1,0:T(8,128)(2,1)S(1)} %copy-done.3, f32[1,1536]{1,0:T(1,128)S(1)} %broadcast_in_dim.38.m_ref, bf16[3,64,8,192]{3,2,1,0:T(8,128)(2,1)S(1)} %bitcast.74, ...), custom_call_target="tpu_custom_call" | custom-call | flops 1 | bytes 1 | tf_op jit(solution)/shard_map/bases/pallas_call | solution.py:164
  196.4 3.5 %bases.3.refs_2_.base_ref = f32[64,8,1536]{2,1,0:T(8,128)S(1)} custom-call(bf16[64,3,8,1536]{3,2,1,0:T(8,128)(2,1)S(1)} %bitcast.45, bf16[64,3,8,1536]{3,2,1,0:T(8,128)(2,1)S(1)} %bitcast.46, bf16[1536,1536]{1,0:T(8,128)(2,1)S(1)} %copy-done.3, f32[1,1536]{1,0:T(1,128)S(1)} %broadcast_in_dim.38.m_ref, bf16[3,64,8,192]{3,2,1,0:T(8,128)(2,1)S(1)} %bitcast.75, ...), custom_call_target="tpu_custom_call" | custom-call | flops 1 | bytes 1 | tf_op jit(solution)/shard_map/bases/pallas_call | solution.py:164
  199.9 2.8 %collective-permute-start.30 = (bf16[8,32,384]{2,1,0:T(8,128)(2,1)S(1)}, bf16[8,32,384]{2,1,0:T(8,128)(2,1)S(1)}, u32[]{:S(2)}, u32[]{:S(2)}) collective-permute-start(bf16[8,32,384]{2,1,0:T(8,128)(2,1)S(1)} %get-tuple-element.155), channel_id=1, source_target_pairs={{0,7},{1,6},{2,5},{3,4},{4,3},{5,2},{6,1},{7,0},{8,15},{9,14},{10,... | collective-permute-start | bytes 589832 | tf_op jit(solution)/shard_map/ppermute | solution.py:250
  206.7 3.2 %collective-permute-start.28 = (bf16[8,32,384]{2,1,0:T(8,128)(2,1)S(1)}, bf16[8,32,384]{2,1,0:T(8,128)(2,1)S(1)}, u32[]{:S(2)}, u32[]{:S(2)}) collective-permute-start(bf16[8,32,384]{2,1,0:T(8,128)(2,1)S(1)} %get-tuple-element.151), channel_id=1, source_target_pairs={{0,6},{1,7},{2,4},{3,5},{4,2},{5,3},{6,0},{7,1},{8,14},{9,15},{10,... | collective-permute-start | bytes 589832 | tf_op jit(solution)/shard_map/ppermute | solution.py:250
  (153 shorter events, 99.2 us)
Async XLA Ops:
  4.3 54.4 %collective-permute-start.12 = (bf16[16,32,384]{2,1,0:T(8,128)(2,1)}, bf16[16,32,384]{2,1,0:T(8,128)(2,1)S(1)}, u32[]{:S(2)}, u32[]{:S(2)}) collective-permute-start(bf16[16,32,384]{2,1,0:T(8,128)(2,1)} %get-tuple-element.102), channel_id=1, source_target_pairs={{0,2},{1,3},{2,0},{3,1},{4,6},{5,7},{6,4},{7,5},{8,10},{9,11},{10,... | collective-permute-start | bytes 1179656 | tf_op jit(solution)/shard_map/ppermute | solution.py:250
  10.2 40.5 %collective-permute-start.3 = (bf16[16,32,384]{2,1,0:T(8,128)(2,1)}, bf16[16,32,384]{2,1,0:T(8,128)(2,1)S(1)}, u32[]{:S(2)}, u32[]{:S(2)}) collective-permute-start(bf16[16,32,384]{2,1,0:T(8,128)(2,1)} %get-tuple-element.88), channel_id=1, source_target_pairs={{0,4},{1,5},{2,6},{3,7},{4,0},{5,1},{6,2},{7,3},{8,12},{9,13},{10,... | collective-permute-start | bytes 1179656 | tf_op jit(solution)/shard_map/ppermute | solution.py:250
  12.8 41.4 %collective-permute-start = (bf16[16,3,4,192]{3,0,2,1:T(8,128)(2,1)S(1)}, bf16[16,3,4,192]{3,0,2,1:T(8,128)(2,1)S(1)}, u32[]{:S(2)}, u32[]{:S(2)}) collective-permute-start(bf16[16,3,4,192]{3,0,2,1:T(8,128)(2,1)S(1)} %bitcast.79), channel_id=1, source_target_pairs={{0,4},{1,5},{2,6},{3,7},{4,0},{5,1},{6,2},{7,3},{8,12},{9,13},{10,... | collective-permute-start | bytes 221192 | tf_op jit(solution)/shard_map/ppermute | solution.py:250
  13.2 57.5 %collective-permute-start.1 = (bf16[16,32,384]{2,1,0:T(8,128)(2,1)}, bf16[16,32,384]{2,1,0:T(8,128)(2,1)S(1)}, u32[]{:S(2)}, u32[]{:S(2)}) collective-permute-start(bf16[16,32,384]{2,1,0:T(8,128)(2,1)} %get-tuple-element.84), channel_id=1, source_target_pairs={{0,5},{1,4},{2,7},{3,6},{4,1},{5,0},{6,3},{7,2},{8,13},{9,12},{10,... | collective-permute-start | bytes 1179656 | tf_op jit(solution)/shard_map/ppermute | solution.py:250
  19.6 68.9 %collective-permute-start.8 = (bf16[16,32,384]{2,1,0:T(8,128)(2,1)}, bf16[16,32,384]{2,1,0:T(8,128)(2,1)S(1)}, u32[]{:S(2)}, u32[]{:S(2)}) collective-permute-start(bf16[16,32,384]{2,1,0:T(8,128)(2,1)} %get-tuple-element.94), channel_id=1, source_target_pairs={{0,6},{1,7},{2,4},{3,5},{4,2},{5,3},{6,0},{7,1},{8,14},{9,15},{10,... | collective-permute-start | bytes 1179656 | tf_op jit(solution)/shard_map/ppermute | solution.py:250
  50.7 32.3 %collective-permute-start.4 = (bf16[16,32,384]{2,1,0:T(8,128)(2,1)}, bf16[16,32,384]{2,1,0:T(8,128)(2,1)S(1)}, u32[]{:S(2)}, u32[]{:S(2)}) collective-permute-start(bf16[16,32,384]{2,1,0:T(8,128)(2,1)} %get-tuple-element.89), channel_id=1, source_target_pairs={{0,7},{1,6},{2,5},{3,4},{4,3},{5,2},{6,1},{7,0},{8,15},{9,14},{10,... | collective-permute-start | bytes 1179656 | tf_op jit(solution)/shard_map/ppermute | solution.py:250
  54.2 34.4 %collective-permute-start.10 = (bf16[16,32,384]{2,1,0:T(8,128)(2,1)}, bf16[16,32,384]{2,1,0:T(8,128)(2,1)S(1)}, u32[]{:S(2)}, u32[]{:S(2)}) collective-permute-start(bf16[16,32,384]{2,1,0:T(8,128)(2,1)} %get-tuple-element.98), channel_id=1, source_target_pairs={{0,3},{1,2},{2,1},{3,0},{4,7},{5,6},{6,5},{7,4},{8,11},{9,10},{10,... | collective-permute-start | bytes 1179656 | tf_op jit(solution)/shard_map/ppermute | solution.py:250
  58.7 49.9 %collective-permute-start.13 = (bf16[16,32,384]{2,1,0:T(8,128)(2,1)}, bf16[16,32,384]{2,1,0:T(8,128)(2,1)}, u32[]{:S(2)}, u32[]{:S(2)}) collective-permute-start(bf16[16,32,384]{2,1,0:T(8,128)(2,1)} %get-tuple-element.103), channel_id=1, source_target_pairs={{0,1},{1,0},{2,3},{3,2},{4,5},{5,4},{6,7},{7,6},{8,9},{9,8},{10,11... | collective-permute-start | bytes 1179656 | tf_op jit(solution)/shard_map/ppermute | solution.py:250
  70.7 19.7 %collective-permute-start.2 = (bf16[32,3,4,192]{3,0,2,1:T(8,128)(2,1)}, bf16[32,3,4,192]{3,0,2,1:T(8,128)(2,1)}, u32[]{:S(2)}, u32[]{:S(2)}) collective-permute-start(bf16[32,3,4,192]{3,0,2,1:T(8,128)(2,1)} %pad_maximum_fusion.4), channel_id=1, source_target_pairs={{0,2},{1,3},{2,0},{3,1},{4,6},{5,7},{6,4},{7,5},{8,10},{9,11},{10,... | collective-permute-start | bytes 442376 | tf_op jit(solution)/shard_map/ppermute | solution.py:250
  102.1 27.2 %collective-permute-start.6 = (bf16[64,3,4,192]{3,0,2,1:T(8,128)(2,1)}, bf16[64,3,4,192]{3,0,2,1:T(8,128)(2,1)}, u32[]{:S(2)}, u32[]{:S(2)}) collective-permute-start(bf16[64,3,4,192]{3,0,2,1:T(8,128)(2,1)} %pad_maximum_fusion.3), channel_id=1, source_target_pairs={{0,1},{1,0},{2,3},{3,2},{4,5},{5,4},{6,7},{7,6},{8,9},{9,8},{10,11... | collective-permute-start | bytes 884744 | tf_op jit(solution)/shard_map/ppermute | solution.py:250
  121.8 37.2 %collective-permute-start.24 = (bf16[16,32,384]{2,1,0:T(8,128)(2,1)}, bf16[16,32,384]{2,1,0:T(8,128)(2,1)S(1)}, u32[]{:S(2)}, u32[]{:S(2)}) collective-permute-start(bf16[16,32,384]{2,1,0:T(8,128)(2,1)} %get-tuple-element.128), channel_id=1, source_target_pairs={{0,5},{1,4},{2,7},{3,6},{4,1},{5,0},{6,3},{7,2},{8,13},{9,12},{10,... | collective-permute-start | bytes 1179656 | tf_op jit(solution)/shard_map/ppermute | solution.py:250
  122.9 24.6 %collective-permute-start.18 = (bf16[16,32,384]{2,1,0:T(8,128)(2,1)}, bf16[16,32,384]{2,1,0:T(8,128)(2,1)S(1)}, u32[]{:S(2)}, u32[]{:S(2)}) collective-permute-start(bf16[16,32,384]{2,1,0:T(8,128)(2,1)} %get-tuple-element.117), channel_id=1, source_target_pairs={{0,2},{1,3},{2,0},{3,1},{4,6},{5,7},{6,4},{7,5},{8,10},{9,11},{10,... | collective-permute-start | bytes 1179656 | tf_op jit(solution)/shard_map/ppermute | solution.py:250
  124.0 35.0 %collective-permute-start.21 = (bf16[16,32,384]{2,1,0:T(8,128)(2,1)}, bf16[16,32,384]{2,1,0:T(8,128)(2,1)S(1)}, u32[]{:S(2)}, u32[]{:S(2)}) collective-permute-start(bf16[16,32,384]{2,1,0:T(8,128)(2,1)} %get-tuple-element.122), channel_id=1, source_target_pairs={{0,6},{1,7},{2,4},{3,5},{4,2},{5,3},{6,0},{7,1},{8,14},{9,15},{10,... | collective-permute-start | bytes 1179656 | tf_op jit(solution)/shard_map/ppermute | solution.py:250
  126.3 52.7 %collective-permute-start.22 = (bf16[16,32,384]{2,1,0:T(8,128)(2,1)}, bf16[16,32,384]{2,1,0:T(8,128)(2,1)S(1)}, u32[]{:S(2)}, u32[]{:S(2)}) collective-permute-start(bf16[16,32,384]{2,1,0:T(8,128)(2,1)} %get-tuple-element.125), channel_id=1, source_target_pairs={{0,4},{1,5},{2,6},{3,7},{4,0},{5,1},{6,2},{7,3},{8,12},{9,13},{10,... | collective-permute-start | bytes 1179656 | tf_op jit(solution)/shard_map/ppermute | solution.py:250
  139.2 39.9 %collective-permute-start.7 = (bf16[64,1,3,192]{3,0,2,1:T(8,128)(2,1)}, bf16[64,1,3,192]{3,0,2,1:T(8,128)(2,1)}, u32[]{:S(2)}, u32[]{:S(2)}) collective-permute-start(bf16[64,1,3,192]{3,0,2,1:T(8,128)(2,1)} %slice.13), channel_id=1, source_target_pairs={{8,0},{16,8},{24,16},{9,1},{17,9},{25,17},{10,2},{18,10},{26,18},{... | collective-permute-start | bytes 221192 | tf_op jit(solution)/shard_map/ppermute | solution.py:52
  147.6 57.1 %collective-permute-start.19 = (bf16[16,32,384]{2,1,0:T(8,128)(2,1)}, bf16[16,32,384]{2,1,0:T(8,128)(2,1)S(1)}, u32[]{:S(2)}, u32[]{:S(2)}) collective-permute-start(bf16[16,32,384]{2,1,0:T(8,128)(2,1)} %copy-done.17), channel_id=1, source_target_pairs={{0,1},{1,0},{2,3},{3,2},{4,5},{5,4},{6,7},{7,6},{8,9},{9,8},{10,11... | collective-permute-start | bytes 1179656 | tf_op jit(solution)/shard_map/ppermute | solution.py:250
  159.0 40.9 %collective-permute-start.29 = (bf16[8,32,384]{2,1,0:T(8,128)(2,1)S(1)}, bf16[8,32,384]{2,1,0:T(8,128)(2,1)S(1)}, u32[]{:S(2)}, u32[]{:S(2)}) collective-permute-start(bf16[8,32,384]{2,1,0:T(8,128)(2,1)S(1)} %get-tuple-element.154), channel_id=1, source_target_pairs={{0,4},{1,5},{2,6},{3,7},{4,0},{5,1},{6,2},{7,3},{8,12},{9,13},{10,... | collective-permute-start | bytes 589832 | tf_op jit(solution)/shard_map/ppermute | solution.py:250
  159.0 68.9 %collective-permute-start.25 = (bf16[8,32,384]{2,1,0:T(8,128)(2,1)S(1)}, bf16[8,32,384]{2,1,0:T(8,128)(2,1)S(1)}, u32[]{:S(2)}, u32[]{:S(2)}) collective-permute-start(bf16[8,32,384]{2,1,0:T(8,128)(2,1)S(1)} %get-tuple-element.146), channel_id=1, source_target_pairs={{0,2},{1,3},{2,0},{3,1},{4,6},{5,7},{6,4},{7,5},{8,10},{9,11},{10,... | collective-permute-start | bytes 589832 | tf_op jit(solution)/shard_map/ppermute | solution.py:250
  179.1 26.7 %collective-permute-start.20 = (bf16[16,32,384]{2,1,0:T(8,128)(2,1)}, bf16[16,32,384]{2,1,0:T(8,128)(2,1)S(1)}, u32[]{:S(2)}, u32[]{:S(2)}) collective-permute-start(bf16[16,32,384]{2,1,0:T(8,128)(2,1)} %copy-done.16), channel_id=1, source_target_pairs={{0,3},{1,2},{2,1},{3,0},{4,7},{5,6},{6,5},{7,4},{8,11},{9,10},{10,... | collective-permute-start | bytes 1179656 | tf_op jit(solution)/shard_map/ppermute | solution.py:250
  179.1 27.6 %collective-permute-start.23 = (bf16[16,32,384]{2,1,0:T(8,128)(2,1)}, bf16[16,32,384]{2,1,0:T(8,128)(2,1)S(1)}, u32[]{:S(2)}, u32[]{:S(2)}) collective-permute-start(bf16[16,32,384]{2,1,0:T(8,128)(2,1)} %copy-done.15), channel_id=1, source_target_pairs={{0,7},{1,6},{2,5},{3,4},{4,3},{5,2},{6,1},{7,0},{8,15},{9,14},{10,... | collective-permute-start | bytes 1179656 | tf_op jit(solution)/shard_map/ppermute | solution.py:250
  199.9 30.1 %collective-permute-start.30 = (bf16[8,32,384]{2,1,0:T(8,128)(2,1)S(1)}, bf16[8,32,384]{2,1,0:T(8,128)(2,1)S(1)}, u32[]{:S(2)}, u32[]{:S(2)}) collective-permute-start(bf16[8,32,384]{2,1,0:T(8,128)(2,1)S(1)} %get-tuple-element.155), channel_id=1, source_target_pairs={{0,7},{1,6},{2,5},{3,4},{4,3},{5,2},{6,1},{7,0},{8,15},{9,14},{10,... | collective-permute-start | bytes 589832 | tf_op jit(solution)/shard_map/ppermute | solution.py:250
  204.6 27.2 %collective-permute-start.27 = (bf16[8,32,384]{2,1,0:T(8,128)(2,1)S(1)}, bf16[8,32,384]{2,1,0:T(8,128)(2,1)S(1)}, u32[]{:S(2)}, u32[]{:S(2)}) collective-permute-start(bf16[8,32,384]{2,1,0:T(8,128)(2,1)S(1)} %get-tuple-element.149), channel_id=1, source_target_pairs={{0,3},{1,2},{2,1},{3,0},{4,7},{5,6},{6,5},{7,4},{8,11},{9,10},{10,... | collective-permute-start | bytes 589832 | tf_op jit(solution)/shard_map/ppermute | solution.py:250
  205.8 22.3 %collective-permute-start.31 = (bf16[8,32,384]{2,1,0:T(8,128)(2,1)S(1)}, bf16[8,32,384]{2,1,0:T(8,128)(2,1)S(1)}, u32[]{:S(2)}, u32[]{:S(2)}) collective-permute-start(bf16[8,32,384]{2,1,0:T(8,128)(2,1)S(1)} %get-tuple-element.157), channel_id=1, source_target_pairs={{0,5},{1,4},{2,7},{3,6},{4,1},{5,0},{6,3},{7,2},{8,13},{9,12},{10,... | collective-permute-start | bytes 589832 | tf_op jit(solution)/shard_map/ppermute | solution.py:250
  206.7 23.2 %collective-permute-start.28 = (bf16[8,32,384]{2,1,0:T(8,128)(2,1)S(1)}, bf16[8,32,384]{2,1,0:T(8,128)(2,1)S(1)}, u32[]{:S(2)}, u32[]{:S(2)}) collective-permute-start(bf16[8,32,384]{2,1,0:T(8,128)(2,1)S(1)} %get-tuple-element.151), channel_id=1, source_target_pairs={{0,6},{1,7},{2,4},{3,5},{4,2},{5,3},{6,0},{7,1},{8,14},{9,15},{10,... | collective-permute-start | bytes 589832 | tf_op jit(solution)/shard_map/ppermute | solution.py:250
  (32 other events, 377.4 us)

commit v3 on v2

--- a/solution.py
+++ b/solution.py
@@ -56,7 +56,7 @@
 
 
 def pack_kernel(xi_ref, v_ref, *refs):
-    blocks, wide = refs[:-1], refs[-1]
+    blocks, wide = refs[-3:-1], refs[-1]
     rows, comps, levels, width = v_ref.shape
     half = levels // 2
     for c in range(comps):
@@ -70,7 +70,7 @@
                     block[c * half + l, :, lane] = level.astype(block.dtype)
 
 
-def pack(v, comps, s, prefetch):
+def pack(v, comps, s, prefetch, after):
     rows, _, levels, fine_width = v.shape
     zs = prefetch.shape[0] - 1
     width = fine_width // zs
@@ -87,7 +87,8 @@
                     (part, len(comps), levels, width),
                     lambda g, xi: (g, comps[0] // len(comps), 0, xi[1 + s]),
                 )
-            ],
+            ]
+            + [pl.BlockSpec(memory_space=pl.ANY)] * len(after),
             out_specs=[pl.BlockSpec((planes, part, width), lambda g, xi: (g, 0, 0))] * 2,
             scratch_shapes=[pltpu.VMEM((part * levels, lanes), jnp.float32)],
         ),
@@ -95,16 +96,21 @@
         compiler_params=pltpu.CompilerParams(vmem_limit_bytes=60 * mib),
         cost_estimate=light,
         name="pack",
-    )(prefetch, v)
-
-
-def slope_kernel(planes, d_ref, m_ref, *refs):
-    count = len(refs) // 2
-    sources, results = refs[:count], refs[count:]
+    )(prefetch, v, *after)
+
+
+def slope_kernel(planes, places, riders, d_ref, m_ref, *refs):
+    count = len(places)
+    sources, results = refs[:count], refs[-count:]
     part, width = sources[0].shape[1:]
     for q in range(planes):
         columns = jnp.concatenate(
-            [source[h * planes + q] for source in sources for h in range(2)], axis=0
+            [
+                source[h * stride + start + q]
+                for source, (stride, start) in zip(sources, places)
+                for h in range(2)
+            ],
+            axis=0,
         )
         slope = jnp.dot(d_ref[...], columns, preferred_element_type=jnp.float32) * m_ref[...]
         slope = slope.astype(jnp.bfloat16)
@@ -112,22 +118,26 @@
             for h in range(2):
                 at = (2 * k + h) * part
                 result[h * planes + q] = slope[at : at + part]
-
-
-def slopes(blocks, planes, deriv, metric):
+    for at in riders:
+        results[at][2 * planes :] = refs[count][...]
+
+
+def slopes(blocks, places, planes, deriv, metric, rider=None, riders=()):
     part, width = blocks[0].shape[1:]
     count = len(blocks)
-    result = jax.ShapeDtypeStruct((2 * planes, part, width), jnp.bfloat16)
-    area = deriv.shape[0] * planes * width
-    return pl.pallas_call(
-        functools.partial(slope_kernel, planes),
-        in_specs=[pl.BlockSpec(memory_space=pltpu.VMEM)] * (2 + count),
+    more = [rider] if riders else []
+    extra = [rider.shape[0] if at in riders else 0 for at in range(count)]
+    return pl.pallas_call(
+        functools.partial(slope_kernel, planes, places, riders),
+        in_specs=[pl.BlockSpec(memory_space=pltpu.VMEM)] * (2 + count + len(more)),
         out_specs=[pl.BlockSpec(memory_space=pltpu.VMEM)] * count,
-        out_shape=[result] * count,
-        compiler_params=pltpu.CompilerParams(vmem_limit_bytes=32 * mib),
+        out_shape=[
+            jax.ShapeDtypeStruct((2 * planes + e, part, width), jnp.bfloat16) for e in extra
+        ],
+        compiler_params=pltpu.CompilerParams(vmem_limit_bytes=60 * mib),
         cost_estimate=light,
         name="slopes",
-    )(deriv, metric, *blocks)
+    )(deriv, metric, *blocks, *more)
 
 
 def hold_kernel(block_ref, *refs):
@@ -145,6 +155,84 @@
         cost_estimate=light,
         name="hold",
     )(block, *after)
+
+
+def choose_kernel(pick_ref, spread_ref, rider_ref, *refs):
+    blocks, (levels_ref, rim_ref) = refs[:-2], refs[-2:]
+    planes, part, width = rider_ref.shape
+    rows = levels_ref.shape[1]
+    parts = [rider_ref[...]] + [block[block.shape[0] - planes :] for block in blocks]
+    source = jnp.concatenate(
+        [p.astype(jnp.float32).reshape(planes * part, width) for p in parts], axis=0
+    ).astype(jnp.bfloat16)
+    chosen = jnp.dot(pick_ref[...], source, preferred_element_type=jnp.float32)
+    chosen = chosen.astype(jnp.bfloat16)
+    count = spread_ref.shape[0]
+    pieces = pick_ref.shape[0] // rows
+    for u in range(pieces):
+        for h in range(count):
+            level = jnp.dot(
+                chosen[u * rows : (u + 1) * rows],
+                spread_ref[h],
+                preferred_element_type=jnp.float32,
+            ).astype(jnp.bfloat16)
+            levels_ref[u * count + h] = level
+            if h == 0 and u % (pieces // rim_ref.shape[0]) == 0:
+                rim_ref[u // (pieces // rim_ref.shape[0])] = level
+
+
+def choose(pick, spread, rider, blocks, components):
+    count, _, wide = spread.shape
+    rows = 2 * rider.shape[1]
+    pieces = pick.shape[0] // rows
+    whole = pl.BlockSpec(memory_space=pltpu.VMEM)
+    return pl.pallas_call(
+        choose_kernel,
+        in_specs=[whole] * (3 + len(blocks)),
+        out_specs=[whole] * 2,
+        out_shape=[
+            jax.ShapeDtypeStruct((pieces * count, rows, wide), jnp.bfloat16),
+            jax.ShapeDtypeStruct((components, rows, wide), jnp.bfloat16),
+        ],
+        compiler_params=pltpu.CompilerParams(vmem_limit_bytes=32 * mib),
+        cost_estimate=light,
+        name="choose",
+    )(pick, spread, rider, *blocks)
+
+
+def refine_kernel(top_ref, levels_ref, rim_ref, force_ref, wide):
+    components, rows, fine, width = force_ref.shape
+    coarse = fine // 2
+    for c in range(components):
+        level = [levels_ref[c * coarse + m].astype(jnp.float32) for m in range(coarse)]
+        above = rim_ref[c].astype(jnp.float32)
+        level.append(jnp.where(top_ref[0] == 1, level[-1], above))
+        for j in range(width // lanes):
+            lane = slice(j * lanes, (j + 1) * lanes)
+            for m in range(coarse):
+                low, high = level[m][:, lane], level[m + 1][:, lane]
+                wide[pl.ds(2 * m, rows, stride=fine), :] = low
+                middle = (0.5 * (low + high)).astype(jnp.bfloat16).astype(jnp.float32)
+                wide[pl.ds(2 * m + 1, rows, stride=fine), :] = middle
+            force_ref[c, :, :, lane] = (
+                wide[...].reshape(rows, fine, lanes).astype(jnp.bfloat16)
+            )
+
+
+def refine(levels, rim, is_topmost):
+    components, rows, width = rim.shape
+    fine = 2 * levels.shape[0] // components
+    whole = pl.BlockSpec(memory_space=pltpu.VMEM)
+    return pl.pallas_call(
+        refine_kernel,
+        in_specs=[pl.BlockSpec(memory_space=pltpu.SMEM), whole, whole],
+        out_specs=whole,
+        out_shape=jax.ShapeDtypeStruct((components, rows, fine, width), jnp.bfloat16),
+        scratch_shapes=[pltpu.VMEM((rows * fine, lanes), jnp.float32)],
+        compiler_params=pltpu.CompilerParams(vmem_limit_bytes=32 * mib),
+        cost_estimate=light,
+        name="refine",
+    )(is_topmost.astype(jnp.int32)[None], levels, rim)
 
 
 def base_kernel(v_ref, v0_ref, d_ref, m_ref, f_ref, t_ref, base_ref):
@@ -157,23 +245,24 @@
     base_ref[...] = (forcing - carry * along).reshape(rows, levels, width)
 
 
-def bases(v, component, deriv_x, metric_x, force, table):
+def bases(v, comps, deriv_x, metric_x, force, table):
     rows, _, levels, width = v.shape
     part = 32
     coarse_width = table.shape[0]
+    first = comps[0]
     return pl.pallas_call(
         base_kernel,
-        grid=(rows // part,),
+        grid=(rows // part, len(comps)),
         in_specs=[
-            pl.BlockSpec((part, None, levels, width), lambda g: (g, component, 0, 0)),
-            pl.BlockSpec((part, None, levels, width), lambda g: (g, 0, 0, 0)),
-            pl.BlockSpec(deriv_x.shape, lambda g: (0, 0)),
-            pl.BlockSpec(metric_x.shape, lambda g: (0, 0)),
-            pl.BlockSpec((None, part, levels, coarse_width), lambda g: (component, g, 0, 0)),
-            pl.BlockSpec(table.shape, lambda g: (0, 0)),
+            pl.BlockSpec((part, None, levels, width), lambda g, c: (g, first + c, 0, 0)),
+            pl.BlockSpec((part, None, levels, width), lambda g, c: (g, 0, 0, 0)),
+            pl.BlockSpec(deriv_x.shape, lambda g, c: (0, 0)),
+            pl.BlockSpec(metric_x.shape, lambda g, c: (0, 0)),
+            pl.BlockSpec((None, part, levels, coarse_width), lambda g, c: (first + c, g, 0, 0)),
+            pl.BlockSpec(table.shape, lambda g, c: (0, 0)),
         ],
-        out_specs=pl.BlockSpec((part, levels, width), lambda g: (g, 0, 0)),
-        out_shape=jax.ShapeDtypeStruct((rows, levels, width), jnp.float32),
+        out_specs=pl.BlockSpec((part, None, levels, width), lambda g, c: (g, c, 0, 0)),
+        out_shape=jax.ShapeDtypeStruct((rows, len(comps), levels, width), jnp.float32),
         compiler_params=pltpu.CompilerParams(vmem_limit_bytes=32 * mib),
         cost_estimate=light,
         name="bases",
@@ -181,7 +270,8 @@
 
 
 def combine_kernel(xi_ref, base_ref, v_ref, v1_ref, near_ref, far_ref, *refs):
-    t_ref, u_ref, along = refs[-3:]
+    t_ref, u_ref, mark_ref, along = refs[-4:]
+    mark_ref[...] = jnp.zeros(mark_ref.shape, mark_ref.dtype)
     rows, levels, width = base_ref.shape
     half = levels // 2
     for j in range(width // lanes):
@@ -198,37 +288,37 @@
         u_ref[:, :, lane] = moved.astype(jnp.bfloat16)
 
 
-def combine(v, component, at, s, prefetch, base, near, far, outs):
+def combine(v, comps, s, prefetch, base, near, far, outs, after):
     rows, _, levels, fine_width = v.shape
     part, width = near.shape[1:]
     half = levels // 2
-    per_half = near.shape[0] // 2 // half
-    column = lambda c: pl.BlockSpec(
-        (part, None, levels, width), lambda g, xi: (g, c, 0, xi[1 + s])
-    )
-    planes = pl.BlockSpec((half, part, width), lambda g, xi: (g * per_half + at, 0, 0))
+    first, count = comps[0], len(comps)
+    block = (part, None, levels, width)
+    column = pl.BlockSpec(block, lambda g, c, xi: (g, first + c, 0, xi[1 + s]))
+    planes = pl.BlockSpec((half, part, width), lambda g, c, xi: (g * count + c, 0, 0))
     return pl.pallas_call(
         combine_kernel,
         grid_spec=pltpu.PrefetchScalarGridSpec(
             num_scalar_prefetch=1,
-            grid=(rows // part,),
+            grid=(rows // part, count),
             in_specs=[
-                pl.BlockSpec((part, levels, width), lambda g, xi: (g, 0, xi[1 + s])),
-                column(component),
-                column(1),
+                pl.BlockSpec(block, lambda g, c, xi: (g, c, 0, xi[1 + s])),
+                column,
+                pl.BlockSpec(block, lambda g, c, xi: (g, 1, 0, xi[1 + s])),
                 planes,
                 planes,
             ]
-            + [pl.BlockSpec(memory_space=pl.ANY)] * len(outs),
-            out_specs=[column(component), column(component)],
+            + [pl.BlockSpec(memory_space=pl.ANY)] * len((*outs[:2], *after)),
+            out_specs=[column, column, pl.BlockSpec((8, lanes), lambda g, c, xi: (0, 0))],
             scratch_shapes=[pltpu.VMEM((part * levels, lanes), jnp.float32)],
         ),
-        out_shape=[jax.ShapeDtypeStruct(v.shape, v.dtype)] * 2,
+        out_shape=[jax.ShapeDtypeStruct(v.shape, v.dtype)] * 2
+        + [jax.ShapeDtypeStruct((8, lanes), jnp.float32)],
         input_output_aliases={6: 0, 7: 1} if outs else {},
         compiler_params=pltpu.CompilerParams(vmem_limit_bytes=16 * mib),
         cost_estimate=light,
         name="combine",
-    )(prefetch, base, v, v, near, far, *outs)
+    )(prefetch, base, v, v, near, far, *outs[:2], *after)
 
 
 def ring_shards(
@@ -237,73 +327,116 @@
     rows, levels, components, fine_width = velocity.shape
     devices = lax.axis_size("row")
     zs = devices // 2
+    width = fine_width // zs
     me = lax.axis_index("row").astype(jnp.int32)
     prefetch = jnp.concatenate([(me % 2)[None], (me // 2) ^ jnp.arange(zs, dtype=jnp.int32)])
     v = jnp.transpose(velocity, (0, 2, 1, 3))
-    arrival = [0, 4, 2, 5, 6, 3, 7, 1]
+    arrival = [0, 4, 5, 6, 7, 2, 3, 1]
     place = {k: at for at, k in enumerate(arrival)}
-    moved = []
+    moved, ready = [], []
 
     def trade(block, k):
+        if ready:
+            block, ready[-1] = lax.optimization_barrier((block, ready[-1]))
         if len(moved) >= in_flight:
             block, moved[-in_flight] = lax.optimization_barrier((block, moved[-in_flight]))
+        ready.append(block)
+        at = len(moved)
         moved.append(lax.ppermute(block, "row", [(i, i ^ k) for i in range(devices)]))
-        return moved[-1]
-
-    def exchange(blocks):
-        here = [blocks[0]]
-        for k, block in zip(arrival[1:], blocks[1:]):
-            here.append(trade(block, k))
-        return here
+        return at
 
     coarse_here, coarse_levels, _, coarse_width = coarse_force.shape
     row_size = coarse_levels * components * coarse_width
-    coarse = jnp.transpose(coarse_force, (0, 2, 1, 3))
-    portion = jnp.concatenate([coarse, trade(coarse, 4)], axis=0)
-
-    chunks = [(0, 1), (2,)]
-    arrived = []
-    for comps in chunks:
-        blocks = {}
-        for s in (2, 1, 3, 0):
-            blocks[2 * s], blocks[2 * s + 1] = pack(v, comps, s, prefetch)
-        arrived.append(exchange([blocks[k] for k in arrival]))
-        k = 2 if len(arrived) == 1 else 1
-        portion = jnp.concatenate([portion, trade(portion, k)], axis=0)
-
+    every = tuple(range(components))
+    chunks = one, two = [every[2:], every[:2]]
+    blocks, after = {}, ()
+    for which, s in ((one, 2), (every, 1), (one, 3), (every, 0), (two, 2), (two, 3)):
+        pair = pack(v, which, s, prefetch, after)
+        blocks[which, 2 * s], blocks[which, 2 * s + 1] = pair
+        after = pair[:1]
+    landed = {(every, 0): blocks[every, 0]}
+    rider = (
+        jnp.transpose(coarse_force, (0, 2, 1, 3))
+        .reshape(coarse_here, row_size)
+        .reshape(-1, rows // 2, width)
+    )
+    blocks[one, 4] = jnp.concatenate([blocks[one, 4], rider], axis=0)
+    steps = [
+        (one, 5), (one, 4), (one, 6), (every, 2), (one, 7), (every, 3), (two, 4), (every, 1),
+        (two, 5), (two, 6), (two, 7),
+    ]
     partners = [me ^ k for k in arrival]
     piece = lambda a, at, axis: lax.dynamic_slice_in_dim(a, at * rows, rows, axis)
     by_column = jnp.concatenate([piece(deriv_y, at, 1) for at in partners], axis=1)
     deriv = jnp.concatenate([piece(by_column, at, 0) for at in partners], axis=0)
     metric = jnp.concatenate([piece(metric_y, at, 0) for at in partners], axis=0)[:, None]
-
-    holders = jnp.stack([me ^ k for k in (0, 4, 2, 6, 1, 5, 3, 7)])
-    coarse_rows = (
-        holders[:, None] * coarse_here + jnp.arange(coarse_here, dtype=jnp.int32)
-    ).reshape(-1)
-    portion = portion.reshape(-1, row_size)
-    selector = (row_map[:, None] == coarse_rows[None, :]).astype(jnp.bfloat16)
-    chosen = jnp.dot(selector, portion, preferred_element_type=jnp.float32).astype(jnp.bfloat16)
-    chosen = chosen.reshape(rows, components, coarse_levels, coarse_width)
-    force = jnp.transpose(
-        extended_levels(jnp.transpose(chosen, (0, 2, 1, 3))), (2, 0, 1, 3)
-    )
-    table = upsample_table(x_index, x_weight, coarse_width)
-
-    base = [
-        bases(v, c, deriv_x, metric_x[None, :], force, table) for c in range(components)
-    ]
+    numbers = {}
+
+    for step in steps:
+        block = blocks[step]
+        if step == (every, 2):
+            block, deriv, metric = lax.optimization_barrier((block, deriv, metric))
+        numbers[step] = trade(block, step[1])
+    rider = jnp.concatenate([rider, moved[numbers[one, 4]][-rider.shape[0] :]], axis=0)
+
+    def derivatives(chunk, *carried):
+        names = [(every if k < 4 else chunk, k) for k in arrival]
+        blocks = [landed[n] if n in landed else moved[numbers[n]] for n in names]
+        half = levels // 2
+        places = [
+            (len(every) * half, chunk[0] * half) if k < 4 else (len(chunk) * half, 0)
+            for k in arrival
+        ]
+        return slopes(blocks, places, len(chunk) * half, deriv, metric, *carried)
+
+    sent = {0: derivatives(one, rider, [place[k] for k in (2, 3, 1)])}
+    sent[1] = derivatives(two)
+    back = {0: {0: sent[0][0]}, 1: {0: sent[1][0]}}
+    for at, k in ((0, 5), (0, 4), (0, 2), (0, 6), (0, 3), (0, 1), (0, 7), (1, 4), (1, 5)):
+        back[at][k] = trade(sent[at][place[k]], k)
+
+    holders = jnp.stack([me ^ k for k in (0, 4, 2, 6, 3, 7, 1, 5)])
+    pieces = row_size // width
+    held = coarse_here * pieces
+    names = (holders[:, None] * held + jnp.arange(held, dtype=jnp.int32)).reshape(-1)
+    wanted = row_map[None, :] * pieces + jnp.arange(pieces, dtype=jnp.int32)[:, None]
+    pick = (wanted.reshape(-1, 1) == names[None, :]).astype(jnp.bfloat16)
+    side = width // coarse_width
+    wide = -(-coarse_width // lanes) * lanes
+    column = jnp.arange(wide, dtype=jnp.int32)
+    source = jnp.arange(side, dtype=jnp.int32)[:, None] * coarse_width + column
+    source = jnp.where(column < coarse_width, source, -1)
+    spread = (
+        jnp.arange(width, dtype=jnp.int32)[None, :, None] == source[:, None, :]
+    ).astype(jnp.bfloat16)
+    carriers = [moved[back[0][k]] for k in (2, 3, 1)]
+    chosen, lowest = choose(pick, spread, rider, carriers, components)
+    slabs = lax.axis_size("slab")
+    rim = lax.ppermute(lowest, "slab", [(i + 1, i) for i in range(slabs - 1)])
+    force = refine(chosen, rim, lax.axis_index("slab") == slabs - 1)
+    table = upsample_table(x_index, x_weight, wide)
+    base = [bases(v, c, deriv_x, metric_x[None, :], force, table) for c in chunks]
+
+    def combined(at, s, outs, after=()):
+        near, far = (back[at][k] if k == 0 else moved[back[at][k]] for k in (2 * s, 2 * s + 1))
+        return combine(v, chunks[at], s, prefetch, base[at], near, far, outs, after)
+
+    for k in (2, 6):
+        back[1][k] = trade(sent[1][place[k]], k)
+    back[1][7] = trade(hold(sent[1][place[7]], base), 7)
     outs = ()
-    for comps, blocks in zip(chunks, arrived):
-        sent = list(slopes(blocks, len(comps) * levels // 2, deriv, metric))
-        if outs:
-            sent[-1] = hold(sent[-1], (*outs, base[comps[0]]))
-        along_y = exchange(sent)
-        for at, c in enumerate(comps):
-            for s in (2, 3, 1, 0):
-                near, far = along_y[place[2 * s]], along_y[place[2 * s + 1]]
-                outs = combine(v, c, at, s, prefetch, base[c], near, far, outs)
-    tendency, updated = (jnp.transpose(o, (0, 2, 1, 3)) for o in outs)
+    for s in (2, 1):
+        outs = combined(0, s, outs)
+    back[1][3] = trade(hold(sent[1][place[3]], outs[2:]), 3)
+    back[1][1] = trade(sent[1][place[1]], 1)
+    for s in (0, 3):
+        outs = combined(0, s, outs)
+    slabs = lax.axis_size("slab")
+    mark = lax.ppermute(outs[2], "slab", [(i, (i + 1) % slabs) for i in range(slabs)])
+    for s in (2, 1, 0):
+        outs = combined(1, s, outs)
+    outs = combined(1, 3, outs, (mark,))
+    tendency, updated = (jnp.transpose(o, (0, 2, 1, 3)) for o in outs[:2])
     return tendency, updated
 
 

time: 237 us -> 228 us (0.962)
  local copies, waits for them, and re-layouts: 32.5 us -> 10.9 us
  waiting for transfers between devices: 63.7 us -> 83.5 us
  other arithmetic: 11 us -> 3.78 us
    ppermute x31 -> x25, waiting for transfers between devices: 63.7 us -> 82 us  [trade(): lax.ppermute(block, 'row', [(i, i ^ k) for i in range(devices)])]
    unnamed x56 -> x65, local copies, waits for them, and re-layouts: 18.4 us -> 7.77 us
    pallas_call x5 -> x6, Pallas kernels: 17.3 us -> 23.4 us  [the longest x2 10.8 us: slopes(): pl.pallas_call(functools.partial(slope_kernel, planes, places, riders), i...]
    ppermute x3 -> x0, local copies, waits for them, and re-layouts: 5.07 us -> none  [trade(): lax.ppermute(block, 'row', [(i, i ^ k) for i in range(devices)])]
    pallas_call x8 -> x6, Pallas kernels: 21.9 us -> 17.6 us  [pack(): pl.pallas_call(pack_kernel, grid_spec=pltpu.PrefetchScalarGridSpec(num_sc...]
    pallas_call x12 -> x8, Pallas kernels: 22.8 us -> 20.1 us  [combine(): pl.pallas_call(combine_kernel, grid_spec=pltpu.PrefetchScalarGridSpec(num...]
    reshape x3 -> x0, local copies, waits for them, and re-layouts: 2.58 us -> none  [the longest x2 2.15 us: ring_shards(): chosen = chosen.reshape(rows, components, coarse_levels, coarse_width)]
    concatenate x3 -> x2, other arithmetic: 4.83 us -> 2.36 us  [the longest x1 1.68 us: ring_shards(): blocks[one, 4] = jnp.concatenate([blocks[one, 4], rider], axis=0)]
  transfers between devices with their start and end apart: 32 -> 27, of which waited for: 6 -> 11; matrix products, arithmetic and copies ran while one was open for 12% -> 3% of each run, Pallas kernels for 24% -> 25%
where the time goes in v3:
time: 228 us; the launch traced here: 225 us
  waiting for transfers between devices  83.5 us (37%)
  starting transfers between devices  64.3 us (28%)
  Pallas kernels  61.2 us (27%)
  local copies, waits for them, and re-layouts  10.9 us (5%)
  other arithmetic  3.78 us (2%)
    ppermute x25, waiting for transfers between devices, trade(): lax.ppermute(block, 'row', [(i, i ^ k) for i in range(devices)])  82 us
    ppermute x25, starting transfers between devices, trade(): lax.ppermute(block, 'row', [(i, i ^ k) for i in range(devices)])  62.9 us
    pallas_call x8, Pallas kernels, combine(): pl.pallas_call(combine_kernel, grid_spec=pltpu.PrefetchScalarGridSpec(num...  20.1 us
    pallas_call x6, Pallas kernels, pack(): pl.pallas_call(pack_kernel, grid_spec=pltpu.PrefetchScalarGridSpec(num_sc...  17.6 us
    pallas_call x2, Pallas kernels, slopes(): pl.pallas_call(functools.partial(slope_kernel, planes, places, riders), i...  10.8 us
    pallas_call x2, Pallas kernels, bases(): pl.pallas_call(base_kernel, grid=(rows // part, len(comps)), in_specs=[pl...  10.7 us
    unnamed x65, local copies, waits for them, and re-layouts  7.77 us
  transfers between devices with their start and end apart: 27, of which 11 were waited for; matrix products, arithmetic and copies ran while one was open for 3% of the time, Pallas kernels for 25%

profile of v3, /device:TPU:0, one launch (start us, length us, event | category | flops | bytes accessed | tf_op | source)
XLA Modules:
  0.0 224.8 jit_solution(14852149065513866713)
XLA Ops:
  3.9 5.0 %collective-permute-start = (bf16[8,32,384]{2,1,0:T(8,128)(2,1)}, bf16[8,32,384]{2,1,0:T(8,128)(2,1)}, u32[]{:S(2)}, u32[]{:S(2)}) collective-permute-start(bf16[8,32,384]{2,1,0:T(8,128)(2,1)} %get-tuple-element.120), channel_id=1, source_target_pairs={{0,5},{1,4},{2,7},{3,6},{4,1},{5,0},{6,3},{7,2},{8,13},{9,12},{10,... | collective-permute-start | bytes 589832 | tf_op jit(solution)/shard_map/ppermute | solution.py:345
  11.0 3.2 %pack.7 = (bf16[24,32,384]{2,1,0:T(8,128)(2,1)}, bf16[24,32,384]{2,1,0:T(8,128)(2,1)}) custom-call(s32[5]{0:T(128)} %pad_add_fusion.xi_ref, bf16[64,3,8,1536]{3,2,1,0:T(8,128)(2,1)} %bitcast.16, bf16[8,32,384]{2,1,0:T(8,128)(2,1)} %get-tuple-element.112.refs_0_), custom_call_target="tpu_custom_call" | custom-call | flops 1 | bytes 1 | tf_op jit(solution)/shard_map/pack/pallas_call | solution.py:80
  16.9 3.6 %collective-permute-start.3 = (bf16[8,32,384]{2,1,0:T(8,128)(2,1)}, bf16[8,32,384]{2,1,0:T(8,128)(2,1)}, u32[]{:S(2)}, u32[]{:S(2)}) collective-permute-start(bf16[8,32,384]{2,1,0:T(8,128)(2,1)} %get-tuple-element.122.refs_0_), channel_id=1, source_target_pairs={{0,6},{1,7},{2,4},{3,5},{4,2},{5,3},{6,0},{7,1},{8,14},{9,15},{10,... | collective-permute-start | bytes 589832 | tf_op jit(solution)/shard_map/ppermute | solution.py:345
  22.8 3.2 %pack.9 = (bf16[24,32,384]{2,1,0:T(8,128)(2,1)}, bf16[24,32,384]{2,1,0:T(8,128)(2,1)}) custom-call(s32[5]{0:T(128)} %pad_add_fusion.xi_ref, bf16[64,3,8,1536]{3,2,1,0:T(8,128)(2,1)} %bitcast.18, bf16[8,32,384]{2,1,0:T(8,128)(2,1)} %get-tuple-element.122.refs_0_), custom_call_target="tpu_custom_call" | custom-call | flops 1 | bytes 1 | tf_op jit(solution)/shard_map/pack/pallas_call | solution.py:80
  30.5 4.8 %collective-permute-done.1.refs_1_ = bf16[11,32,384]{2,1,0:T(8,128)(2,1)} collective-permute-done((bf16[11,32,384]{2,1,0:T(8,128)(2,1)}, bf16[11,32,384]{2,1,0:T(8,128)(2,1)}, u32[]{:S(2)}, u32[]{:S(2)}) %collective-permute-start.1) | collective-permute-done | bytes 270368 | tf_op jit(solution)/shard_map/ppermute | solution.py:345
  35.7 9.2 %collective-permute-start.2 = (bf16[16,32,384]{2,1,0:T(8,128)(2,1)}, bf16[16,32,384]{2,1,0:T(8,128)(2,1)S(1)}, u32[]{:S(2)}, u32[]{:S(2)}) collective-permute-start(bf16[16,32,384]{2,1,0:T(8,128)(2,1)} %get-tuple-element.131.refs_0_), channel_id=1, source_target_pairs={{0,4},{1,5},{2,6},{3,7},{4,0},{5,1},{6,2},{7,3},{8,12},{9,13},{10,... | collective-permute-start | bytes 1179656 | tf_op jit(solution)/shard_map/ppermute | solution.py:345
  44.9 3.0 %pack.11 = (bf16[16,32,384]{2,1,0:T(8,128)(2,1)}, bf16[16,32,384]{2,1,0:T(8,128)(2,1)}) custom-call(s32[5]{0:T(128)} %pad_add_fusion.xi_ref, bf16[64,3,8,1536]{3,2,1,0:T(8,128)(2,1)} %bitcast.20, bf16[16,32,384]{2,1,0:T(8,128)(2,1)} %get-tuple-element.131.refs_0_), custom_call_target="tpu_custom_call" | custom-call | flops 1 | bytes 1 | tf_op jit(solution)/shard_map/pack/pallas_call | solution.py:80
  48.0 11.5 %collective-permute-done.4.refs_5_ = bf16[24,32,384]{2,1,0:T(8,128)(2,1)S(1)} collective-permute-done((bf16[24,32,384]{2,1,0:T(8,128)(2,1)}, bf16[24,32,384]{2,1,0:T(8,128)(2,1)S(1)}, u32[]{:S(2)}, u32[]{:S(2)}) %collective-permute-start.4) | collective-permute-done | bytes 589856 | tf_op jit(solution)/shard_map/ppermute | solution.py:345
  62.0 10.0 %collective-permute-done.8.refs_6_ = bf16[24,32,384]{2,1,0:T(8,128)(2,1)S(1)} collective-permute-done((bf16[24,32,384]{2,1,0:T(8,128)(2,1)}, bf16[24,32,384]{2,1,0:T(8,128)(2,1)S(1)}, u32[]{:S(2)}, u32[]{:S(2)}) %collective-permute-start.8) | collective-permute-done | bytes 589856 | tf_op jit(solution)/shard_map/ppermute | solution.py:345
  72.1 3.7 %collective-permute-start.9 = (bf16[16,32,384]{2,1,0:T(8,128)(2,1)}, bf16[16,32,384]{2,1,0:T(8,128)(2,1)}, u32[]{:S(2)}, u32[]{:S(2)}) collective-permute-start(bf16[16,32,384]{2,1,0:T(8,128)(2,1)} %get-tuple-element.143), channel_id=1, source_target_pairs={{0,7},{1,6},{2,5},{3,4},{4,3},{5,2},{6,1},{7,0},{8,15},{9,14},{10,... | collective-permute-start | bytes 1179656 | tf_op jit(solution)/shard_map/ppermute | solution.py:345
  79.1 4.6 %slopes.3 = (bf16[8,32,384]{2,1,0:T(8,128)(2,1)}, bf16[8,32,384]{2,1,0:T(8,128)(2,1)}, bf16[8,32,384]{2,1,0:T(8,128)(2,1)}, bf16[8,32,384]{2,1,0:T(8,128)(2,1)},...) custom-call(bf16[512,512]{1,0:T(8,128)(2,1)} %copy-done.14, ...), custom_call_target="tpu_custom_call" | custom-call | flops 1 | bytes 1 | tf_op jit(solution)/shard_map/slopes/pallas_call | solution.py:130
  83.7 3.1 %collective-permute-start.11 = (bf16[8,32,384]{2,1,0:T(8,128)(2,1)}, bf16[8,32,384]{2,1,0:T(8,128)(2,1)S(1)}, u32[]{:S(2)}, u32[]{:S(2)}) collective-permute-start(bf16[8,32,384]{2,1,0:T(8,128)(2,1)} %get-tuple-element.158), channel_id=1, source_target_pairs={{0,5},{1,4},{2,7},{3,6},{4,1},{5,0},{6,3},{7,2},{8,13},{9,12},{10,... | collective-permute-start | bytes 589832 | tf_op jit(solution)/shard_map/ppermute | solution.py:345
  86.9 18.3 %collective-permute-done.5.refs_2_ = bf16[16,32,384]{2,1,0:T(8,128)(2,1)S(1)} collective-permute-done((bf16[16,32,384]{2,1,0:T(8,128)(2,1)}, bf16[16,32,384]{2,1,0:T(8,128)(2,1)S(1)}, u32[]{:S(2)}, u32[]{:S(2)}) %collective-permute-start.5) | collective-permute-done | bytes 393248 | tf_op jit(solution)/shard_map/ppermute | solution.py:345
  106.0 17.6 %collective-permute-start.14 = (bf16[14,32,384]{2,1,0:T(8,128)(2,1)}, bf16[14,32,384]{2,1,0:T(8,128)(2,1)S(1)}, u32[]{:S(2)}, u32[]{:S(2)}) collective-permute-start(bf16[14,32,384]{2,1,0:T(8,128)(2,1)} %get-tuple-element.166), channel_id=1, source_target_pairs={{0,3},{1,2},{2,1},{3,0},{4,7},{5,6},{6,5},{7,4},{8,11},{9,10},{10,... | collective-permute-start | bytes 1032200 | tf_op jit(solution)/shard_map/ppermute | solution.py:345
  131.1 14.6 %collective-permute-done.12.near_ref = bf16[8,32,384]{2,1,0:T(8,128)(2,1)S(1)} collective-permute-done((bf16[8,32,384]{2,1,0:T(8,128)(2,1)}, bf16[8,32,384]{2,1,0:T(8,128)(2,1)S(1)}, u32[]{:S(2)}, u32[]{:S(2)}) %collective-permute-start.12) | collective-permute-done | bytes 196640 | tf_op jit(solution)/shard_map/ppermute | solution.py:345
  148.4 6.2 %slopes.2 = (bf16[16,32,384]{2,1,0:T(8,128)(2,1)}, bf16[16,32,384]{2,1,0:T(8,128)(2,1)}, bf16[16,32,384]{2,1,0:T(8,128)(2,1)}, bf16[16,32,384]{2,1,0:T(8,128)(2,...) custom-call(bf16[512,512]{1,0:T(8,128)(2,1)} %copy-done.14, ...), custom_call_target="tpu_custom_call" | custom-call | flops 1 | bytes 1 | tf_op jit(solution)/shard_map/slopes/pallas_call | solution.py:130
  154.7 3.8 %collective-permute-start.22 = (bf16[16,32,384]{2,1,0:T(8,128)(2,1)}, bf16[16,32,384]{2,1,0:T(8,128)(2,1)S(1)}, u32[]{:S(2)}, u32[]{:S(2)}) collective-permute-start(bf16[16,32,384]{2,1,0:T(8,128)(2,1)} %get-tuple-element.180), channel_id=1, source_target_pairs={{0,5},{1,4},{2,7},{3,6},{4,1},{5,0},{6,3},{7,2},{8,13},{9,12},{10,... | collective-permute-start | bytes 1179656 | tf_op jit(solution)/shard_map/ppermute | solution.py:345
  168.5 3.4 %bases.3.refs_0_.base_ref = f32[64,1,8,1536]{3,2,1,0:T(8,128)S(1)} custom-call(bf16[64,3,8,1536]{3,2,1,0:T(8,128)(2,1)S(1)} %bitcast.21, bf16[64,3,8,1536]{3,2,1,0:T(8,128)(2,1)S(1)} %bitcast.22, bf16[1536,1536]{1,0:T(8,128)(2,1)S(1)} %copy-done.1, f32[1,1536]{1,0:T(1,128)S(1)} %broadcast_in_dim.55.m_ref, bf16[3,64,8,256]{3,2,1,0:T(8,128)(2,1)S(1)} %refine.1.f_ref, ...), custom_call_target="tpu_custom_call" | custom-call | flops 1 | bytes 1 | tf_op jit(solution)/shard_map/bases/pallas_call | solution.py:253
  172.0 7.3 %bases.2.refs_1_.base_ref = f32[64,2,8,1536]{3,2,1,0:T(8,128)S(1)} custom-call(bf16[64,3,8,1536]{3,2,1,0:T(8,128)(2,1)S(1)} %bitcast.23, bf16[64,3,8,1536]{3,2,1,0:T(8,128)(2,1)S(1)} %bitcast.24, bf16[1536,1536]{1,0:T(8,128)(2,1)S(1)} %copy-done.1, f32[1,1536]{1,0:T(1,128)S(1)} %broadcast_in_dim.55.m_ref, bf16[3,64,8,256]{3,2,1,0:T(8,128)(2,1)S(1)} %refine.1.f_ref, ...), custom_call_target="tpu_custom_call" | custom-call | flops 1 | bytes 1 | tf_op jit(solution)/shard_map/bases/pallas_call | solution.py:253
  183.9 7.0 %collective-permute-done.22.far_ref = bf16[16,32,384]{2,1,0:T(8,128)(2,1)S(1)} collective-permute-done((bf16[16,32,384]{2,1,0:T(8,128)(2,1)}, bf16[16,32,384]{2,1,0:T(8,128)(2,1)S(1)}, u32[]{:S(2)}, u32[]{:S(2)}) %collective-permute-start.22) | collective-permute-done | bytes 393248 | tf_op jit(solution)/shard_map/ppermute | solution.py:345
  200.8 2.9 %combine.12 = (bf16[64,3,8,1536]{3,2,1,0:T(8,128)(2,1)}, bf16[64,3,8,1536]{3,2,1,0:T(8,128)(2,1)}, f32[8,128]{1,0:T(8,128)}) custom-call(s32[5]{0:T(128)S(1)} %copy-done.13, f32[64,2,8,1536]{3,2,1,0:T(8,128)S(1)} %bases.2.refs_1_.base_ref, bf16[64,3,8,1536]{3,2,1,0:T(8,128)(2,1)S(1)} %bitcast.33, ...), custom_call_target="tpu_custom_call", output_to_operand_aliasing={{0}: (6, {}), {1}: (7, {})} | custom-call | flops 1 | bytes 1 | tf_op jit(solution)/shard_map/combine/pallas_call | solution.py:299
  203.8 12.3 %collective-permute-done.25.far_ref = bf16[16,32,384]{2,1,0:T(8,128)(2,1)S(1)} collective-permute-done((bf16[16,32,384]{2,1,0:T(8,128)(2,1)S(1)}, bf16[16,32,384]{2,1,0:T(8,128)(2,1)S(1)}, u32[]{:S(2)}, u32[]{:S(2)}) %collective-permute-start.25) | collective-permute-done | bytes 393248 | tf_op jit(solution)/shard_map/ppermute | solution.py:345
  219.0 2.9 %combine.14 = (bf16[64,3,8,1536]{3,2,1,0:T(8,128)(2,1)}, bf16[64,3,8,1536]{3,2,1,0:T(8,128)(2,1)}, f32[8,128]{1,0:T(8,128)}) custom-call(s32[5]{0:T(128)S(1)} %copy-done.13, f32[64,2,8,1536]{3,2,1,0:T(8,128)S(1)} %bases.2.refs_1_.base_ref, bf16[64,3,8,1536]{3,2,1,0:T(8,128)(2,1)S(1)} %bitcast.37, ...), custom_call_target="tpu_custom_call", output_to_operand_aliasing={{0}: (6, {}), {1}: (7, {})} | custom-call | flops 1 | bytes 1 | tf_op jit(solution)/shard_map/combine/pallas_call | solution.py:299
  221.9 2.9 %combine.15 = (bf16[64,3,8,1536]{3,2,1,0:T(8,128)(2,1)}, bf16[64,3,8,1536]{3,2,1,0:T(8,128)(2,1)}, f32[8,128]{1,0:T(8,128)}) custom-call(s32[5]{0:T(128)S(1)} %copy-done.13, f32[64,2,8,1536]{3,2,1,0:T(8,128)S(1)} %bases.2.refs_1_.base_ref, bf16[64,3,8,1536]{3,2,1,0:T(8,128)(2,1)S(1)} %bitcast.39, ...), custom_call_target="tpu_custom_call", output_to_operand_aliasing={{0}: (6, {}), {1}: (7, {})} | custom-call | flops 1 | bytes 1 | tf_op jit(solution)/shard_map/combine/pallas_call | solution.py:299
  (145 shorter events, 59.4 us)
Async XLA Ops:
  3.9 25.4 %collective-permute-start = (bf16[8,32,384]{2,1,0:T(8,128)(2,1)}, bf16[8,32,384]{2,1,0:T(8,128)(2,1)}, u32[]{:S(2)}, u32[]{:S(2)}) collective-permute-start(bf16[8,32,384]{2,1,0:T(8,128)(2,1)} %get-tuple-element.120), channel_id=1, source_target_pairs={{0,5},{1,4},{2,7},{3,6},{4,1},{5,0},{6,3},{7,2},{8,13},{9,12},{10,... | collective-permute-start | bytes 589832 | tf_op jit(solution)/shard_map/ppermute | solution.py:345
  10.7 24.6 %collective-permute-start.1 = (bf16[11,32,384]{2,1,0:T(8,128)(2,1)}, bf16[11,32,384]{2,1,0:T(8,128)(2,1)}, u32[]{:S(2)}, u32[]{:S(2)}) collective-permute-start(bf16[11,32,384]{2,1,0:T(8,128)(2,1)} %pad_maximum_fusion), channel_id=1, source_target_pairs={{0,4},{1,5},{2,6},{3,7},{4,0},{5,1},{6,2},{7,3},{8,12},{9,13},{10,... | collective-permute-start | bytes 811016 | tf_op jit(solution)/shard_map/ppermute | solution.py:345
  21.8 37.7 %collective-permute-start.4 = (bf16[24,32,384]{2,1,0:T(8,128)(2,1)}, bf16[24,32,384]{2,1,0:T(8,128)(2,1)S(1)}, u32[]{:S(2)}, u32[]{:S(2)}) collective-permute-start(bf16[24,32,384]{2,1,0:T(8,128)(2,1)} %get-tuple-element.123.refs_0_), channel_id=1, source_target_pairs={{0,2},{1,3},{2,0},{3,1},{4,6},{5,7},{6,4},{7,5},{8,10},{9,11},{10,... | collective-permute-start | bytes 1769480 | tf_op jit(solution)/shard_map/ppermute | solution.py:345
  21.8 38.1 %collective-permute-start.6 = (bf16[8,32,384]{2,1,0:T(8,128)(2,1)}, bf16[8,32,384]{2,1,0:T(8,128)(2,1)}, u32[]{:S(2)}, u32[]{:S(2)}) collective-permute-start(bf16[8,32,384]{2,1,0:T(8,128)(2,1)} %get-tuple-element.124), channel_id=1, source_target_pairs={{0,7},{1,6},{2,5},{3,4},{4,3},{5,2},{6,1},{7,0},{8,15},{9,14},{10,... | collective-permute-start | bytes 589832 | tf_op jit(solution)/shard_map/ppermute | solution.py:345
  29.2 42.8 %collective-permute-start.8 = (bf16[24,32,384]{2,1,0:T(8,128)(2,1)}, bf16[24,32,384]{2,1,0:T(8,128)(2,1)S(1)}, u32[]{:S(2)}, u32[]{:S(2)}) collective-permute-start(bf16[24,32,384]{2,1,0:T(8,128)(2,1)} %get-tuple-element.126), channel_id=1, source_target_pairs={{0,3},{1,2},{2,1},{3,0},{4,7},{5,6},{6,5},{7,4},{8,11},{9,10},{10,... | collective-permute-start | bytes 1769480 | tf_op jit(solution)/shard_map/ppermute | solution.py:345
  35.3 42.9 %collective-permute-start.10 = (bf16[24,32,384]{2,1,0:T(8,128)(2,1)}, bf16[24,32,384]{2,1,0:T(8,128)(2,1)S(1)}, u32[]{:S(2)}, u32[]{:S(2)}) collective-permute-start(bf16[24,32,384]{2,1,0:T(8,128)(2,1)} %get-tuple-element.135), channel_id=1, source_target_pairs={{0,1},{1,0},{2,3},{3,2},{4,5},{5,4},{6,7},{7,6},{8,9},{9,8},{10,11... | collective-permute-start | bytes 1769480 | tf_op jit(solution)/shard_map/ppermute | solution.py:345
  35.7 48.0 %collective-permute-start.2 = (bf16[16,32,384]{2,1,0:T(8,128)(2,1)}, bf16[16,32,384]{2,1,0:T(8,128)(2,1)S(1)}, u32[]{:S(2)}, u32[]{:S(2)}) collective-permute-start(bf16[16,32,384]{2,1,0:T(8,128)(2,1)} %get-tuple-element.131.refs_0_), channel_id=1, source_target_pairs={{0,4},{1,5},{2,6},{3,7},{4,0},{5,1},{6,2},{7,3},{8,12},{9,13},{10,... | collective-permute-start | bytes 1179656 | tf_op jit(solution)/shard_map/ppermute | solution.py:345
  59.4 45.8 %collective-permute-start.5 = (bf16[16,32,384]{2,1,0:T(8,128)(2,1)}, bf16[16,32,384]{2,1,0:T(8,128)(2,1)S(1)}, u32[]{:S(2)}, u32[]{:S(2)}) collective-permute-start(bf16[16,32,384]{2,1,0:T(8,128)(2,1)} %get-tuple-element.137), channel_id=1, source_target_pairs={{0,5},{1,4},{2,7},{3,6},{4,1},{5,0},{6,3},{7,2},{8,13},{9,12},{10,... | collective-permute-start | bytes 1179656 | tf_op jit(solution)/shard_map/ppermute | solution.py:345
  59.8 45.4 %collective-permute-start.7 = (bf16[16,32,384]{2,1,0:T(8,128)(2,1)}, bf16[16,32,384]{2,1,0:T(8,128)(2,1)}, u32[]{:S(2)}, u32[]{:S(2)}) collective-permute-start(bf16[16,32,384]{2,1,0:T(8,128)(2,1)} %get-tuple-element.140), channel_id=1, source_target_pairs={{0,6},{1,7},{2,4},{3,5},{4,2},{5,3},{6,0},{7,1},{8,14},{9,15},{10,... | collective-permute-start | bytes 1179656 | tf_op jit(solution)/shard_map/ppermute | solution.py:345
  72.1 33.9 %collective-permute-start.9 = (bf16[16,32,384]{2,1,0:T(8,128)(2,1)}, bf16[16,32,384]{2,1,0:T(8,128)(2,1)}, u32[]{:S(2)}, u32[]{:S(2)}) collective-permute-start(bf16[16,32,384]{2,1,0:T(8,128)(2,1)} %get-tuple-element.143), channel_id=1, source_target_pairs={{0,7},{1,6},{2,5},{3,4},{4,3},{5,2},{6,1},{7,0},{8,15},{9,14},{10,... | collective-permute-start | bytes 1179656 | tf_op jit(solution)/shard_map/ppermute | solution.py:345
  83.7 42.6 %collective-permute-start.11 = (bf16[8,32,384]{2,1,0:T(8,128)(2,1)}, bf16[8,32,384]{2,1,0:T(8,128)(2,1)S(1)}, u32[]{:S(2)}, u32[]{:S(2)}) collective-permute-start(bf16[8,32,384]{2,1,0:T(8,128)(2,1)} %get-tuple-element.158), channel_id=1, source_target_pairs={{0,5},{1,4},{2,7},{3,6},{4,1},{5,0},{6,3},{7,2},{8,13},{9,12},{10,... | collective-permute-start | bytes 589832 | tf_op jit(solution)/shard_map/ppermute | solution.py:345
  105.2 49.4 %collective-permute-start.13 = (bf16[14,32,384]{2,1,0:T(8,128)(2,1)}, bf16[14,32,384]{2,1,0:T(8,128)(2,1)S(1)}, u32[]{:S(2)}, u32[]{:S(2)}) collective-permute-start(bf16[14,32,384]{2,1,0:T(8,128)(2,1)} %get-tuple-element.162), channel_id=1, source_target_pairs={{0,2},{1,3},{2,0},{3,1},{4,6},{5,7},{6,4},{7,5},{8,10},{9,11},{10,... | collective-permute-start | bytes 1032200 | tf_op jit(solution)/shard_map/ppermute | solution.py:345
  106.0 52.6 %collective-permute-start.14 = (bf16[14,32,384]{2,1,0:T(8,128)(2,1)}, bf16[14,32,384]{2,1,0:T(8,128)(2,1)S(1)}, u32[]{:S(2)}, u32[]{:S(2)}) collective-permute-start(bf16[14,32,384]{2,1,0:T(8,128)(2,1)} %get-tuple-element.166), channel_id=1, source_target_pairs={{0,3},{1,2},{2,1},{3,0},{4,7},{5,6},{6,5},{7,4},{8,11},{9,10},{10,... | collective-permute-start | bytes 1032200 | tf_op jit(solution)/shard_map/ppermute | solution.py:345
  127.0 31.6 %collective-permute-start.15 = (bf16[14,32,384]{2,1,0:T(8,128)(2,1)}, bf16[14,32,384]{2,1,0:T(8,128)(2,1)S(1)}, u32[]{:S(2)}, u32[]{:S(2)}) collective-permute-start(bf16[14,32,384]{2,1,0:T(8,128)(2,1)} %get-tuple-element.168), channel_id=1, source_target_pairs={{0,1},{1,0},{2,3},{3,2},{4,5},{5,4},{6,7},{7,6},{8,9},{9,8},{10,11... | collective-permute-start | bytes 1032200 | tf_op jit(solution)/shard_map/ppermute | solution.py:345
  128.4 26.3 %collective-permute-start.17 = (bf16[8,32,384]{2,1,0:T(8,128)(2,1)}, bf16[8,32,384]{2,1,0:T(8,128)(2,1)S(1)}, u32[]{:S(2)}, u32[]{:S(2)}) collective-permute-start(bf16[8,32,384]{2,1,0:T(8,128)(2,1)} %get-tuple-element.164), channel_id=1, source_target_pairs={{0,6},{1,7},{2,4},{3,5},{4,2},{5,3},{6,0},{7,1},{8,14},{9,15},{10,... | collective-permute-start | bytes 589832 | tf_op jit(solution)/shard_map/ppermute | solution.py:345
  146.4 36.8 %collective-permute-start.19 = (bf16[8,32,384]{2,1,0:T(8,128)(2,1)}, bf16[8,32,384]{2,1,0:T(8,128)(2,1)}, u32[]{:S(2)}, u32[]{:S(2)}) collective-permute-start(bf16[8,32,384]{2,1,0:T(8,128)(2,1)} %get-tuple-element.170), channel_id=1, source_target_pairs={{0,7},{1,6},{2,5},{3,4},{4,3},{5,2},{6,1},{7,0},{8,15},{9,14},{10,... | collective-permute-start | bytes 589832 | tf_op jit(solution)/shard_map/ppermute | solution.py:345
  154.6 29.0 %collective-permute-start.21 = (bf16[16,32,384]{2,1,0:T(8,128)(2,1)}, bf16[16,32,384]{2,1,0:T(8,128)(2,1)S(1)}, u32[]{:S(2)}, u32[]{:S(2)}) collective-permute-start(bf16[16,32,384]{2,1,0:T(8,128)(2,1)} %get-tuple-element.178), channel_id=1, source_target_pairs={{0,4},{1,5},{2,6},{3,7},{4,0},{5,1},{6,2},{7,3},{8,12},{9,13},{10,... | collective-permute-start | bytes 1179656 | tf_op jit(solution)/shard_map/ppermute | solution.py:345
  154.7 36.2 %collective-permute-start.22 = (bf16[16,32,384]{2,1,0:T(8,128)(2,1)}, bf16[16,32,384]{2,1,0:T(8,128)(2,1)S(1)}, u32[]{:S(2)}, u32[]{:S(2)}) collective-permute-start(bf16[16,32,384]{2,1,0:T(8,128)(2,1)} %get-tuple-element.180), channel_id=1, source_target_pairs={{0,5},{1,4},{2,7},{3,6},{4,1},{5,0},{6,3},{7,2},{8,13},{9,12},{10,... | collective-permute-start | bytes 1179656 | tf_op jit(solution)/shard_map/ppermute | solution.py:345
  161.5 39.4 %collective-permute-start.24 = (bf16[16,32,384]{2,1,0:T(8,128)(2,1)}, bf16[16,32,384]{2,1,0:T(8,128)(2,1)S(1)}, u32[]{:S(2)}, u32[]{:S(2)}) collective-permute-start(bf16[16,32,384]{2,1,0:T(8,128)(2,1)} %get-tuple-element.182), channel_id=1, source_target_pairs={{0,2},{1,3},{2,0},{3,1},{4,6},{5,7},{6,4},{7,5},{8,10},{9,11},{10,... | collective-permute-start | bytes 1179656 | tf_op jit(solution)/shard_map/ppermute | solution.py:345
  183.7 32.4 %collective-permute-start.25 = (bf16[16,32,384]{2,1,0:T(8,128)(2,1)S(1)}, bf16[16,32,384]{2,1,0:T(8,128)(2,1)S(1)}, u32[]{:S(2)}, u32[]{:S(2)}) collective-permute-start(bf16[16,32,384]{2,1,0:T(8,128)(2,1)S(1)} %hold.3), channel_id=1, source_target_pairs={{0,3},{1,2},{2,1},{3,0},{4,7},{5,6},{6,5},{7,4},{8,11},{9,10},{10,... | collective-permute-start | bytes 1179656 | tf_op jit(solution)/shard_map/ppermute | solution.py:345
  190.9 28.0 %collective-permute-start.23 = (bf16[16,32,384]{2,1,0:T(8,128)(2,1)S(1)}, bf16[16,32,384]{2,1,0:T(8,128)(2,1)S(1)}, u32[]{:S(2)}, u32[]{:S(2)}) collective-permute-start(bf16[16,32,384]{2,1,0:T(8,128)(2,1)S(1)} %copy-done.27), channel_id=1, source_target_pairs={{0,1},{1,0},{2,3},{3,2},{4,5},{5,4},{6,7},{7,6},{8,9},{9,8},{10,11... | collective-permute-start | bytes 1179656 | tf_op jit(solution)/shard_map/ppermute | solution.py:345
  192.4 29.5 %collective-permute-start.18 = (bf16[16,32,384]{2,1,0:T(8,128)(2,1)S(1)}, bf16[16,32,384]{2,1,0:T(8,128)(2,1)S(1)}, u32[]{:S(2)}, u32[]{:S(2)}) collective-permute-start(bf16[16,32,384]{2,1,0:T(8,128)(2,1)S(1)} %copy-done.26), channel_id=1, source_target_pairs={{0,6},{1,7},{2,4},{3,5},{4,2},{5,3},{6,0},{7,1},{8,14},{9,15},{10,... | collective-permute-start | bytes 1179656 | tf_op jit(solution)/shard_map/ppermute | solution.py:345
  195.0 26.9 %collective-permute-start.20 = (bf16[16,32,384]{2,1,0:T(8,128)(2,1)S(1)}, bf16[16,32,384]{2,1,0:T(8,128)(2,1)S(1)}, u32[]{:S(2)}, u32[]{:S(2)}) collective-permute-start(bf16[16,32,384]{2,1,0:T(8,128)(2,1)S(1)} %hold.2), channel_id=1, source_target_pairs={{0,7},{1,6},{2,5},{3,4},{4,3},{5,2},{6,1},{7,0},{8,15},{9,14},{10,... | collective-permute-start | bytes 1179656 | tf_op jit(solution)/shard_map/ppermute | solution.py:345
  200.8 21.0 %collective-permute-start.26 = (f32[8,128]{1,0:T(8,128)S(1)}, f32[8,128]{1,0:T(8,128)S(1)}, u32[]{:S(2)}, u32[]{:S(2)}) collective-permute-start(f32[8,128]{1,0:T(8,128)S(1)} %get-tuple-element.219), channel_id=1, source_target_pairs={{0,8},{8,16},{16,24},{24,0},{1,9},{9,17},{17,25},{25,1},{2,10},{10... | collective-permute-start | bytes 12296 | tf_op jit(solution)/shard_map/ppermute | solution.py:435
  (32 other events, 579.0 us)

commit v4 on v3

--- a/solution.py
+++ b/solution.py
@@ -10,7 +10,7 @@
 rk_weight = 0.5
 mib = 1024 * 1024
 lanes = 128
-in_flight = 5
+in_flight = 8
 light = pl.CostEstimate(flops=1, bytes_accessed=1, transcendentals=0)
 
 

time: 228 us -> 223 us (0.978)
  waiting for transfers between devices: 83.5 us -> 77.3 us
  starting transfers between devices: 64.3 us -> 68.2 us
    ppermute x25, waiting for transfers between devices: 82 us -> 77.3 us  [trade(): lax.ppermute(block, 'row', [(i, i ^ k) for i in range(devices)])]
    ppermute x25, starting transfers between devices: 62.9 us -> 66.7 us  [trade(): lax.ppermute(block, 'row', [(i, i ^ k) for i in range(devices)])]
    unnamed x65 -> x69, local copies, waits for them, and re-layouts: 7.77 us -> 7.94 us
  transfers between devices with their start and end apart: 27 -> 27, of which waited for: 11 -> 9; matrix products, arithmetic and copies ran while one was open for 3% -> 2% of each run, Pallas kernels for 25% -> 25%
where the time goes in v4:
time: 223 us; the launch traced here: 221 us
  waiting for transfers between devices  77.3 us (35%)
  starting transfers between devices  68.2 us (31%)
  Pallas kernels  60.9 us (27%)
  local copies, waits for them, and re-layouts  10.2 us (5%)
  other arithmetic  3.73 us (2%)
    ppermute x25, waiting for transfers between devices, trade(): lax.ppermute(block, 'row', [(i, i ^ k) for i in range(devices)])  77.3 us
    ppermute x25, starting transfers between devices, trade(): lax.ppermute(block, 'row', [(i, i ^ k) for i in range(devices)])  66.7 us
    pallas_call x8, Pallas kernels, combine(): pl.pallas_call(combine_kernel, grid_spec=pltpu.PrefetchScalarGridSpec(num...  20.1 us
    pallas_call x6, Pallas kernels, pack(): pl.pallas_call(pack_kernel, grid_spec=pltpu.PrefetchScalarGridSpec(num_sc...  17.8 us
    pallas_call x2, Pallas kernels, slopes(): pl.pallas_call(functools.partial(slope_kernel, planes, places, riders), i...  10.9 us
    pallas_call x2, Pallas kernels, bases(): pl.pallas_call(base_kernel, grid=(rows // part, len(comps)), in_specs=[pl...  10.7 us
    unnamed x69, local copies, waits for them, and re-layouts  7.94 us
  transfers between devices with their start and end apart: 27, of which 9 were waited for; matrix products, arithmetic and copies ran while one was open for 2% of the time, Pallas kernels for 25%

profile of v4, /device:TPU:0, one launch (start us, length us, event | category | flops | bytes accessed | tf_op | source)
XLA Modules:
  0.0 221.4 jit_solution(1597609025290597558)
XLA Ops:
  3.8 5.0 %collective-permute-start = (bf16[8,32,384]{2,1,0:T(8,128)(2,1)}, bf16[8,32,384]{2,1,0:T(8,128)(2,1)S(1)}, u32[]{:S(2)}, u32[]{:S(2)}) collective-permute-start(bf16[8,32,384]{2,1,0:T(8,128)(2,1)} %get-tuple-element.113), channel_id=1, source_target_pairs={{0,5},{1,4},{2,7},{3,6},{4,1},{5,0},{6,3},{7,2},{8,13},{9,12},{10,... | collective-permute-start | bytes 589832 | tf_op jit(solution)/shard_map/ppermute | solution.py:345
  10.9 3.2 %pack.7 = (bf16[24,32,384]{2,1,0:T(8,128)(2,1)}, bf16[24,32,384]{2,1,0:T(8,128)(2,1)}) custom-call(s32[5]{0:T(128)} %pad_add_fusion.xi_ref, bf16[64,3,8,1536]{3,2,1,0:T(8,128)(2,1)} %bitcast.16, bf16[8,32,384]{2,1,0:T(8,128)(2,1)} %get-tuple-element.102.refs_0_), custom_call_target="tpu_custom_call" | custom-call | flops 1 | bytes 1 | tf_op jit(solution)/shard_map/pack/pallas_call | solution.py:80
  16.8 3.6 %collective-permute-start.2 = (bf16[8,32,384]{2,1,0:T(8,128)(2,1)}, bf16[8,32,384]{2,1,0:T(8,128)(2,1)}, u32[]{:S(2)}, u32[]{:S(2)}) collective-permute-start(bf16[8,32,384]{2,1,0:T(8,128)(2,1)} %get-tuple-element.115.refs_0_), channel_id=1, source_target_pairs={{0,6},{1,7},{2,4},{3,5},{4,2},{5,3},{6,0},{7,1},{8,14},{9,15},{10,... | collective-permute-start | bytes 589832 | tf_op jit(solution)/shard_map/ppermute | solution.py:345
  22.7 3.4 %pack.9 = (bf16[24,32,384]{2,1,0:T(8,128)(2,1)}, bf16[24,32,384]{2,1,0:T(8,128)(2,1)}) custom-call(s32[5]{0:T(128)} %pad_add_fusion.xi_ref, bf16[64,3,8,1536]{3,2,1,0:T(8,128)(2,1)} %bitcast.18, bf16[8,32,384]{2,1,0:T(8,128)(2,1)} %get-tuple-element.115.refs_0_), custom_call_target="tpu_custom_call" | custom-call | flops 1 | bytes 1 | tf_op jit(solution)/shard_map/pack/pallas_call | solution.py:80
  29.1 4.2 %collective-permute-done.refs_2_ = bf16[8,32,384]{2,1,0:T(8,128)(2,1)S(1)} collective-permute-done((bf16[8,32,384]{2,1,0:T(8,128)(2,1)}, bf16[8,32,384]{2,1,0:T(8,128)(2,1)S(1)}, u32[]{:S(2)}, u32[]{:S(2)}) %collective-permute-start) | collective-permute-done | bytes 196640 | tf_op jit(solution)/shard_map/ppermute | solution.py:345
  35.1 14.5 %collective-permute-start.8 = (bf16[16,32,384]{2,1,0:T(8,128)(2,1)}, bf16[16,32,384]{2,1,0:T(8,128)(2,1)S(1)}, u32[]{:S(2)}, u32[]{:S(2)}) collective-permute-start(bf16[16,32,384]{2,1,0:T(8,128)(2,1)} %get-tuple-element.119.refs_0_), channel_id=1, source_target_pairs={{0,4},{1,5},{2,6},{3,7},{4,0},{5,1},{6,2},{7,3},{8,12},{9,13},{10,... | collective-permute-start | bytes 1179656 | tf_op jit(solution)/shard_map/ppermute | solution.py:345
  50.5 3.1 %pack.11 = (bf16[16,32,384]{2,1,0:T(8,128)(2,1)}, bf16[16,32,384]{2,1,0:T(8,128)(2,1)}) custom-call(s32[5]{0:T(128)} %pad_add_fusion.xi_ref, bf16[64,3,8,1536]{3,2,1,0:T(8,128)(2,1)} %bitcast.20, bf16[16,32,384]{2,1,0:T(8,128)(2,1)} %get-tuple-element.119.refs_0_), custom_call_target="tpu_custom_call" | custom-call | flops 1 | bytes 1 | tf_op jit(solution)/shard_map/pack/pallas_call | solution.py:80
  55.4 5.5 %collective-permute-done.6.refs_7_ = bf16[24,32,384]{2,1,0:T(8,128)(2,1)S(1)} collective-permute-done((bf16[24,32,384]{2,1,0:T(8,128)(2,1)}, bf16[24,32,384]{2,1,0:T(8,128)(2,1)S(1)}, u32[]{:S(2)}, u32[]{:S(2)}) %collective-permute-start.6) | collective-permute-done | bytes 589856 | tf_op jit(solution)/shard_map/ppermute | solution.py:345
  60.9 6.7 %collective-permute-done.4.refs_5_ = bf16[24,32,384]{2,1,0:T(8,128)(2,1)S(1)} collective-permute-done((bf16[24,32,384]{2,1,0:T(8,128)(2,1)S(1)}, bf16[24,32,384]{2,1,0:T(8,128)(2,1)S(1)}, u32[]{:S(2)}, u32[]{:S(2)}) %collective-permute-start.4) | collective-permute-done | bytes 589856 | tf_op jit(solution)/shard_map/ppermute | solution.py:345
  68.4 4.7 %slopes.2 = (bf16[8,32,384]{2,1,0:T(8,128)(2,1)}, bf16[8,32,384]{2,1,0:T(8,128)(2,1)}, bf16[8,32,384]{2,1,0:T(8,128)(2,1)}, bf16[8,32,384]{2,1,0:T(8,128)(2,1)},...) custom-call(bf16[512,512]{1,0:T(8,128)(2,1)} %copy-done.12, ...), custom_call_target="tpu_custom_call" | custom-call | flops 1 | bytes 1 | tf_op jit(solution)/shard_map/slopes/pallas_call | solution.py:130
  73.2 3.6 %collective-permute-done.8.refs_1_ = bf16[16,32,384]{2,1,0:T(8,128)(2,1)S(1)} collective-permute-done((bf16[16,32,384]{2,1,0:T(8,128)(2,1)}, bf16[16,32,384]{2,1,0:T(8,128)(2,1)S(1)}, u32[]{:S(2)}, u32[]{:S(2)}) %collective-permute-start.8) | collective-permute-done | bytes 393248 | tf_op jit(solution)/shard_map/ppermute | solution.py:345
  76.8 8.5 %collective-permute-done.10.refs_2_ = bf16[16,32,384]{2,1,0:T(8,128)(2,1)} collective-permute-done((bf16[16,32,384]{2,1,0:T(8,128)(2,1)}, bf16[16,32,384]{2,1,0:T(8,128)(2,1)}, u32[]{:S(2)}, u32[]{:S(2)}) %collective-permute-start.10) | collective-permute-done | bytes 393248 | tf_op jit(solution)/shard_map/ppermute | solution.py:345
  86.5 4.3 %collective-permute-start.14 = (bf16[16,32,384]{2,1,0:T(8,128)(2,1)}, bf16[16,32,384]{2,1,0:T(8,128)(2,1)S(1)}, u32[]{:S(2)}, u32[]{:S(2)}) collective-permute-start(bf16[16,32,384]{2,1,0:T(8,128)(2,1)} %get-tuple-element.135), channel_id=1, source_target_pairs={{0,7},{1,6},{2,5},{3,4},{4,3},{5,2},{6,1},{7,0},{8,15},{9,14},{10,... | collective-permute-start | bytes 1179656 | tf_op jit(solution)/shard_map/ppermute | solution.py:345
  90.8 6.9 %collective-permute-done.11.refs_2_.far_ref = bf16[14,32,384]{2,1,0:T(8,128)(2,1)S(1)} collective-permute-done((bf16[14,32,384]{2,1,0:T(8,128)(2,1)}, bf16[14,32,384]{2,1,0:T(8,128)(2,1)S(1)}, u32[]{:S(2)}, u32[]{:S(2)}) %collective-permute-start.11) | collective-permute-done | bytes 344096 | tf_op jit(solution)/shard_map/ppermute | solution.py:345
  97.7 4.1 %collective-permute-start.15 = (bf16[8,32,384]{2,1,0:T(8,128)(2,1)}, bf16[8,32,384]{2,1,0:T(8,128)(2,1)S(1)}, u32[]{:S(2)}, u32[]{:S(2)}) collective-permute-start(bf16[8,32,384]{2,1,0:T(8,128)(2,1)} %get-tuple-element.137), channel_id=1, source_target_pairs={{0,5},{1,4},{2,7},{3,6},{4,1},{5,0},{6,3},{7,2},{8,13},{9,12},{10,... | collective-permute-start | bytes 589832 | tf_op jit(solution)/shard_map/ppermute | solution.py:345
  101.8 15.0 %collective-permute-done.9.refs_1_.far_ref = bf16[14,32,384]{2,1,0:T(8,128)(2,1)S(1)} collective-permute-done((bf16[14,32,384]{2,1,0:T(8,128)(2,1)}, bf16[14,32,384]{2,1,0:T(8,128)(2,1)S(1)}, u32[]{:S(2)}, u32[]{:S(2)}) %collective-permute-start.9) | collective-permute-done | bytes 344096 | tf_op jit(solution)/shard_map/ppermute | solution.py:345
  124.1 6.2 %slopes.3 = (bf16[16,32,384]{2,1,0:T(8,128)(2,1)}, bf16[16,32,384]{2,1,0:T(8,128)(2,1)}, bf16[16,32,384]{2,1,0:T(8,128)(2,1)}, bf16[16,32,384]{2,1,0:T(8,128)(2,...) custom-call(bf16[512,512]{1,0:T(8,128)(2,1)} %copy-done.12, ...), custom_call_target="tpu_custom_call" | custom-call | flops 1 | bytes 1 | tf_op jit(solution)/shard_map/slopes/pallas_call | solution.py:130
  130.4 11.9 %collective-permute-done.15.far_ref = bf16[8,32,384]{2,1,0:T(8,128)(2,1)S(1)} collective-permute-done((bf16[8,32,384]{2,1,0:T(8,128)(2,1)}, bf16[8,32,384]{2,1,0:T(8,128)(2,1)S(1)}, u32[]{:S(2)}, u32[]{:S(2)}) %collective-permute-start.15) | collective-permute-done | bytes 196640 | tf_op jit(solution)/shard_map/ppermute | solution.py:345
  143.0 4.8 %collective-permute-start.23 = (bf16[16,32,384]{2,1,0:T(8,128)(2,1)}, bf16[16,32,384]{2,1,0:T(8,128)(2,1)S(1)}, u32[]{:S(2)}, u32[]{:S(2)}) collective-permute-start(bf16[16,32,384]{2,1,0:T(8,128)(2,1)} %get-tuple-element.161), channel_id=1, source_target_pairs={{0,4},{1,5},{2,6},{3,7},{4,0},{5,1},{6,2},{7,3},{8,12},{9,13},{10,... | collective-permute-start | bytes 1179656 | tf_op jit(solution)/shard_map/ppermute | solution.py:345
  157.6 3.4 %bases.3.refs_0_.base_ref = f32[64,1,8,1536]{3,2,1,0:T(8,128)S(1)} custom-call(bf16[64,3,8,1536]{3,2,1,0:T(8,128)(2,1)S(1)} %bitcast.21, bf16[64,3,8,1536]{3,2,1,0:T(8,128)(2,1)S(1)} %bitcast.22, bf16[1536,1536]{1,0:T(8,128)(2,1)S(1)} %copy-done.1, f32[1,1536]{1,0:T(1,128)S(1)} %broadcast_in_dim.55.m_ref, bf16[3,64,8,256]{3,2,1,0:T(8,128)(2,1)S(1)} %refine.1.f_ref, ...), custom_call_target="tpu_custom_call" | custom-call | flops 1 | bytes 1 | tf_op jit(solution)/shard_map/bases/pallas_call | solution.py:253
  161.1 7.3 %bases.2.refs_1_.base_ref = f32[64,2,8,1536]{3,2,1,0:T(8,128)S(1)} custom-call(bf16[64,3,8,1536]{3,2,1,0:T(8,128)(2,1)S(1)} %bitcast.23, bf16[64,3,8,1536]{3,2,1,0:T(8,128)(2,1)S(1)} %bitcast.24, bf16[1536,1536]{1,0:T(8,128)(2,1)S(1)} %copy-done.1, f32[1,1536]{1,0:T(1,128)S(1)} %broadcast_in_dim.55.m_ref, bf16[3,64,8,256]{3,2,1,0:T(8,128)(2,1)S(1)} %refine.1.f_ref, ...), custom_call_target="tpu_custom_call" | custom-call | flops 1 | bytes 1 | tf_op jit(solution)/shard_map/bases/pallas_call | solution.py:253
  172.3 12.0 %collective-permute-start.22 = (bf16[16,32,384]{2,1,0:T(8,128)(2,1)S(1)}, bf16[16,32,384]{2,1,0:T(8,128)(2,1)S(1)}, u32[]{:S(2)}, u32[]{:S(2)}) collective-permute-start(bf16[16,32,384]{2,1,0:T(8,128)(2,1)S(1)} %hold.3), channel_id=1, source_target_pairs={{0,3},{1,2},{2,1},{3,0},{4,7},{5,6},{6,5},{7,4},{8,11},{9,10},{10,... | collective-permute-start | bytes 1179656 | tf_op jit(solution)/shard_map/ppermute | solution.py:345
  186.4 14.9 %collective-permute-done.24.far_ref = bf16[16,32,384]{2,1,0:T(8,128)(2,1)S(1)} collective-permute-done((bf16[16,32,384]{2,1,0:T(8,128)(2,1)}, bf16[16,32,384]{2,1,0:T(8,128)(2,1)S(1)}, u32[]{:S(2)}, u32[]{:S(2)}) %collective-permute-start.24) | collective-permute-done | bytes 393248 | tf_op jit(solution)/shard_map/ppermute | solution.py:345
  201.3 3.7 %collective-permute-start.19 = (bf16[16,32,384]{2,1,0:T(8,128)(2,1)S(1)}, bf16[16,32,384]{2,1,0:T(8,128)(2,1)S(1)}, u32[]{:S(2)}, u32[]{:S(2)}) collective-permute-start(bf16[16,32,384]{2,1,0:T(8,128)(2,1)S(1)} %hold.2), channel_id=1, source_target_pairs={{0,7},{1,6},{2,5},{3,4},{4,3},{5,2},{6,1},{7,0},{8,15},{9,14},{10,... | collective-permute-start | bytes 1179656 | tf_op jit(solution)/shard_map/ppermute | solution.py:345
  (149 shorter events, 59.8 us)
Async XLA Ops:
  3.8 29.5 %collective-permute-start = (bf16[8,32,384]{2,1,0:T(8,128)(2,1)}, bf16[8,32,384]{2,1,0:T(8,128)(2,1)S(1)}, u32[]{:S(2)}, u32[]{:S(2)}) collective-permute-start(bf16[8,32,384]{2,1,0:T(8,128)(2,1)} %get-tuple-element.113), channel_id=1, source_target_pairs={{0,5},{1,4},{2,7},{3,6},{4,1},{5,0},{6,3},{7,2},{8,13},{9,12},{10,... | collective-permute-start | bytes 589832 | tf_op jit(solution)/shard_map/ppermute | solution.py:345
  10.6 39.1 %collective-permute-start.1 = (bf16[11,32,384]{2,1,0:T(8,128)(2,1)}, bf16[11,32,384]{2,1,0:T(8,128)(2,1)S(1)}, u32[]{:S(2)}, u32[]{:S(2)}) collective-permute-start(bf16[11,32,384]{2,1,0:T(8,128)(2,1)} %pad_maximum_fusion), channel_id=1, source_target_pairs={{0,4},{1,5},{2,6},{3,7},{4,0},{5,1},{6,2},{7,3},{8,12},{9,13},{10,... | collective-permute-start | bytes 811016 | tf_op jit(solution)/shard_map/ppermute | solution.py:345
  16.8 16.5 %collective-permute-start.2 = (bf16[8,32,384]{2,1,0:T(8,128)(2,1)}, bf16[8,32,384]{2,1,0:T(8,128)(2,1)}, u32[]{:S(2)}, u32[]{:S(2)}) collective-permute-start(bf16[8,32,384]{2,1,0:T(8,128)(2,1)} %get-tuple-element.115.refs_0_), channel_id=1, source_target_pairs={{0,6},{1,7},{2,4},{3,5},{4,2},{5,3},{6,0},{7,1},{8,14},{9,15},{10,... | collective-permute-start | bytes 589832 | tf_op jit(solution)/shard_map/ppermute | solution.py:345
  21.7 39.2 %collective-permute-start.5 = (bf16[24,32,384]{2,1,0:T(8,128)(2,1)}, bf16[24,32,384]{2,1,0:T(8,128)(2,1)S(1)}, u32[]{:S(2)}, u32[]{:S(2)}) collective-permute-start(bf16[24,32,384]{2,1,0:T(8,128)(2,1)} %get-tuple-element.118), channel_id=1, source_target_pairs={{0,3},{1,2},{2,1},{3,0},{4,7},{5,6},{6,5},{7,4},{8,11},{9,10},{10,... | collective-permute-start | bytes 1769480 | tf_op jit(solution)/shard_map/ppermute | solution.py:345
  33.2 34.4 %collective-permute-start.4 = (bf16[24,32,384]{2,1,0:T(8,128)(2,1)S(1)}, bf16[24,32,384]{2,1,0:T(8,128)(2,1)S(1)}, u32[]{:S(2)}, u32[]{:S(2)}) collective-permute-start(bf16[24,32,384]{2,1,0:T(8,128)(2,1)S(1)} %copy-done.17), channel_id=1, source_target_pairs={{0,2},{1,3},{2,0},{3,1},{4,6},{5,7},{6,4},{7,5},{8,10},{9,11},{10,... | collective-permute-start | bytes 1769480 | tf_op jit(solution)/shard_map/ppermute | solution.py:345
  33.3 27.6 %collective-permute-start.6 = (bf16[24,32,384]{2,1,0:T(8,128)(2,1)}, bf16[24,32,384]{2,1,0:T(8,128)(2,1)S(1)}, u32[]{:S(2)}, u32[]{:S(2)}) collective-permute-start(bf16[24,32,384]{2,1,0:T(8,128)(2,1)} %get-tuple-element.120), channel_id=1, source_target_pairs={{0,1},{1,0},{2,3},{3,2},{4,5},{5,4},{6,7},{7,6},{8,9},{9,8},{10,11... | collective-permute-start | bytes 1769480 | tf_op jit(solution)/shard_map/ppermute | solution.py:345
  35.1 41.6 %collective-permute-start.8 = (bf16[16,32,384]{2,1,0:T(8,128)(2,1)}, bf16[16,32,384]{2,1,0:T(8,128)(2,1)S(1)}, u32[]{:S(2)}, u32[]{:S(2)}) collective-permute-start(bf16[16,32,384]{2,1,0:T(8,128)(2,1)} %get-tuple-element.119.refs_0_), channel_id=1, source_target_pairs={{0,4},{1,5},{2,6},{3,7},{4,0},{5,1},{6,2},{7,3},{8,12},{9,13},{10,... | collective-permute-start | bytes 1179656 | tf_op jit(solution)/shard_map/ppermute | solution.py:345
  49.7 35.6 %collective-permute-start.10 = (bf16[16,32,384]{2,1,0:T(8,128)(2,1)}, bf16[16,32,384]{2,1,0:T(8,128)(2,1)}, u32[]{:S(2)}, u32[]{:S(2)}) collective-permute-start(bf16[16,32,384]{2,1,0:T(8,128)(2,1)} %get-tuple-element.122), channel_id=1, source_target_pairs={{0,5},{1,4},{2,7},{3,6},{4,1},{5,0},{6,3},{7,2},{8,13},{9,12},{10,... | collective-permute-start | bytes 1179656 | tf_op jit(solution)/shard_map/ppermute | solution.py:345
  73.1 43.6 %collective-permute-start.7 = (bf16[14,32,384]{2,1,0:T(8,128)(2,1)}, bf16[14,32,384]{2,1,0:T(8,128)(2,1)S(1)}, u32[]{:S(2)}, u32[]{:S(2)}) collective-permute-start(bf16[14,32,384]{2,1,0:T(8,128)(2,1)} %get-tuple-element.141), channel_id=1, source_target_pairs={{0,2},{1,3},{2,0},{3,1},{4,6},{5,7},{6,4},{7,5},{8,10},{9,11},{10,... | collective-permute-start | bytes 1032200 | tf_op jit(solution)/shard_map/ppermute | solution.py:345
  76.8 40.0 %collective-permute-start.9 = (bf16[14,32,384]{2,1,0:T(8,128)(2,1)}, bf16[14,32,384]{2,1,0:T(8,128)(2,1)S(1)}, u32[]{:S(2)}, u32[]{:S(2)}) collective-permute-start(bf16[14,32,384]{2,1,0:T(8,128)(2,1)} %get-tuple-element.147), channel_id=1, source_target_pairs={{0,3},{1,2},{2,1},{3,0},{4,7},{5,6},{6,5},{7,4},{8,11},{9,10},{10,... | collective-permute-start | bytes 1032200 | tf_op jit(solution)/shard_map/ppermute | solution.py:345
  86.2 33.9 %collective-permute-start.13 = (bf16[16,32,384]{2,1,0:T(8,128)(2,1)}, bf16[16,32,384]{2,1,0:T(8,128)(2,1)S(1)}, u32[]{:S(2)}, u32[]{:S(2)}) collective-permute-start(bf16[16,32,384]{2,1,0:T(8,128)(2,1)} %get-tuple-element.129), channel_id=1, source_target_pairs={{0,6},{1,7},{2,4},{3,5},{4,2},{5,3},{6,0},{7,1},{8,14},{9,15},{10,... | collective-permute-start | bytes 1179656 | tf_op jit(solution)/shard_map/ppermute | solution.py:345
  86.5 34.9 %collective-permute-start.14 = (bf16[16,32,384]{2,1,0:T(8,128)(2,1)}, bf16[16,32,384]{2,1,0:T(8,128)(2,1)S(1)}, u32[]{:S(2)}, u32[]{:S(2)}) collective-permute-start(bf16[16,32,384]{2,1,0:T(8,128)(2,1)} %get-tuple-element.135), channel_id=1, source_target_pairs={{0,7},{1,6},{2,5},{3,4},{4,3},{5,2},{6,1},{7,0},{8,15},{9,14},{10,... | collective-permute-start | bytes 1179656 | tf_op jit(solution)/shard_map/ppermute | solution.py:345
  97.7 44.6 %collective-permute-start.15 = (bf16[8,32,384]{2,1,0:T(8,128)(2,1)}, bf16[8,32,384]{2,1,0:T(8,128)(2,1)S(1)}, u32[]{:S(2)}, u32[]{:S(2)}) collective-permute-start(bf16[8,32,384]{2,1,0:T(8,128)(2,1)} %get-tuple-element.137), channel_id=1, source_target_pairs={{0,5},{1,4},{2,7},{3,6},{4,1},{5,0},{6,3},{7,2},{8,13},{9,12},{10,... | collective-permute-start | bytes 589832 | tf_op jit(solution)/shard_map/ppermute | solution.py:345
  116.7 31.0 %collective-permute-start.16 = (bf16[8,32,384]{2,1,0:T(8,128)(2,1)}, bf16[8,32,384]{2,1,0:T(8,128)(2,1)S(1)}, u32[]{:S(2)}, u32[]{:S(2)}) collective-permute-start(bf16[8,32,384]{2,1,0:T(8,128)(2,1)} %get-tuple-element.139), channel_id=1, source_target_pairs={{0,4},{1,5},{2,6},{3,7},{4,0},{5,1},{6,2},{7,3},{8,12},{9,13},{10,... | collective-permute-start | bytes 589832 | tf_op jit(solution)/shard_map/ppermute | solution.py:345
  118.5 30.7 %collective-permute-start.12 = (bf16[3,64,256]{2,1,0:T(8,128)(2,1)S(1)}, bf16[3,64,256]{2,1,0:T(8,128)(2,1)S(1)}, u32[]{:S(2)}, u32[]{:S(2)}) collective-permute-start(bf16[3,64,256]{2,1,0:T(8,128)(2,1)S(1)} %get-tuple-element.152), channel_id=1, source_target_pairs={{8,0},{16,8},{24,16},{9,1},{17,9},{25,17},{10,2},{18,10},{26,18},{... | collective-permute-start | bytes 294920 | tf_op jit(solution)/shard_map/ppermute | solution.py:415
  120.1 52.3 %collective-permute-start.18 = (bf16[8,32,384]{2,1,0:T(8,128)(2,1)}, bf16[8,32,384]{2,1,0:T(8,128)(2,1)}, u32[]{:S(2)}, u32[]{:S(2)}) collective-permute-start(bf16[8,32,384]{2,1,0:T(8,128)(2,1)} %get-tuple-element.145), channel_id=1, source_target_pairs={{0,6},{1,7},{2,4},{3,5},{4,2},{5,3},{6,0},{7,1},{8,14},{9,15},{10,... | collective-permute-start | bytes 589832 | tf_op jit(solution)/shard_map/ppermute | solution.py:345
  121.4 62.9 %collective-permute-start.25 = (bf16[8,32,384]{2,1,0:T(8,128)(2,1)}, bf16[8,32,384]{2,1,0:T(8,128)(2,1)}, u32[]{:S(2)}, u32[]{:S(2)}) collective-permute-start(bf16[8,32,384]{2,1,0:T(8,128)(2,1)} %get-tuple-element.159), channel_id=1, source_target_pairs={{0,7},{1,6},{2,5},{3,4},{4,3},{5,2},{6,1},{7,0},{8,15},{9,14},{10,... | collective-permute-start | bytes 589832 | tf_op jit(solution)/shard_map/ppermute | solution.py:345
  143.0 42.8 %collective-permute-start.23 = (bf16[16,32,384]{2,1,0:T(8,128)(2,1)}, bf16[16,32,384]{2,1,0:T(8,128)(2,1)S(1)}, u32[]{:S(2)}, u32[]{:S(2)}) collective-permute-start(bf16[16,32,384]{2,1,0:T(8,128)(2,1)} %get-tuple-element.161), channel_id=1, source_target_pairs={{0,4},{1,5},{2,6},{3,7},{4,0},{5,1},{6,2},{7,3},{8,12},{9,13},{10,... | collective-permute-start | bytes 1179656 | tf_op jit(solution)/shard_map/ppermute | solution.py:345
  148.5 52.9 %collective-permute-start.24 = (bf16[16,32,384]{2,1,0:T(8,128)(2,1)}, bf16[16,32,384]{2,1,0:T(8,128)(2,1)S(1)}, u32[]{:S(2)}, u32[]{:S(2)}) collective-permute-start(bf16[16,32,384]{2,1,0:T(8,128)(2,1)} %get-tuple-element.163), channel_id=1, source_target_pairs={{0,5},{1,4},{2,7},{3,6},{4,1},{5,0},{6,3},{7,2},{8,13},{9,12},{10,... | collective-permute-start | bytes 1179656 | tf_op jit(solution)/shard_map/ppermute | solution.py:345
  149.2 60.5 %collective-permute-start.21 = (bf16[16,32,384]{2,1,0:T(8,128)(2,1)}, bf16[16,32,384]{2,1,0:T(8,128)(2,1)S(1)}, u32[]{:S(2)}, u32[]{:S(2)}) collective-permute-start(bf16[16,32,384]{2,1,0:T(8,128)(2,1)} %get-tuple-element.165), channel_id=1, source_target_pairs={{0,2},{1,3},{2,0},{3,1},{4,6},{5,7},{6,4},{7,5},{8,10},{9,11},{10,... | collective-permute-start | bytes 1179656 | tf_op jit(solution)/shard_map/ppermute | solution.py:345
  172.3 40.3 %collective-permute-start.22 = (bf16[16,32,384]{2,1,0:T(8,128)(2,1)S(1)}, bf16[16,32,384]{2,1,0:T(8,128)(2,1)S(1)}, u32[]{:S(2)}, u32[]{:S(2)}) collective-permute-start(bf16[16,32,384]{2,1,0:T(8,128)(2,1)S(1)} %hold.3), channel_id=1, source_target_pairs={{0,3},{1,2},{2,1},{3,0},{4,7},{5,6},{6,5},{7,4},{8,11},{9,10},{10,... | collective-permute-start | bytes 1179656 | tf_op jit(solution)/shard_map/ppermute | solution.py:345
  184.3 31.2 %collective-permute-start.20 = (bf16[16,32,384]{2,1,0:T(8,128)(2,1)S(1)}, bf16[16,32,384]{2,1,0:T(8,128)(2,1)S(1)}, u32[]{:S(2)}, u32[]{:S(2)}) collective-permute-start(bf16[16,32,384]{2,1,0:T(8,128)(2,1)S(1)} %copy-done.29), channel_id=1, source_target_pairs={{0,1},{1,0},{2,3},{3,2},{4,5},{5,4},{6,7},{7,6},{8,9},{9,8},{10,11... | collective-permute-start | bytes 1179656 | tf_op jit(solution)/shard_map/ppermute | solution.py:345
  185.8 32.7 %collective-permute-start.17 = (bf16[16,32,384]{2,1,0:T(8,128)(2,1)S(1)}, bf16[16,32,384]{2,1,0:T(8,128)(2,1)S(1)}, u32[]{:S(2)}, u32[]{:S(2)}) collective-permute-start(bf16[16,32,384]{2,1,0:T(8,128)(2,1)S(1)} %copy-done.28), channel_id=1, source_target_pairs={{0,6},{1,7},{2,4},{3,5},{4,2},{5,3},{6,0},{7,1},{8,14},{9,15},{10,... | collective-permute-start | bytes 1179656 | tf_op jit(solution)/shard_map/ppermute | solution.py:345
  201.3 17.1 %collective-permute-start.19 = (bf16[16,32,384]{2,1,0:T(8,128)(2,1)S(1)}, bf16[16,32,384]{2,1,0:T(8,128)(2,1)S(1)}, u32[]{:S(2)}, u32[]{:S(2)}) collective-permute-start(bf16[16,32,384]{2,1,0:T(8,128)(2,1)S(1)} %hold.2), channel_id=1, source_target_pairs={{0,7},{1,6},{2,5},{3,4},{4,3},{5,2},{6,1},{7,0},{8,15},{9,14},{10,... | collective-permute-start | bytes 1179656 | tf_op jit(solution)/shard_map/ppermute | solution.py:345
  (34 other events, 487.5 us)

commit v5 on v4

--- a/solution.py
+++ b/solution.py
@@ -349,18 +349,16 @@
     row_size = coarse_levels * components * coarse_width
     every = tuple(range(components))
     chunks = one, two = [every[2:], every[:2]]
+    coarse = jnp.transpose(coarse_force, (0, 2, 1, 3))
+    across = lax.ppermute(coarse, "row", [(i, i ^ 4) for i in range(devices)])
+    planes = lambda a: a.reshape(coarse_here, row_size).reshape(-1, rows // 2, width)
     blocks, after = {}, ()
     for which, s in ((one, 2), (every, 1), (one, 3), (every, 0), (two, 2), (two, 3)):
         pair = pack(v, which, s, prefetch, after)
         blocks[which, 2 * s], blocks[which, 2 * s + 1] = pair
         after = pair[:1]
     landed = {(every, 0): blocks[every, 0]}
-    rider = (
-        jnp.transpose(coarse_force, (0, 2, 1, 3))
-        .reshape(coarse_here, row_size)
-        .reshape(-1, rows // 2, width)
-    )
-    blocks[one, 4] = jnp.concatenate([blocks[one, 4], rider], axis=0)
+    blocks[one, 7], across = lax.optimization_barrier((blocks[one, 7], across))
     steps = [
         (one, 5), (one, 4), (one, 6), (every, 2), (one, 7), (every, 3), (two, 4), (every, 1),
         (two, 5), (two, 6), (two, 7),
@@ -377,7 +375,7 @@
         if step == (every, 2):
             block, deriv, metric = lax.optimization_barrier((block, deriv, metric))
         numbers[step] = trade(block, step[1])
-    rider = jnp.concatenate([rider, moved[numbers[one, 4]][-rider.shape[0] :]], axis=0)
+    rider = jnp.concatenate([planes(coarse), planes(across)], axis=0)
 
     def derivatives(chunk, *carried):
         names = [(every if k < 4 else chunk, k) for k in arrival]
@@ -392,7 +390,7 @@
     sent = {0: derivatives(one, rider, [place[k] for k in (2, 3, 1)])}
     sent[1] = derivatives(two)
     back = {0: {0: sent[0][0]}, 1: {0: sent[1][0]}}
-    for at, k in ((0, 5), (0, 4), (0, 2), (0, 6), (0, 3), (0, 1), (0, 7), (1, 4), (1, 5)):
+    for at, k in ((0, 5), (0, 2), (0, 4), (0, 3), (0, 6), (0, 1), (0, 7), (1, 5), (1, 4)):
         back[at][k] = trade(sent[at][place[k]], k)
 
     holders = jnp.stack([me ^ k for k in (0, 4, 2, 6, 3, 7, 1, 5)])

time: 223 us -> 222 us (level)
  waiting for transfers between devices: 77.3 us -> 95.2 us
  starting transfers between devices: 68.2 us -> 51.2 us
  other arithmetic: 3.73 us -> 1.43 us
    ppermute x25, starting transfers between devices: 66.7 us -> 45.6 us  [trade(): lax.ppermute(block, 'row', [(i, i ^ k) for i in range(devices)])]
    ppermute x25, waiting for transfers between devices: 77.3 us -> 95.2 us  [trade(): lax.ppermute(block, 'row', [(i, i ^ k) for i in range(devices)])]
    ppermute x0 -> x1, starting transfers between devices: none -> 4.1 us  [ring_shards(): across = lax.ppermute(coarse, 'row', [(i, i ^ 4) for i in range(devices)])]
    concatenate x2 -> x0, other arithmetic: 2.37 us -> none  [the longest x1 1.68 us: ring_shards(): blocks[one, 4] = jnp.concatenate([blocks[one, 4], rider], axis=0)]
    unnamed x69 -> x72, local copies, waits for them, and re-layouts: 7.94 us -> 8.63 us
  transfers between devices with their start and end apart: 27 -> 28, of which waited for: 9 -> 12; matrix products, arithmetic and copies ran while one was open for 2% -> 2% of each run, Pallas kernels for 25% -> 26%
where the time goes in v5:
time: 222 us; the launch traced here: 221 us
  waiting for transfers between devices  95.2 us (43%)
  Pallas kernels  60.8 us (27%)
  starting transfers between devices  51.2 us (23%)
  local copies, waits for them, and re-layouts  11 us (5%)
    ppermute x25, waiting for transfers between devices, trade(): lax.ppermute(block, 'row', [(i, i ^ k) for i in range(devices)])  95.2 us
    ppermute x25, starting transfers between devices, trade(): lax.ppermute(block, 'row', [(i, i ^ k) for i in range(devices)])  45.6 us
    pallas_call x8, Pallas kernels, combine(): pl.pallas_call(combine_kernel, grid_spec=pltpu.PrefetchScalarGridSpec(num...  20.1 us
    pallas_call x6, Pallas kernels, pack(): pl.pallas_call(pack_kernel, grid_spec=pltpu.PrefetchScalarGridSpec(num_sc...  17.6 us
    pallas_call x2, Pallas kernels, slopes(): pl.pallas_call(functools.partial(slope_kernel, planes, places, riders), i...  10.9 us
    pallas_call x2, Pallas kernels, bases(): pl.pallas_call(base_kernel, grid=(rows // part, len(comps)), in_specs=[pl...  10.8 us
    unnamed x72, local copies, waits for them, and re-layouts  8.63 us
  transfers between devices with their start and end apart: 28, of which 12 were waited for; matrix products, arithmetic and copies ran while one was open for 2% of the time, Pallas kernels for 26%

profile of v5, /device:TPU:0, one launch (start us, length us, event | category | flops | bytes accessed | tf_op | source)
XLA Modules:
  0.0 220.8 jit_solution(13732122601260576216)
XLA Ops:
  0.6 4.1 %collective-permute-start = (bf16[16,3,4,192]{3,2,1,0:T(4,128)(2,1)}, bf16[16,3,4,192]{3,2,1,0:T(4,128)(2,1)S(1)}, u32[]{:S(2)}, u32[]{:S(2)}) collective-permute-start(bf16[16,3,4,192]{3,2,1,0:T(4,128)(2,1)} %bitcast.43), channel_id=1, source_target_pairs={{0,4},{1,5},{2,6},{3,7},{4,0},{5,1},{6,2},{7,3},{8,12},{9,13},{10,... | collective-permute-start | bytes 221192 | tf_op jit(solution)/shard_map/ppermute | solution.py:353
  11.8 3.2 %pack.7 = (bf16[24,32,384]{2,1,0:T(8,128)(2,1)}, bf16[24,32,384]{2,1,0:T(8,128)(2,1)}) custom-call(s32[5]{0:T(128)} %pad_add_fusion.xi_ref, bf16[64,3,8,1536]{3,2,1,0:T(8,128)(2,1)} %bitcast.16, bf16[8,32,384]{2,1,0:T(8,128)(2,1)} %get-tuple-element.105.refs_0_), custom_call_target="tpu_custom_call" | custom-call | flops 1 | bytes 1 | tf_op jit(solution)/shard_map/pack/pallas_call | solution.py:80
  20.5 3.2 %pack.9 = (bf16[24,32,384]{2,1,0:T(8,128)(2,1)}, bf16[24,32,384]{2,1,0:T(8,128)(2,1)}) custom-call(s32[5]{0:T(128)} %pad_add_fusion.xi_ref, bf16[64,3,8,1536]{3,2,1,0:T(8,128)(2,1)} %bitcast.18, bf16[8,32,384]{2,1,0:T(8,128)(2,1)} %get-tuple-element.120.refs_0_), custom_call_target="tpu_custom_call" | custom-call | flops 1 | bytes 1 | tf_op jit(solution)/shard_map/pack/pallas_call | solution.py:80
  35.0 3.3 %collective-permute-start.9 = (bf16[16,32,384]{2,1,0:T(8,128)(2,1)}, bf16[16,32,384]{2,1,0:T(8,128)(2,1)S(1)}, u32[]{:S(2)}, u32[]{:S(2)}) collective-permute-start(bf16[16,32,384]{2,1,0:T(8,128)(2,1)} %get-tuple-element.124.refs_0_), channel_id=1, source_target_pairs={{0,4},{1,5},{2,6},{3,7},{4,0},{5,1},{6,2},{7,3},{8,12},{9,13},{10,... | collective-permute-start | bytes 1179656 | tf_op jit(solution)/shard_map/ppermute | solution.py:345
  38.3 21.9 %collective-permute-done.4.refs_4_ = bf16[8,32,384]{2,1,0:T(8,128)(2,1)S(1)} collective-permute-done((bf16[8,32,384]{2,1,0:T(8,128)(2,1)}, bf16[8,32,384]{2,1,0:T(8,128)(2,1)S(1)}, u32[]{:S(2)}, u32[]{:S(2)}) %collective-permute-start.4) | collective-permute-done | bytes 196640 | tf_op jit(solution)/shard_map/ppermute | solution.py:345
  60.9 3.0 %pack.11 = (bf16[16,32,384]{2,1,0:T(8,128)(2,1)}, bf16[16,32,384]{2,1,0:T(8,128)(2,1)}) custom-call(s32[5]{0:T(128)} %pad_add_fusion.xi_ref, bf16[64,3,8,1536]{3,2,1,0:T(8,128)(2,1)} %bitcast.20, bf16[16,32,384]{2,1,0:T(8,128)(2,1)} %get-tuple-element.124.refs_0_), custom_call_target="tpu_custom_call" | custom-call | flops 1 | bytes 1 | tf_op jit(solution)/shard_map/pack/pallas_call | solution.py:80
  65.3 5.8 %collective-permute-done.6.refs_6_ = bf16[24,32,384]{2,1,0:T(8,128)(2,1)S(1)} collective-permute-done((bf16[24,32,384]{2,1,0:T(8,128)(2,1)}, bf16[24,32,384]{2,1,0:T(8,128)(2,1)S(1)}, u32[]{:S(2)}, u32[]{:S(2)}) %collective-permute-start.6) | collective-permute-done | bytes 589856 | tf_op jit(solution)/shard_map/ppermute | solution.py:345
  72.0 4.7 %slopes.2 = (bf16[8,32,384]{2,1,0:T(8,128)(2,1)}, bf16[8,32,384]{2,1,0:T(8,128)(2,1)}, bf16[8,32,384]{2,1,0:T(8,128)(2,1)}, bf16[8,32,384]{2,1,0:T(8,128)(2,1)},...) custom-call(bf16[512,512]{1,0:T(8,128)(2,1)} %copy-done.13, ...), custom_call_target="tpu_custom_call" | custom-call | flops 1 | bytes 1 | tf_op jit(solution)/shard_map/slopes/pallas_call | solution.py:130
  79.7 4.3 %collective-permute-done.11.refs_2_ = bf16[16,32,384]{2,1,0:T(8,128)(2,1)} collective-permute-done((bf16[16,32,384]{2,1,0:T(8,128)(2,1)}, bf16[16,32,384]{2,1,0:T(8,128)(2,1)}, u32[]{:S(2)}, u32[]{:S(2)}) %collective-permute-start.11) | collective-permute-done | bytes 393248 | tf_op jit(solution)/shard_map/ppermute | solution.py:345
  86.5 3.0 %collective-permute-start.15 = (bf16[16,32,384]{2,1,0:T(8,128)(2,1)}, bf16[16,32,384]{2,1,0:T(8,128)(2,1)S(1)}, u32[]{:S(2)}, u32[]{:S(2)}) collective-permute-start(bf16[16,32,384]{2,1,0:T(8,128)(2,1)} %get-tuple-element.138), channel_id=1, source_target_pairs={{0,7},{1,6},{2,5},{3,4},{4,3},{5,2},{6,1},{7,0},{8,15},{9,14},{10,... | collective-permute-start | bytes 1179656 | tf_op jit(solution)/shard_map/ppermute | solution.py:345
  90.8 7.0 %collective-permute-done.12.refs_2_.far_ref = bf16[14,32,384]{2,1,0:T(8,128)(2,1)S(1)} collective-permute-done((bf16[14,32,384]{2,1,0:T(8,128)(2,1)}, bf16[14,32,384]{2,1,0:T(8,128)(2,1)S(1)}, u32[]{:S(2)}, u32[]{:S(2)}) %collective-permute-start.12) | collective-permute-done | bytes 344096 | tf_op jit(solution)/shard_map/ppermute | solution.py:345
  97.8 4.1 %collective-permute-start.17 = (bf16[8,32,384]{2,1,0:T(8,128)(2,1)}, bf16[8,32,384]{2,1,0:T(8,128)(2,1)S(1)}, u32[]{:S(2)}, u32[]{:S(2)}) collective-permute-start(bf16[8,32,384]{2,1,0:T(8,128)(2,1)} %get-tuple-element.146), channel_id=1, source_target_pairs={{0,4},{1,5},{2,6},{3,7},{4,0},{5,1},{6,2},{7,3},{8,12},{9,13},{10,... | collective-permute-start | bytes 589832 | tf_op jit(solution)/shard_map/ppermute | solution.py:345
  101.9 13.5 %collective-permute-done.10.refs_1_.far_ref = bf16[14,32,384]{2,1,0:T(8,128)(2,1)S(1)} collective-permute-done((bf16[14,32,384]{2,1,0:T(8,128)(2,1)}, bf16[14,32,384]{2,1,0:T(8,128)(2,1)S(1)}, u32[]{:S(2)}, u32[]{:S(2)}) %collective-permute-start.10) | collective-permute-done | bytes 344096 | tf_op jit(solution)/shard_map/ppermute | solution.py:345
  119.7 3.5 %collective-permute-start.26 = (bf16[8,32,384]{2,1,0:T(8,128)(2,1)}, bf16[8,32,384]{2,1,0:T(8,128)(2,1)}, u32[]{:S(2)}, u32[]{:S(2)}) collective-permute-start(bf16[8,32,384]{2,1,0:T(8,128)(2,1)} %get-tuple-element.163), channel_id=1, source_target_pairs={{0,7},{1,6},{2,5},{3,4},{4,3},{5,2},{6,1},{7,0},{8,15},{9,14},{10,... | collective-permute-start | bytes 589832 | tf_op jit(solution)/shard_map/ppermute | solution.py:345
  123.1 6.2 %slopes.3 = (bf16[16,32,384]{2,1,0:T(8,128)(2,1)}, bf16[16,32,384]{2,1,0:T(8,128)(2,1)}, bf16[16,32,384]{2,1,0:T(8,128)(2,1)}, bf16[16,32,384]{2,1,0:T(8,128)(2,...) custom-call(bf16[512,512]{1,0:T(8,128)(2,1)} %copy-done.13, ...), custom_call_target="tpu_custom_call" | custom-call | flops 1 | bytes 1 | tf_op jit(solution)/shard_map/slopes/pallas_call | solution.py:130
  129.4 12.2 %collective-permute-done.16.far_ref = bf16[8,32,384]{2,1,0:T(8,128)(2,1)S(1)} collective-permute-done((bf16[8,32,384]{2,1,0:T(8,128)(2,1)}, bf16[8,32,384]{2,1,0:T(8,128)(2,1)S(1)}, u32[]{:S(2)}, u32[]{:S(2)}) %collective-permute-start.16) | collective-permute-done | bytes 196640 | tf_op jit(solution)/shard_map/ppermute | solution.py:345
  142.3 5.0 %collective-permute-start.25 = (bf16[16,32,384]{2,1,0:T(8,128)(2,1)}, bf16[16,32,384]{2,1,0:T(8,128)(2,1)S(1)}, u32[]{:S(2)}, u32[]{:S(2)}) collective-permute-start(bf16[16,32,384]{2,1,0:T(8,128)(2,1)} %get-tuple-element.165), channel_id=1, source_target_pairs={{0,5},{1,4},{2,7},{3,6},{4,1},{5,0},{6,3},{7,2},{8,13},{9,12},{10,... | collective-permute-start | bytes 1179656 | tf_op jit(solution)/shard_map/ppermute | solution.py:345
  147.9 3.1 %collective-permute-start.22 = (bf16[16,32,384]{2,1,0:T(8,128)(2,1)}, bf16[16,32,384]{2,1,0:T(8,128)(2,1)S(1)}, u32[]{:S(2)}, u32[]{:S(2)}) collective-permute-start(bf16[16,32,384]{2,1,0:T(8,128)(2,1)} %get-tuple-element.169), channel_id=1, source_target_pairs={{0,2},{1,3},{2,0},{3,1},{4,6},{5,7},{6,4},{7,5},{8,10},{9,11},{10,... | collective-permute-start | bytes 1179656 | tf_op jit(solution)/shard_map/ppermute | solution.py:345
  156.6 3.5 %bases.3.refs_0_.base_ref = f32[64,1,8,1536]{3,2,1,0:T(8,128)S(1)} custom-call(bf16[64,3,8,1536]{3,2,1,0:T(8,128)(2,1)S(1)} %bitcast.21, bf16[64,3,8,1536]{3,2,1,0:T(8,128)(2,1)S(1)} %bitcast.22, bf16[1536,1536]{1,0:T(8,128)(2,1)S(1)} %copy-done.1, f32[1,1536]{1,0:T(1,128)S(1)} %broadcast_in_dim.55.m_ref, bf16[3,64,8,256]{3,2,1,0:T(8,128)(2,1)S(1)} %refine.1.f_ref, ...), custom_call_target="tpu_custom_call" | custom-call | flops 1 | bytes 1 | tf_op jit(solution)/shard_map/bases/pallas_call | solution.py:253
  160.1 7.3 %bases.2.refs_1_.base_ref = f32[64,2,8,1536]{3,2,1,0:T(8,128)S(1)} custom-call(bf16[64,3,8,1536]{3,2,1,0:T(8,128)(2,1)S(1)} %bitcast.23, bf16[64,3,8,1536]{3,2,1,0:T(8,128)(2,1)S(1)} %bitcast.24, bf16[1536,1536]{1,0:T(8,128)(2,1)S(1)} %copy-done.1, f32[1,1536]{1,0:T(1,128)S(1)} %broadcast_in_dim.55.m_ref, bf16[3,64,8,256]{3,2,1,0:T(8,128)(2,1)S(1)} %refine.1.f_ref, ...), custom_call_target="tpu_custom_call" | custom-call | flops 1 | bytes 1 | tf_op jit(solution)/shard_map/bases/pallas_call | solution.py:253
  173.0 6.7 %collective-permute-done.25.far_ref = bf16[16,32,384]{2,1,0:T(8,128)(2,1)S(1)} collective-permute-done((bf16[16,32,384]{2,1,0:T(8,128)(2,1)}, bf16[16,32,384]{2,1,0:T(8,128)(2,1)S(1)}, u32[]{:S(2)}, u32[]{:S(2)}) %collective-permute-start.25) | collective-permute-done | bytes 393248 | tf_op jit(solution)/shard_map/ppermute | solution.py:345
  182.3 13.3 %collective-permute-done.24.near_ref = bf16[16,32,384]{2,1,0:T(8,128)(2,1)S(1)} collective-permute-done((bf16[16,32,384]{2,1,0:T(8,128)(2,1)}, bf16[16,32,384]{2,1,0:T(8,128)(2,1)S(1)}, u32[]{:S(2)}, u32[]{:S(2)}) %collective-permute-start.24) | collective-permute-done | bytes 393248 | tf_op jit(solution)/shard_map/ppermute | solution.py:345
  195.6 3.4 %collective-permute-start.19 = (bf16[16,32,384]{2,1,0:T(8,128)(2,1)S(1)}, bf16[16,32,384]{2,1,0:T(8,128)(2,1)S(1)}, u32[]{:S(2)}, u32[]{:S(2)}) collective-permute-start(bf16[16,32,384]{2,1,0:T(8,128)(2,1)S(1)} %hold.2), channel_id=1, source_target_pairs={{0,7},{1,6},{2,5},{3,4},{4,3},{5,2},{6,1},{7,0},{8,15},{9,14},{10,... | collective-permute-start | bytes 1179656 | tf_op jit(solution)/shard_map/ppermute | solution.py:345
  206.7 5.4 %collective-permute-done.23.far_ref = bf16[16,32,384]{2,1,0:T(8,128)(2,1)S(1)} collective-permute-done((bf16[16,32,384]{2,1,0:T(8,128)(2,1)S(1)}, bf16[16,32,384]{2,1,0:T(8,128)(2,1)S(1)}, u32[]{:S(2)}, u32[]{:S(2)}) %collective-permute-start.23) | collective-permute-done | bytes 393248 | tf_op jit(solution)/shard_map/ppermute | solution.py:345
  (153 shorter events, 68.7 us)
Async XLA Ops:
  0.6 26.4 %collective-permute-start = (bf16[16,3,4,192]{3,2,1,0:T(4,128)(2,1)}, bf16[16,3,4,192]{3,2,1,0:T(4,128)(2,1)S(1)}, u32[]{:S(2)}, u32[]{:S(2)}) collective-permute-start(bf16[16,3,4,192]{3,2,1,0:T(4,128)(2,1)} %bitcast.43), channel_id=1, source_target_pairs={{0,4},{1,5},{2,6},{3,7},{4,0},{5,1},{6,2},{7,3},{8,12},{9,13},{10,... | collective-permute-start | bytes 221192 | tf_op jit(solution)/shard_map/ppermute | solution.py:353
  7.9 22.3 %collective-permute-start.1 = (bf16[8,32,384]{2,1,0:T(8,128)(2,1)}, bf16[8,32,384]{2,1,0:T(8,128)(2,1)S(1)}, u32[]{:S(2)}, u32[]{:S(2)}) collective-permute-start(bf16[8,32,384]{2,1,0:T(8,128)(2,1)} %get-tuple-element.127), channel_id=1, source_target_pairs={{0,5},{1,4},{2,7},{3,6},{4,1},{5,0},{6,3},{7,2},{8,13},{9,12},{10,... | collective-permute-start | bytes 589832 | tf_op jit(solution)/shard_map/ppermute | solution.py:345
  9.2 25.2 %collective-permute-start.2 = (bf16[8,32,384]{2,1,0:T(8,128)(2,1)}, bf16[8,32,384]{2,1,0:T(8,128)(2,1)S(1)}, u32[]{:S(2)}, u32[]{:S(2)}) collective-permute-start(bf16[8,32,384]{2,1,0:T(8,128)(2,1)} %get-tuple-element.105.refs_0_), channel_id=1, source_target_pairs={{0,4},{1,5},{2,6},{3,7},{4,0},{5,1},{6,2},{7,3},{8,12},{9,13},{10,... | collective-permute-start | bytes 589832 | tf_op jit(solution)/shard_map/ppermute | solution.py:345
  20.3 45.0 %collective-permute-start.5 = (bf16[24,32,384]{2,1,0:T(8,128)(2,1)}, bf16[24,32,384]{2,1,0:T(8,128)(2,1)S(1)}, u32[]{:S(2)}, u32[]{:S(2)}) collective-permute-start(bf16[24,32,384]{2,1,0:T(8,128)(2,1)} %get-tuple-element.121.refs_0_), channel_id=1, source_target_pairs={{0,2},{1,3},{2,0},{3,1},{4,6},{5,7},{6,4},{7,5},{8,10},{9,11},{10,... | collective-permute-start | bytes 1769480 | tf_op jit(solution)/shard_map/ppermute | solution.py:345
  27.0 44.1 %collective-permute-start.6 = (bf16[24,32,384]{2,1,0:T(8,128)(2,1)}, bf16[24,32,384]{2,1,0:T(8,128)(2,1)S(1)}, u32[]{:S(2)}, u32[]{:S(2)}) collective-permute-start(bf16[24,32,384]{2,1,0:T(8,128)(2,1)} %get-tuple-element.123), channel_id=1, source_target_pairs={{0,3},{1,2},{2,1},{3,0},{4,7},{5,6},{6,5},{7,4},{8,11},{9,10},{10,... | collective-permute-start | bytes 1769480 | tf_op jit(solution)/shard_map/ppermute | solution.py:345
  30.2 30.0 %collective-permute-start.4 = (bf16[8,32,384]{2,1,0:T(8,128)(2,1)}, bf16[8,32,384]{2,1,0:T(8,128)(2,1)S(1)}, u32[]{:S(2)}, u32[]{:S(2)}) collective-permute-start(bf16[8,32,384]{2,1,0:T(8,128)(2,1)} %get-tuple-element.122), channel_id=1, source_target_pairs={{0,7},{1,6},{2,5},{3,4},{4,3},{5,2},{6,1},{7,0},{8,15},{9,14},{10,... | collective-permute-start | bytes 589832 | tf_op jit(solution)/shard_map/ppermute | solution.py:345
  34.4 30.9 %collective-permute-start.7 = (bf16[24,32,384]{2,1,0:T(8,128)(2,1)}, bf16[24,32,384]{2,1,0:T(8,128)(2,1)S(1)}, u32[]{:S(2)}, u32[]{:S(2)}) collective-permute-start(bf16[24,32,384]{2,1,0:T(8,128)(2,1)} %get-tuple-element.125), channel_id=1, source_target_pairs={{0,1},{1,0},{2,3},{3,2},{4,5},{5,4},{6,7},{7,6},{8,9},{9,8},{10,11... | collective-permute-start | bytes 1769480 | tf_op jit(solution)/shard_map/ppermute | solution.py:345
  35.0 41.8 %collective-permute-start.9 = (bf16[16,32,384]{2,1,0:T(8,128)(2,1)}, bf16[16,32,384]{2,1,0:T(8,128)(2,1)S(1)}, u32[]{:S(2)}, u32[]{:S(2)}) collective-permute-start(bf16[16,32,384]{2,1,0:T(8,128)(2,1)} %get-tuple-element.124.refs_0_), channel_id=1, source_target_pairs={{0,4},{1,5},{2,6},{3,7},{4,0},{5,1},{6,2},{7,3},{8,12},{9,13},{10,... | collective-permute-start | bytes 1179656 | tf_op jit(solution)/shard_map/ppermute | solution.py:345
  60.9 23.1 %collective-permute-start.11 = (bf16[16,32,384]{2,1,0:T(8,128)(2,1)}, bf16[16,32,384]{2,1,0:T(8,128)(2,1)}, u32[]{:S(2)}, u32[]{:S(2)}) collective-permute-start(bf16[16,32,384]{2,1,0:T(8,128)(2,1)} %get-tuple-element.128), channel_id=1, source_target_pairs={{0,5},{1,4},{2,7},{3,6},{4,1},{5,0},{6,3},{7,2},{8,13},{9,12},{10,... | collective-permute-start | bytes 1179656 | tf_op jit(solution)/shard_map/ppermute | solution.py:345
  76.8 38.7 %collective-permute-start.10 = (bf16[14,32,384]{2,1,0:T(8,128)(2,1)}, bf16[14,32,384]{2,1,0:T(8,128)(2,1)S(1)}, u32[]{:S(2)}, u32[]{:S(2)}) collective-permute-start(bf16[14,32,384]{2,1,0:T(8,128)(2,1)} %get-tuple-element.148), channel_id=1, source_target_pairs={{0,3},{1,2},{2,1},{3,0},{4,7},{5,6},{6,5},{7,4},{8,11},{9,10},{10,... | collective-permute-start | bytes 1032200 | tf_op jit(solution)/shard_map/ppermute | solution.py:345
  85.2 33.6 %collective-permute-start.14 = (bf16[16,32,384]{2,1,0:T(8,128)(2,1)}, bf16[16,32,384]{2,1,0:T(8,128)(2,1)S(1)}, u32[]{:S(2)}, u32[]{:S(2)}) collective-permute-start(bf16[16,32,384]{2,1,0:T(8,128)(2,1)} %get-tuple-element.133), channel_id=1, source_target_pairs={{0,6},{1,7},{2,4},{3,5},{4,2},{5,3},{6,0},{7,1},{8,14},{9,15},{10,... | collective-permute-start | bytes 1179656 | tf_op jit(solution)/shard_map/ppermute | solution.py:345
  86.5 33.2 %collective-permute-start.15 = (bf16[16,32,384]{2,1,0:T(8,128)(2,1)}, bf16[16,32,384]{2,1,0:T(8,128)(2,1)S(1)}, u32[]{:S(2)}, u32[]{:S(2)}) collective-permute-start(bf16[16,32,384]{2,1,0:T(8,128)(2,1)} %get-tuple-element.138), channel_id=1, source_target_pairs={{0,7},{1,6},{2,5},{3,4},{4,3},{5,2},{6,1},{7,0},{8,15},{9,14},{10,... | collective-permute-start | bytes 1179656 | tf_op jit(solution)/shard_map/ppermute | solution.py:345
  90.8 50.8 %collective-permute-start.16 = (bf16[8,32,384]{2,1,0:T(8,128)(2,1)}, bf16[8,32,384]{2,1,0:T(8,128)(2,1)S(1)}, u32[]{:S(2)}, u32[]{:S(2)}) collective-permute-start(bf16[8,32,384]{2,1,0:T(8,128)(2,1)} %get-tuple-element.140), channel_id=1, source_target_pairs={{0,5},{1,4},{2,7},{3,6},{4,1},{5,0},{6,3},{7,2},{8,13},{9,12},{10,... | collective-permute-start | bytes 589832 | tf_op jit(solution)/shard_map/ppermute | solution.py:345
  97.8 49.4 %collective-permute-start.17 = (bf16[8,32,384]{2,1,0:T(8,128)(2,1)}, bf16[8,32,384]{2,1,0:T(8,128)(2,1)S(1)}, u32[]{:S(2)}, u32[]{:S(2)}) collective-permute-start(bf16[8,32,384]{2,1,0:T(8,128)(2,1)} %get-tuple-element.146), channel_id=1, source_target_pairs={{0,4},{1,5},{2,6},{3,7},{4,0},{5,1},{6,2},{7,3},{8,12},{9,13},{10,... | collective-permute-start | bytes 589832 | tf_op jit(solution)/shard_map/ppermute | solution.py:345
  117.2 30.7 %collective-permute-start.13 = (bf16[3,64,256]{2,1,0:T(8,128)(2,1)S(1)}, bf16[3,64,256]{2,1,0:T(8,128)(2,1)S(1)}, u32[]{:S(2)}, u32[]{:S(2)}) collective-permute-start(bf16[3,64,256]{2,1,0:T(8,128)(2,1)S(1)} %get-tuple-element.156), channel_id=1, source_target_pairs={{8,0},{16,8},{24,16},{9,1},{17,9},{25,17},{10,2},{18,10},{26,18},{... | collective-permute-start | bytes 294920 | tf_op jit(solution)/shard_map/ppermute | solution.py:413
  118.8 52.7 %collective-permute-start.20 = (bf16[8,32,384]{2,1,0:T(8,128)(2,1)}, bf16[8,32,384]{2,1,0:T(8,128)(2,1)}, u32[]{:S(2)}, u32[]{:S(2)}) collective-permute-start(bf16[8,32,384]{2,1,0:T(8,128)(2,1)} %get-tuple-element.152), channel_id=1, source_target_pairs={{0,6},{1,7},{2,4},{3,5},{4,2},{5,3},{6,0},{7,1},{8,14},{9,15},{10,... | collective-permute-start | bytes 589832 | tf_op jit(solution)/shard_map/ppermute | solution.py:345
  119.7 52.3 %collective-permute-start.26 = (bf16[8,32,384]{2,1,0:T(8,128)(2,1)}, bf16[8,32,384]{2,1,0:T(8,128)(2,1)}, u32[]{:S(2)}, u32[]{:S(2)}) collective-permute-start(bf16[8,32,384]{2,1,0:T(8,128)(2,1)} %get-tuple-element.163), channel_id=1, source_target_pairs={{0,7},{1,6},{2,5},{3,4},{4,3},{5,2},{6,1},{7,0},{8,15},{9,14},{10,... | collective-permute-start | bytes 589832 | tf_op jit(solution)/shard_map/ppermute | solution.py:345
  142.3 37.4 %collective-permute-start.25 = (bf16[16,32,384]{2,1,0:T(8,128)(2,1)}, bf16[16,32,384]{2,1,0:T(8,128)(2,1)S(1)}, u32[]{:S(2)}, u32[]{:S(2)}) collective-permute-start(bf16[16,32,384]{2,1,0:T(8,128)(2,1)} %get-tuple-element.165), channel_id=1, source_target_pairs={{0,5},{1,4},{2,7},{3,6},{4,1},{5,0},{6,3},{7,2},{8,13},{9,12},{10,... | collective-permute-start | bytes 1179656 | tf_op jit(solution)/shard_map/ppermute | solution.py:345
  147.9 47.7 %collective-permute-start.24 = (bf16[16,32,384]{2,1,0:T(8,128)(2,1)}, bf16[16,32,384]{2,1,0:T(8,128)(2,1)S(1)}, u32[]{:S(2)}, u32[]{:S(2)}) collective-permute-start(bf16[16,32,384]{2,1,0:T(8,128)(2,1)} %get-tuple-element.167), channel_id=1, source_target_pairs={{0,4},{1,5},{2,6},{3,7},{4,0},{5,1},{6,2},{7,3},{8,12},{9,13},{10,... | collective-permute-start | bytes 1179656 | tf_op jit(solution)/shard_map/ppermute | solution.py:345
  147.9 55.8 %collective-permute-start.22 = (bf16[16,32,384]{2,1,0:T(8,128)(2,1)}, bf16[16,32,384]{2,1,0:T(8,128)(2,1)S(1)}, u32[]{:S(2)}, u32[]{:S(2)}) collective-permute-start(bf16[16,32,384]{2,1,0:T(8,128)(2,1)} %get-tuple-element.169), channel_id=1, source_target_pairs={{0,2},{1,3},{2,0},{3,1},{4,6},{5,7},{6,4},{7,5},{8,10},{9,11},{10,... | collective-permute-start | bytes 1179656 | tf_op jit(solution)/shard_map/ppermute | solution.py:345
  171.4 40.6 %collective-permute-start.23 = (bf16[16,32,384]{2,1,0:T(8,128)(2,1)S(1)}, bf16[16,32,384]{2,1,0:T(8,128)(2,1)S(1)}, u32[]{:S(2)}, u32[]{:S(2)}) collective-permute-start(bf16[16,32,384]{2,1,0:T(8,128)(2,1)S(1)} %hold.3), channel_id=1, source_target_pairs={{0,3},{1,2},{2,1},{3,0},{4,7},{5,6},{6,5},{7,4},{8,11},{9,10},{10,... | collective-permute-start | bytes 1179656 | tf_op jit(solution)/shard_map/ppermute | solution.py:345
  171.9 43.0 %collective-permute-start.21 = (bf16[16,32,384]{2,1,0:T(8,128)(2,1)S(1)}, bf16[16,32,384]{2,1,0:T(8,128)(2,1)S(1)}, u32[]{:S(2)}, u32[]{:S(2)}) collective-permute-start(bf16[16,32,384]{2,1,0:T(8,128)(2,1)S(1)} %copy-done.30), channel_id=1, source_target_pairs={{0,1},{1,0},{2,3},{3,2},{4,5},{5,4},{6,7},{7,6},{8,9},{9,8},{10,11... | collective-permute-start | bytes 1179656 | tf_op jit(solution)/shard_map/ppermute | solution.py:345
  179.7 38.2 %collective-permute-start.18 = (bf16[16,32,384]{2,1,0:T(8,128)(2,1)S(1)}, bf16[16,32,384]{2,1,0:T(8,128)(2,1)S(1)}, u32[]{:S(2)}, u32[]{:S(2)}) collective-permute-start(bf16[16,32,384]{2,1,0:T(8,128)(2,1)S(1)} %copy-done.29), channel_id=1, source_target_pairs={{0,6},{1,7},{2,4},{3,5},{4,2},{5,3},{6,0},{7,1},{8,14},{9,15},{10,... | collective-permute-start | bytes 1179656 | tf_op jit(solution)/shard_map/ppermute | solution.py:345
  195.6 22.3 %collective-permute-start.19 = (bf16[16,32,384]{2,1,0:T(8,128)(2,1)S(1)}, bf16[16,32,384]{2,1,0:T(8,128)(2,1)S(1)}, u32[]{:S(2)}, u32[]{:S(2)}) collective-permute-start(bf16[16,32,384]{2,1,0:T(8,128)(2,1)S(1)} %hold.2), channel_id=1, source_target_pairs={{0,7},{1,6},{2,5},{3,4},{4,3},{5,2},{6,1},{7,0},{8,15},{9,14},{10,... | collective-permute-start | bytes 1179656 | tf_op jit(solution)/shard_map/ppermute | solution.py:345
  (36 other events, 479.8 us)

commit v6 on v5

--- a/solution.py
+++ b/solution.py
@@ -269,18 +269,21 @@
     )(v, v, deriv_x, metric_x, force, table)
 
 
-def combine_kernel(xi_ref, base_ref, v_ref, v1_ref, near_ref, far_ref, *refs):
+def combine_kernel(xi_ref, base_ref, v_ref, v1_ref, *refs):
     t_ref, u_ref, mark_ref, along = refs[-4:]
     mark_ref[...] = jnp.zeros(mark_ref.shape, mark_ref.dtype)
     rows, levels, width = base_ref.shape
     half = levels // 2
     for j in range(width // lanes):
         lane = slice(j * lanes, (j + 1) * lanes)
-        for i, block in enumerate((near_ref, far_ref)):
+        for at, block in enumerate(refs[:4]):
+            i, h = divmod(at, 2)
+            part = block.shape[1]
             start = (xi_ref[0] ^ i) * half
             for l in range(half):
                 plane = block[l, :, lane].astype(jnp.float32)
-                along[pl.ds(start + l, rows, stride=levels), :] = plane
+                first = h * part * levels + start + l
+                along[pl.ds(first, part, stride=levels), :] = plane
         along_y = along[...].reshape(rows, levels, lanes)
         t = base_ref[:, :, lane] - v1_ref[:, :, lane].astype(jnp.float32) * along_y
         t_ref[:, :, lane] = t.astype(jnp.bfloat16)
@@ -293,32 +296,34 @@
     part, width = near.shape[1:]
     half = levels // 2
     first, count = comps[0], len(comps)
-    block = (part, None, levels, width)
+    block = (rows, None, levels, width)
     column = pl.BlockSpec(block, lambda g, c, xi: (g, first + c, 0, xi[1 + s]))
-    planes = pl.BlockSpec((half, part, width), lambda g, c, xi: (g * count + c, 0, 0))
+    planes = [
+        pl.BlockSpec((half, part, width), lambda g, c, xi, h=h: (h * count + c, 0, 0))
+        for h in range(2)
+    ]
     return pl.pallas_call(
         combine_kernel,
         grid_spec=pltpu.PrefetchScalarGridSpec(
             num_scalar_prefetch=1,
-            grid=(rows // part, count),
+            grid=(1, count),
             in_specs=[
                 pl.BlockSpec(block, lambda g, c, xi: (g, c, 0, xi[1 + s])),
                 column,
                 pl.BlockSpec(block, lambda g, c, xi: (g, 1, 0, xi[1 + s])),
-                planes,
-                planes,
             ]
+            + planes * 2
             + [pl.BlockSpec(memory_space=pl.ANY)] * len((*outs[:2], *after)),
             out_specs=[column, column, pl.BlockSpec((8, lanes), lambda g, c, xi: (0, 0))],
-            scratch_shapes=[pltpu.VMEM((part * levels, lanes), jnp.float32)],
+            scratch_shapes=[pltpu.VMEM((rows * levels, lanes), jnp.float32)],
         ),
         out_shape=[jax.ShapeDtypeStruct(v.shape, v.dtype)] * 2
         + [jax.ShapeDtypeStruct((8, lanes), jnp.float32)],
-        input_output_aliases={6: 0, 7: 1} if outs else {},
+        input_output_aliases={8: 0, 9: 1} if outs else {},
         compiler_params=pltpu.CompilerParams(vmem_limit_bytes=16 * mib),
         cost_estimate=light,
         name="combine",
-    )(prefetch, base, v, v, near, far, *outs[:2], *after)
+    )(prefetch, base, v, v, near, near, far, far, *outs[:2], *after)
 
 
 def ring_shards(

time: 222 us -> 222 us (level)
  local copies, waits for them, and re-layouts: 11 us -> 15.2 us
  waiting for transfers between devices: 95.2 us -> 92.1 us
    ppermute x25, waiting for transfers between devices: 95.2 us -> 92.1 us  [trade(): lax.ppermute(block, 'row', [(i, i ^ k) for i in range(devices)])]
    unnamed x72 -> x76, local copies, waits for them, and re-layouts: 8.63 us -> 10.3 us
  transfers between devices with their start and end apart: 28 -> 28, of which waited for: 12 -> 12; matrix products, arithmetic and copies ran while one was open for 2% -> 3% of each run, Pallas kernels for 26% -> 26%
where the time goes in v6:
time: 222 us; the launch traced here: 221 us
  waiting for transfers between devices  92.1 us (41%)
  Pallas kernels  59.1 us (27%)
  starting transfers between devices  50.4 us (23%)
  local copies, waits for them, and re-layouts  15.2 us (7%)
  other arithmetic  2.67 us (1%)
    ppermute x25, waiting for transfers between devices, trade(): lax.ppermute(block, 'row', [(i, i ^ k) for i in range(devices)])  92.1 us
    ppermute x25, starting transfers between devices, trade(): lax.ppermute(block, 'row', [(i, i ^ k) for i in range(devices)])  44.8 us
    pallas_call x8, Pallas kernels, combine(): pl.pallas_call(combine_kernel, grid_spec=pltpu.PrefetchScalarGridSpec(num...  18.3 us
    pallas_call x6, Pallas kernels, pack(): pl.pallas_call(pack_kernel, grid_spec=pltpu.PrefetchScalarGridSpec(num_sc...  17.6 us
    pallas_call x2, Pallas kernels, slopes(): pl.pallas_call(functools.partial(slope_kernel, planes, places, riders), i...  11 us
    pallas_call x2, Pallas kernels, bases(): pl.pallas_call(base_kernel, grid=(rows // part, len(comps)), in_specs=[pl...  10.8 us
    unnamed x76, local copies, waits for them, and re-layouts  10.3 us
  transfers between devices with their start and end apart: 28, of which 12 were waited for; matrix products, arithmetic and copies ran while one was open for 3% of the time, Pallas kernels for 26%

profile of v6, /device:TPU:0, one launch (start us, length us, event | category | flops | bytes accessed | tf_op | source)
XLA Modules:
  0.0 220.6 jit_solution(2359494203980171757)
XLA Ops:
  0.6 4.1 %collective-permute-start = (bf16[16,3,4,192]{3,2,1,0:T(4,128)(2,1)}, bf16[16,3,4,192]{3,2,1,0:T(4,128)(2,1)S(1)}, u32[]{:S(2)}, u32[]{:S(2)}) collective-permute-start(bf16[16,3,4,192]{3,2,1,0:T(4,128)(2,1)} %bitcast.43), channel_id=1, source_target_pairs={{0,4},{1,5},{2,6},{3,7},{4,0},{5,1},{6,2},{7,3},{8,12},{9,13},{10,... | collective-permute-start | bytes 221192 | tf_op jit(solution)/shard_map/ppermute | solution.py:358
  11.8 3.2 %pack.7 = (bf16[24,32,384]{2,1,0:T(8,128)(2,1)}, bf16[24,32,384]{2,1,0:T(8,128)(2,1)}) custom-call(s32[5]{0:T(128)} %pad_add_fusion.xi_ref, bf16[64,3,8,1536]{3,2,1,0:T(8,128)(2,1)} %bitcast.16, bf16[8,32,384]{2,1,0:T(8,128)(2,1)} %get-tuple-element.105.refs_0_), custom_call_target="tpu_custom_call" | custom-call | flops 1 | bytes 1 | tf_op jit(solution)/shard_map/pack/pallas_call | solution.py:80
  20.6 3.2 %pack.9 = (bf16[24,32,384]{2,1,0:T(8,128)(2,1)}, bf16[24,32,384]{2,1,0:T(8,128)(2,1)}) custom-call(s32[5]{0:T(128)} %pad_add_fusion.xi_ref, bf16[64,3,8,1536]{3,2,1,0:T(8,128)(2,1)} %bitcast.18, bf16[8,32,384]{2,1,0:T(8,128)(2,1)} %get-tuple-element.120.refs_0_), custom_call_target="tpu_custom_call" | custom-call | flops 1 | bytes 1 | tf_op jit(solution)/shard_map/pack/pallas_call | solution.py:80
  38.3 22.0 %collective-permute-done.4.refs_4_ = bf16[8,32,384]{2,1,0:T(8,128)(2,1)S(1)} collective-permute-done((bf16[8,32,384]{2,1,0:T(8,128)(2,1)}, bf16[8,32,384]{2,1,0:T(8,128)(2,1)S(1)}, u32[]{:S(2)}, u32[]{:S(2)}) %collective-permute-start.4) | collective-permute-done | bytes 196640 | tf_op jit(solution)/shard_map/ppermute | solution.py:350
  60.3 3.0 %pack.11 = (bf16[16,32,384]{2,1,0:T(8,128)(2,1)}, bf16[16,32,384]{2,1,0:T(8,128)(2,1)}) custom-call(s32[5]{0:T(128)} %pad_add_fusion.xi_ref, bf16[64,3,8,1536]{3,2,1,0:T(8,128)(2,1)} %bitcast.20, bf16[16,32,384]{2,1,0:T(8,128)(2,1)} %get-tuple-element.124.refs_0_), custom_call_target="tpu_custom_call" | custom-call | flops 1 | bytes 1 | tf_op jit(solution)/shard_map/pack/pallas_call | solution.py:80
  67.1 4.0 %collective-permute-done.6.refs_6_ = bf16[24,32,384]{2,1,0:T(8,128)(2,1)S(1)} collective-permute-done((bf16[24,32,384]{2,1,0:T(8,128)(2,1)}, bf16[24,32,384]{2,1,0:T(8,128)(2,1)S(1)}, u32[]{:S(2)}, u32[]{:S(2)}) %collective-permute-start.6) | collective-permute-done | bytes 589856 | tf_op jit(solution)/shard_map/ppermute | solution.py:350
  71.9 4.7 %slopes.2 = (bf16[8,32,384]{2,1,0:T(8,128)(2,1)}, bf16[8,32,384]{2,1,0:T(8,128)(2,1)}, bf16[8,32,384]{2,1,0:T(8,128)(2,1)}, bf16[8,32,384]{2,1,0:T(8,128)(2,1)},...) custom-call(bf16[512,512]{1,0:T(8,128)(2,1)} %copy-done.15, ...), custom_call_target="tpu_custom_call" | custom-call | flops 1 | bytes 1 | tf_op jit(solution)/shard_map/slopes/pallas_call | solution.py:130
  76.8 2.9 %collective-permute-start.10 = (bf16[14,32,384]{2,1,0:T(8,128)(2,1)}, bf16[14,32,384]{2,1,0:T(8,128)(2,1)S(1)}, u32[]{:S(2)}, u32[]{:S(2)}) collective-permute-start(bf16[14,32,384]{2,1,0:T(8,128)(2,1)} %get-tuple-element.148), channel_id=1, source_target_pairs={{0,3},{1,2},{2,1},{3,0},{4,7},{5,6},{6,5},{7,4},{8,11},{9,10},{10,... | collective-permute-start | bytes 1032200 | tf_op jit(solution)/shard_map/ppermute | solution.py:350
  79.7 4.3 %collective-permute-done.11.refs_2_ = bf16[16,32,384]{2,1,0:T(8,128)(2,1)} collective-permute-done((bf16[16,32,384]{2,1,0:T(8,128)(2,1)}, bf16[16,32,384]{2,1,0:T(8,128)(2,1)}, u32[]{:S(2)}, u32[]{:S(2)}) %collective-permute-start.11) | collective-permute-done | bytes 393248 | tf_op jit(solution)/shard_map/ppermute | solution.py:350
  87.1 3.0 %collective-permute-start.15 = (bf16[16,32,384]{2,1,0:T(8,128)(2,1)}, bf16[16,32,384]{2,1,0:T(8,128)(2,1)}, u32[]{:S(2)}, u32[]{:S(2)}) collective-permute-start(bf16[16,32,384]{2,1,0:T(8,128)(2,1)} %get-tuple-element.138), channel_id=1, source_target_pairs={{0,7},{1,6},{2,5},{3,4},{4,3},{5,2},{6,1},{7,0},{8,15},{9,14},{10,... | collective-permute-start | bytes 1179656 | tf_op jit(solution)/shard_map/ppermute | solution.py:350
  90.8 7.0 %collective-permute-done.12.refs_2_.refs_3_ = bf16[14,32,384]{2,1,0:T(8,128)(2,1)S(1)} collective-permute-done((bf16[14,32,384]{2,1,0:T(8,128)(2,1)}, bf16[14,32,384]{2,1,0:T(8,128)(2,1)S(1)}, u32[]{:S(2)}, u32[]{:S(2)}) %collective-permute-start.12) | collective-permute-done | bytes 344096 | tf_op jit(solution)/shard_map/ppermute | solution.py:350
  97.9 3.4 %collective-permute-start.17 = (bf16[8,32,384]{2,1,0:T(8,128)(2,1)}, bf16[8,32,384]{2,1,0:T(8,128)(2,1)S(1)}, u32[]{:S(2)}, u32[]{:S(2)}) collective-permute-start(bf16[8,32,384]{2,1,0:T(8,128)(2,1)} %get-tuple-element.146), channel_id=1, source_target_pairs={{0,4},{1,5},{2,6},{3,7},{4,0},{5,1},{6,2},{7,3},{8,12},{9,13},{10,... | collective-permute-start | bytes 589832 | tf_op jit(solution)/shard_map/ppermute | solution.py:350
  101.3 14.1 %collective-permute-done.10.refs_1_.refs_2_.refs_3_ = bf16[14,32,384]{2,1,0:T(8,128)(2,1)S(1)} collective-permute-done((bf16[14,32,384]{2,1,0:T(8,128)(2,1)}, bf16[14,32,384]{2,1,0:T(8,128)(2,1)S(1)}, u32[]{:S(2)}, u32[]{:S(2)}) %collective-permute-start.10) | collective-permute-done | bytes 344096 | tf_op jit(solution)/shard_map/ppermute | solution.py:350
  120.4 3.5 %collective-permute-start.26 = (bf16[8,32,384]{2,1,0:T(8,128)(2,1)}, bf16[8,32,384]{2,1,0:T(8,128)(2,1)S(1)}, u32[]{:S(2)}, u32[]{:S(2)}) collective-permute-start(bf16[8,32,384]{2,1,0:T(8,128)(2,1)} %get-tuple-element.163), channel_id=1, source_target_pairs={{0,7},{1,6},{2,5},{3,4},{4,3},{5,2},{6,1},{7,0},{8,15},{9,14},{10,... | collective-permute-start | bytes 589832 | tf_op jit(solution)/shard_map/ppermute | solution.py:350
  123.9 6.2 %slopes.3 = (bf16[16,32,384]{2,1,0:T(8,128)(2,1)}, bf16[16,32,384]{2,1,0:T(8,128)(2,1)}, bf16[16,32,384]{2,1,0:T(8,128)(2,1)}, bf16[16,32,384]{2,1,0:T(8,128)(2,...) custom-call(bf16[512,512]{1,0:T(8,128)(2,1)} %copy-done.15, ...), custom_call_target="tpu_custom_call" | custom-call | flops 1 | bytes 1 | tf_op jit(solution)/shard_map/slopes/pallas_call | solution.py:130
  130.1 12.2 %collective-permute-done.16.refs_2_.refs_3_ = bf16[8,32,384]{2,1,0:T(8,128)(2,1)S(1)} collective-permute-done((bf16[8,32,384]{2,1,0:T(8,128)(2,1)}, bf16[8,32,384]{2,1,0:T(8,128)(2,1)S(1)}, u32[]{:S(2)}, u32[]{:S(2)}) %collective-permute-start.16) | collective-permute-done | bytes 196640 | tf_op jit(solution)/shard_map/ppermute | solution.py:350
  143.0 5.1 %collective-permute-start.25 = (bf16[16,32,384]{2,1,0:T(8,128)(2,1)}, bf16[16,32,384]{2,1,0:T(8,128)(2,1)S(1)}, u32[]{:S(2)}, u32[]{:S(2)}) collective-permute-start(bf16[16,32,384]{2,1,0:T(8,128)(2,1)} %get-tuple-element.165), channel_id=1, source_target_pairs={{0,5},{1,4},{2,7},{3,6},{4,1},{5,0},{6,3},{7,2},{8,13},{9,12},{10,... | collective-permute-start | bytes 1179656 | tf_op jit(solution)/shard_map/ppermute | solution.py:350
  148.7 3.1 %collective-permute-start.22 = (bf16[16,32,384]{2,1,0:T(8,128)(2,1)}, bf16[16,32,384]{2,1,0:T(8,128)(2,1)S(1)}, u32[]{:S(2)}, u32[]{:S(2)}) collective-permute-start(bf16[16,32,384]{2,1,0:T(8,128)(2,1)} %get-tuple-element.169), channel_id=1, source_target_pairs={{0,2},{1,3},{2,0},{3,1},{4,6},{5,7},{6,4},{7,5},{8,10},{9,11},{10,... | collective-permute-start | bytes 1179656 | tf_op jit(solution)/shard_map/ppermute | solution.py:350
  158.3 3.5 %bases.3.refs_0_.base_ref = f32[64,1,8,1536]{3,2,1,0:T(8,128)S(1)} custom-call(bf16[64,3,8,1536]{3,2,1,0:T(8,128)(2,1)S(1)} %bitcast.21, bf16[64,3,8,1536]{3,2,1,0:T(8,128)(2,1)S(1)} %bitcast.22, bf16[1536,1536]{1,0:T(8,128)(2,1)S(1)} %copy-done.1, f32[1,1536]{1,0:T(1,128)S(1)} %broadcast_in_dim.55.m_ref, bf16[3,64,8,256]{3,2,1,0:T(8,128)(2,1)S(1)} %refine.1.f_ref, ...), custom_call_target="tpu_custom_call" | custom-call | flops 1 | bytes 1 | tf_op jit(solution)/shard_map/bases/pallas_call | solution.py:253
  161.8 7.3 %bases.2.refs_1_.base_ref = f32[64,2,8,1536]{3,2,1,0:T(8,128)S(1)} custom-call(bf16[64,3,8,1536]{3,2,1,0:T(8,128)(2,1)S(1)} %bitcast.23, bf16[64,3,8,1536]{3,2,1,0:T(8,128)(2,1)S(1)} %bitcast.24, bf16[1536,1536]{1,0:T(8,128)(2,1)S(1)} %copy-done.1, f32[1,1536]{1,0:T(1,128)S(1)} %broadcast_in_dim.55.m_ref, bf16[3,64,8,256]{3,2,1,0:T(8,128)(2,1)S(1)} %refine.1.f_ref, ...), custom_call_target="tpu_custom_call" | custom-call | flops 1 | bytes 1 | tf_op jit(solution)/shard_map/bases/pallas_call | solution.py:253
  174.8 5.5 %collective-permute-done.25.refs_2_.refs_3_ = bf16[16,32,384]{2,1,0:T(8,128)(2,1)S(1)} collective-permute-done((bf16[16,32,384]{2,1,0:T(8,128)(2,1)}, bf16[16,32,384]{2,1,0:T(8,128)(2,1)S(1)}, u32[]{:S(2)}, u32[]{:S(2)}) %collective-permute-start.25) | collective-permute-done | bytes 393248 | tf_op jit(solution)/shard_map/ppermute | solution.py:350
  182.9 13.4 %collective-permute-done.24.refs_0_.refs_1_ = bf16[16,32,384]{2,1,0:T(8,128)(2,1)S(1)} collective-permute-done((bf16[16,32,384]{2,1,0:T(8,128)(2,1)}, bf16[16,32,384]{2,1,0:T(8,128)(2,1)S(1)}, u32[]{:S(2)}, u32[]{:S(2)}) %collective-permute-start.24) | collective-permute-done | bytes 393248 | tf_op jit(solution)/shard_map/ppermute | solution.py:350
  196.3 3.4 %collective-permute-start.19 = (bf16[16,32,384]{2,1,0:T(8,128)(2,1)S(1)}, bf16[16,32,384]{2,1,0:T(8,128)(2,1)S(1)}, u32[]{:S(2)}, u32[]{:S(2)}) collective-permute-start(bf16[16,32,384]{2,1,0:T(8,128)(2,1)S(1)} %hold.2), channel_id=1, source_target_pairs={{0,7},{1,6},{2,5},{3,4},{4,3},{5,2},{6,1},{7,0},{8,15},{9,14},{10,... | collective-permute-start | bytes 1179656 | tf_op jit(solution)/shard_map/ppermute | solution.py:350
  206.3 6.4 %collective-permute-done.23.refs_2_.refs_3_ = bf16[16,32,384]{2,1,0:T(8,128)(2,1)S(1)} collective-permute-done((bf16[16,32,384]{2,1,0:T(8,128)(2,1)S(1)}, bf16[16,32,384]{2,1,0:T(8,128)(2,1)S(1)}, u32[]{:S(2)}, u32[]{:S(2)}) %collective-permute-start.23) | collective-permute-done | bytes 393248 | tf_op jit(solution)/shard_map/ppermute | solution.py:350
  (157 shorter events, 70.6 us)
Async XLA Ops:
  0.6 26.4 %collective-permute-start = (bf16[16,3,4,192]{3,2,1,0:T(4,128)(2,1)}, bf16[16,3,4,192]{3,2,1,0:T(4,128)(2,1)S(1)}, u32[]{:S(2)}, u32[]{:S(2)}) collective-permute-start(bf16[16,3,4,192]{3,2,1,0:T(4,128)(2,1)} %bitcast.43), channel_id=1, source_target_pairs={{0,4},{1,5},{2,6},{3,7},{4,0},{5,1},{6,2},{7,3},{8,12},{9,13},{10,... | collective-permute-start | bytes 221192 | tf_op jit(solution)/shard_map/ppermute | solution.py:358
  7.9 22.3 %collective-permute-start.1 = (bf16[8,32,384]{2,1,0:T(8,128)(2,1)}, bf16[8,32,384]{2,1,0:T(8,128)(2,1)S(1)}, u32[]{:S(2)}, u32[]{:S(2)}) collective-permute-start(bf16[8,32,384]{2,1,0:T(8,128)(2,1)} %get-tuple-element.127), channel_id=1, source_target_pairs={{0,5},{1,4},{2,7},{3,6},{4,1},{5,0},{6,3},{7,2},{8,13},{9,12},{10,... | collective-permute-start | bytes 589832 | tf_op jit(solution)/shard_map/ppermute | solution.py:350
  9.2 25.3 %collective-permute-start.2 = (bf16[8,32,384]{2,1,0:T(8,128)(2,1)}, bf16[8,32,384]{2,1,0:T(8,128)(2,1)}, u32[]{:S(2)}, u32[]{:S(2)}) collective-permute-start(bf16[8,32,384]{2,1,0:T(8,128)(2,1)} %get-tuple-element.105.refs_0_), channel_id=1, source_target_pairs={{0,4},{1,5},{2,6},{3,7},{4,0},{5,1},{6,2},{7,3},{8,12},{9,13},{10,... | collective-permute-start | bytes 589832 | tf_op jit(solution)/shard_map/ppermute | solution.py:350
  20.3 46.8 %collective-permute-start.5 = (bf16[24,32,384]{2,1,0:T(8,128)(2,1)S(1)}, bf16[24,32,384]{2,1,0:T(8,128)(2,1)S(1)}, u32[]{:S(2)}, u32[]{:S(2)}) collective-permute-start(bf16[24,32,384]{2,1,0:T(8,128)(2,1)S(1)} %copy-done.20), channel_id=1, source_target_pairs={{0,2},{1,3},{2,0},{3,1},{4,6},{5,7},{6,4},{7,5},{8,10},{9,11},{10,... | collective-permute-start | bytes 1769480 | tf_op jit(solution)/shard_map/ppermute | solution.py:350
  27.7 43.4 %collective-permute-start.6 = (bf16[24,32,384]{2,1,0:T(8,128)(2,1)}, bf16[24,32,384]{2,1,0:T(8,128)(2,1)S(1)}, u32[]{:S(2)}, u32[]{:S(2)}) collective-permute-start(bf16[24,32,384]{2,1,0:T(8,128)(2,1)} %get-tuple-element.123), channel_id=1, source_target_pairs={{0,3},{1,2},{2,1},{3,0},{4,7},{5,6},{6,5},{7,4},{8,11},{9,10},{10,... | collective-permute-start | bytes 1769480 | tf_op jit(solution)/shard_map/ppermute | solution.py:350
  30.2 30.1 %collective-permute-start.4 = (bf16[8,32,384]{2,1,0:T(8,128)(2,1)}, bf16[8,32,384]{2,1,0:T(8,128)(2,1)S(1)}, u32[]{:S(2)}, u32[]{:S(2)}) collective-permute-start(bf16[8,32,384]{2,1,0:T(8,128)(2,1)} %get-tuple-element.122), channel_id=1, source_target_pairs={{0,7},{1,6},{2,5},{3,4},{4,3},{5,2},{6,1},{7,0},{8,15},{9,14},{10,... | collective-permute-start | bytes 589832 | tf_op jit(solution)/shard_map/ppermute | solution.py:350
  34.5 32.6 %collective-permute-start.7 = (bf16[24,32,384]{2,1,0:T(8,128)(2,1)}, bf16[24,32,384]{2,1,0:T(8,128)(2,1)S(1)}, u32[]{:S(2)}, u32[]{:S(2)}) collective-permute-start(bf16[24,32,384]{2,1,0:T(8,128)(2,1)} %get-tuple-element.125), channel_id=1, source_target_pairs={{0,1},{1,0},{2,3},{3,2},{4,5},{5,4},{6,7},{7,6},{8,9},{9,8},{10,11... | collective-permute-start | bytes 1769480 | tf_op jit(solution)/shard_map/ppermute | solution.py:350
  35.7 41.1 %collective-permute-start.9 = (bf16[16,32,384]{2,1,0:T(8,128)(2,1)}, bf16[16,32,384]{2,1,0:T(8,128)(2,1)S(1)}, u32[]{:S(2)}, u32[]{:S(2)}) collective-permute-start(bf16[16,32,384]{2,1,0:T(8,128)(2,1)} %get-tuple-element.124.refs_0_), channel_id=1, source_target_pairs={{0,4},{1,5},{2,6},{3,7},{4,0},{5,1},{6,2},{7,3},{8,12},{9,13},{10,... | collective-permute-start | bytes 1179656 | tf_op jit(solution)/shard_map/ppermute | solution.py:350
  60.3 23.8 %collective-permute-start.11 = (bf16[16,32,384]{2,1,0:T(8,128)(2,1)}, bf16[16,32,384]{2,1,0:T(8,128)(2,1)}, u32[]{:S(2)}, u32[]{:S(2)}) collective-permute-start(bf16[16,32,384]{2,1,0:T(8,128)(2,1)} %get-tuple-element.128), channel_id=1, source_target_pairs={{0,5},{1,4},{2,7},{3,6},{4,1},{5,0},{6,3},{7,2},{8,13},{9,12},{10,... | collective-permute-start | bytes 1179656 | tf_op jit(solution)/shard_map/ppermute | solution.py:350
  76.8 38.7 %collective-permute-start.10 = (bf16[14,32,384]{2,1,0:T(8,128)(2,1)}, bf16[14,32,384]{2,1,0:T(8,128)(2,1)S(1)}, u32[]{:S(2)}, u32[]{:S(2)}) collective-permute-start(bf16[14,32,384]{2,1,0:T(8,128)(2,1)} %get-tuple-element.148), channel_id=1, source_target_pairs={{0,3},{1,2},{2,1},{3,0},{4,7},{5,6},{6,5},{7,4},{8,11},{9,10},{10,... | collective-permute-start | bytes 1032200 | tf_op jit(solution)/shard_map/ppermute | solution.py:350
  85.8 33.7 %collective-permute-start.14 = (bf16[16,32,384]{2,1,0:T(8,128)(2,1)}, bf16[16,32,384]{2,1,0:T(8,128)(2,1)S(1)}, u32[]{:S(2)}, u32[]{:S(2)}) collective-permute-start(bf16[16,32,384]{2,1,0:T(8,128)(2,1)} %get-tuple-element.133), channel_id=1, source_target_pairs={{0,6},{1,7},{2,4},{3,5},{4,2},{5,3},{6,0},{7,1},{8,14},{9,15},{10,... | collective-permute-start | bytes 1179656 | tf_op jit(solution)/shard_map/ppermute | solution.py:350
  87.1 33.3 %collective-permute-start.15 = (bf16[16,32,384]{2,1,0:T(8,128)(2,1)}, bf16[16,32,384]{2,1,0:T(8,128)(2,1)}, u32[]{:S(2)}, u32[]{:S(2)}) collective-permute-start(bf16[16,32,384]{2,1,0:T(8,128)(2,1)} %get-tuple-element.138), channel_id=1, source_target_pairs={{0,7},{1,6},{2,5},{3,4},{4,3},{5,2},{6,1},{7,0},{8,15},{9,14},{10,... | collective-permute-start | bytes 1179656 | tf_op jit(solution)/shard_map/ppermute | solution.py:350
  90.8 51.4 %collective-permute-start.16 = (bf16[8,32,384]{2,1,0:T(8,128)(2,1)}, bf16[8,32,384]{2,1,0:T(8,128)(2,1)S(1)}, u32[]{:S(2)}, u32[]{:S(2)}) collective-permute-start(bf16[8,32,384]{2,1,0:T(8,128)(2,1)} %get-tuple-element.140), channel_id=1, source_target_pairs={{0,5},{1,4},{2,7},{3,6},{4,1},{5,0},{6,3},{7,2},{8,13},{9,12},{10,... | collective-permute-start | bytes 589832 | tf_op jit(solution)/shard_map/ppermute | solution.py:350
  97.9 50.1 %collective-permute-start.17 = (bf16[8,32,384]{2,1,0:T(8,128)(2,1)}, bf16[8,32,384]{2,1,0:T(8,128)(2,1)S(1)}, u32[]{:S(2)}, u32[]{:S(2)}) collective-permute-start(bf16[8,32,384]{2,1,0:T(8,128)(2,1)} %get-tuple-element.146), channel_id=1, source_target_pairs={{0,4},{1,5},{2,6},{3,7},{4,0},{5,1},{6,2},{7,3},{8,12},{9,13},{10,... | collective-permute-start | bytes 589832 | tf_op jit(solution)/shard_map/ppermute | solution.py:350
  118.0 30.7 %collective-permute-start.13 = (bf16[3,64,256]{2,1,0:T(8,128)(2,1)S(1)}, bf16[3,64,256]{2,1,0:T(8,128)(2,1)S(1)}, u32[]{:S(2)}, u32[]{:S(2)}) collective-permute-start(bf16[3,64,256]{2,1,0:T(8,128)(2,1)S(1)} %get-tuple-element.156), channel_id=1, source_target_pairs={{8,0},{16,8},{24,16},{9,1},{17,9},{25,17},{10,2},{18,10},{26,18},{... | collective-permute-start | bytes 294920 | tf_op jit(solution)/shard_map/ppermute | solution.py:418
  119.5 53.7 %collective-permute-start.20 = (bf16[8,32,384]{2,1,0:T(8,128)(2,1)}, bf16[8,32,384]{2,1,0:T(8,128)(2,1)S(1)}, u32[]{:S(2)}, u32[]{:S(2)}) collective-permute-start(bf16[8,32,384]{2,1,0:T(8,128)(2,1)} %get-tuple-element.152), channel_id=1, source_target_pairs={{0,6},{1,7},{2,4},{3,5},{4,2},{5,3},{6,0},{7,1},{8,14},{9,15},{10,... | collective-permute-start | bytes 589832 | tf_op jit(solution)/shard_map/ppermute | solution.py:350
  120.4 53.4 %collective-permute-start.26 = (bf16[8,32,384]{2,1,0:T(8,128)(2,1)}, bf16[8,32,384]{2,1,0:T(8,128)(2,1)S(1)}, u32[]{:S(2)}, u32[]{:S(2)}) collective-permute-start(bf16[8,32,384]{2,1,0:T(8,128)(2,1)} %get-tuple-element.163), channel_id=1, source_target_pairs={{0,7},{1,6},{2,5},{3,4},{4,3},{5,2},{6,1},{7,0},{8,15},{9,14},{10,... | collective-permute-start | bytes 589832 | tf_op jit(solution)/shard_map/ppermute | solution.py:350
  143.0 37.4 %collective-permute-start.25 = (bf16[16,32,384]{2,1,0:T(8,128)(2,1)}, bf16[16,32,384]{2,1,0:T(8,128)(2,1)S(1)}, u32[]{:S(2)}, u32[]{:S(2)}) collective-permute-start(bf16[16,32,384]{2,1,0:T(8,128)(2,1)} %get-tuple-element.165), channel_id=1, source_target_pairs={{0,5},{1,4},{2,7},{3,6},{4,1},{5,0},{6,3},{7,2},{8,13},{9,12},{10,... | collective-permute-start | bytes 1179656 | tf_op jit(solution)/shard_map/ppermute | solution.py:350
  148.7 47.6 %collective-permute-start.24 = (bf16[16,32,384]{2,1,0:T(8,128)(2,1)}, bf16[16,32,384]{2,1,0:T(8,128)(2,1)S(1)}, u32[]{:S(2)}, u32[]{:S(2)}) collective-permute-start(bf16[16,32,384]{2,1,0:T(8,128)(2,1)} %get-tuple-element.167), channel_id=1, source_target_pairs={{0,4},{1,5},{2,6},{3,7},{4,0},{5,1},{6,2},{7,3},{8,12},{9,13},{10,... | collective-permute-start | bytes 1179656 | tf_op jit(solution)/shard_map/ppermute | solution.py:350
  148.7 54.9 %collective-permute-start.22 = (bf16[16,32,384]{2,1,0:T(8,128)(2,1)}, bf16[16,32,384]{2,1,0:T(8,128)(2,1)S(1)}, u32[]{:S(2)}, u32[]{:S(2)}) collective-permute-start(bf16[16,32,384]{2,1,0:T(8,128)(2,1)} %get-tuple-element.169), channel_id=1, source_target_pairs={{0,2},{1,3},{2,0},{3,1},{4,6},{5,7},{6,4},{7,5},{8,10},{9,11},{10,... | collective-permute-start | bytes 1179656 | tf_op jit(solution)/shard_map/ppermute | solution.py:350
  173.3 39.4 %collective-permute-start.23 = (bf16[16,32,384]{2,1,0:T(8,128)(2,1)S(1)}, bf16[16,32,384]{2,1,0:T(8,128)(2,1)S(1)}, u32[]{:S(2)}, u32[]{:S(2)}) collective-permute-start(bf16[16,32,384]{2,1,0:T(8,128)(2,1)S(1)} %hold.3), channel_id=1, source_target_pairs={{0,3},{1,2},{2,1},{3,0},{4,7},{5,6},{6,5},{7,4},{8,11},{9,10},{10,... | collective-permute-start | bytes 1179656 | tf_op jit(solution)/shard_map/ppermute | solution.py:350
  173.8 41.5 %collective-permute-start.21 = (bf16[16,32,384]{2,1,0:T(8,128)(2,1)S(1)}, bf16[16,32,384]{2,1,0:T(8,128)(2,1)S(1)}, u32[]{:S(2)}, u32[]{:S(2)}) collective-permute-start(bf16[16,32,384]{2,1,0:T(8,128)(2,1)S(1)} %copy-done.32), channel_id=1, source_target_pairs={{0,1},{1,0},{2,3},{3,2},{4,5},{5,4},{6,7},{7,6},{8,9},{9,8},{10,11... | collective-permute-start | bytes 1179656 | tf_op jit(solution)/shard_map/ppermute | solution.py:350
  180.3 37.6 %collective-permute-start.18 = (bf16[16,32,384]{2,1,0:T(8,128)(2,1)S(1)}, bf16[16,32,384]{2,1,0:T(8,128)(2,1)S(1)}, u32[]{:S(2)}, u32[]{:S(2)}) collective-permute-start(bf16[16,32,384]{2,1,0:T(8,128)(2,1)S(1)} %copy-done.31), channel_id=1, source_target_pairs={{0,6},{1,7},{2,4},{3,5},{4,2},{5,3},{6,0},{7,1},{8,14},{9,15},{10,... | collective-permute-start | bytes 1179656 | tf_op jit(solution)/shard_map/ppermute | solution.py:350
  196.3 21.6 %collective-permute-start.19 = (bf16[16,32,384]{2,1,0:T(8,128)(2,1)S(1)}, bf16[16,32,384]{2,1,0:T(8,128)(2,1)S(1)}, u32[]{:S(2)}, u32[]{:S(2)}) collective-permute-start(bf16[16,32,384]{2,1,0:T(8,128)(2,1)S(1)} %hold.2), channel_id=1, source_target_pairs={{0,7},{1,6},{2,5},{3,4},{4,3},{5,2},{6,1},{7,0},{8,15},{9,14},{10,... | collective-permute-start | bytes 1179656 | tf_op jit(solution)/shard_map/ppermute | solution.py:350
  (38 other events, 409.3 us)
